TPU v7x, 512 devices: a whole 4x8x8 slice. The times are simulated.
512 devices in a mesh: wn: 4 (over x_hi, core), sx: 8 (over y), az: 16 (over z, x_lo).
Axes of the slice: x: 4 (x_hi: 2, x_lo: 2; x = x_hi * 2 + x_lo), y: 8, z: 8, core: 2. Of those that a mesh axis runs over, the one named last changes fastest.
Arguments:
- fields: float32 [5, 64, 128, 1024], P(None, 'wn', 'az', 'sx'), as said below
- shock_height: float32 [128, 1024], P('az', 'sx'), may hold values from 0.5 to 1.5
- behind_shock: float32 [5, 128, 1024], P(None, 'az', 'sx'), as said below
Outputs:
- fields_next: float32 [5, 64, 128, 1024], P(None, 'wn', 'az', 'sx')
- height_next: float32 [128, 1024], P('az', 'sx')
Inputs may be any that keep to these rules, and one draw needn't show every extreme that they name: `fields`: built from densities in 0.7 to 1.3, pressures in 0.6 to 1.4 and velocity components of magnitude at most 0.3 in each cell. `behind_shock`: built from densities in 0.7 to 1.3, pressures in 0.6 to 1.4 and velocity components of magnitude at most 0.3 at each surface point.
All inputs are finite; a program needn't handle non-finite values.
Results may differ from a plain program's by a relative error of at most 0.00002.
Values sent between devices are 32-bit elements; how exact they have to be, the bound alone decides.
No kernel may reach another device: no remote copies, remote signals or barrier semaphores. Data moves between devices by JAX's collectives and lax.ppermute only.
A program may use at most 64 MiB of HBM per device.

v0:
```python
import jax
import jax.numpy as jnp
from jax import lax
from jax.sharding import PartitionSpec as P

GAMMA = 1.4
CFL_STEP = 0.08


def extended(x, sides, width, wrap):
    for axis, dim in sides:
        size, length = (lax.axis_size(axis), x.shape[dim])
        up = [(i, (i + 1) % size) for i in range(size if wrap else size - 1)]
        down = [(j, i) for i, j in up]
        last = lax.slice_in_dim(x, length - width, length, axis=dim)
        initial = lax.slice_in_dim(x, 0, width, axis=dim)
        before = lax.ppermute(last, axis, up)
        after = lax.ppermute(initial, axis, down)
        x = jnp.concatenate([before, x, after], axis=dim)
    return x


def spread(value, axis, source):
    kept = jnp.where(lax.axis_index(axis) == source, value, 0).astype(value.dtype)
    return lax.psum(kept, axis)


def differ(values, axis_index, factor):
    length = values.shape[axis_index] - 4

    def shifted(offset):
        return lax.slice_in_dim(values, offset, offset + length, axis=axis_index)

    return (shifted(0) - 8.0 * shifted(1) + 8.0 * shifted(3) - shifted(4)) * (factor / 12.0)


def pressure(conserved):
    kinetic = (conserved[1] ** 2 + conserved[2] ** 2 + conserved[3] ** 2) / conserved[0]
    return (GAMMA - 1.0) * (conserved[4] - 0.5 * kinetic)


def direction_flux(conserved, component):
    velocity = conserved[component] / conserved[0]
    pressure_now = pressure(conserved)
    pieces = [conserved[component]]
    for moment in (1, 2, 3):
        product = conserved[moment] * velocity
        if moment == component:
            product = product + pressure_now
        pieces.append(product)
    pieces.append((conserved[4] + pressure_now) * velocity)
    return jnp.stack(pieces)


def shock_speed(top_row, behind):
    behind_pressure = pressure(behind)
    return (pressure(top_row) - behind_pressure) / jnp.sqrt(GAMMA * behind_pressure * behind[0])


def tendency(
    normal_slab,
    axial_slab,
    around_slab,
    height,
    slope_axial,
    slope_around,
    speed_now,
    height_frac,
    layers,
):
    axial_term = differ(direction_flux(axial_slab, 1), 3, layers)
    around_term = differ(direction_flux(around_slab, 3), 2, layers)
    normal_axial = differ(direction_flux(normal_slab, 1), 1, layers)
    normal_wall = differ(direction_flux(normal_slab, 2), 1, layers)
    normal_around = differ(direction_flux(normal_slab, 3), 1, layers)
    normal_state = differ(normal_slab, 1, layers)
    inverse = 1.0 / height
    moving = slope_axial * normal_axial + slope_around * normal_around + speed_now * normal_state
    return -axial_term - around_term - inverse * normal_wall + height_frac * inverse * moving


def mend_ends(padded, first_tile, last_tile):
    left_edge = jnp.where(
        first_tile, jnp.broadcast_to(padded[..., 2:3], padded[..., :2].shape), padded[..., :2]
    )
    right_edge = jnp.where(
        last_tile, jnp.broadcast_to(padded[..., -3:-2], padded[..., -2:].shape), padded[..., -2:]
    )
    return jnp.concatenate([left_edge, padded[..., 2:-2], right_edge], axis=-1)


def per_device(fields, shock_height, behind_shock):
    layers_dev = fields.shape[1]
    wn_count = lax.axis_size("wn")
    layers = layers_dev * wn_count
    time_step = CFL_STEP / layers
    layer_index = lax.axis_index("wn")
    tile_index = lax.axis_index("sx")
    top_layer = wn_count - 1
    first_tile = tile_index == 0
    last_tile = tile_index == lax.axis_size("sx") - 1
    at_wall = layer_index == 0
    at_shock = layer_index == top_layer
    offsets = (layer_index * layers_dev).astype(jnp.float32)
    height_frac = ((offsets + jnp.arange(layers_dev, dtype=jnp.float32) + 0.5) / layers)[
        None, :, None, None
    ]
    mirror = jnp.array([1.0, -1.0, -1.0, -1.0, 1.0], dtype=jnp.float32).reshape(5, 1, 1, 1)

    def padded_fields(state):
        around_pad = extended(state, (("az", 2),), 2, True)
        padded = extended(around_pad, (("wn", 1), ("sx", 3)), 2, False)
        return padded

    def rate(padded, height, slope_axial, slope_around, speed_now):
        inner_block = padded[:, :, 2:-2, 2:-2]
        wall_ghost = jnp.where(at_wall, mirror * inner_block[:, 3:1:-1], inner_block[:, :2])
        shock_ghost = jnp.where(
            at_shock,
            jnp.broadcast_to(behind_shock[:, None], inner_block[:, -2:].shape),
            inner_block[:, -2:],
        )
        normal_slab = jnp.concatenate([wall_ghost, inner_block[:, 2:-2], shock_ghost], axis=1)
        axial_slab = mend_ends(padded[:, 2:-2, 2:-2, :], first_tile, last_tile)
        around_slab = padded[:, 2:-2, :, 2:-2]
        return tendency(
            normal_slab,
            axial_slab,
            around_slab,
            height,
            slope_axial,
            slope_around,
            speed_now,
            height_frac,
            layers,
        )

    height_pad = mend_ends(
        extended(shock_height, (("sx", 1), ("az", 0)), 2, True), first_tile, last_tile
    )
    slope_axial = differ(height_pad[2:-2], 1, layers)
    slope_around = differ(height_pad[:, 2:-2], 0, layers)
    padded_zero = padded_fields(fields)
    speed_first = spread(shock_speed(fields[:, -1], behind_shock), "wn", top_layer)
    height_one = shock_height + time_step * speed_first
    next_pad = mend_ends(
        extended(height_one, (("sx", 1), ("az", 0)), 2, True), first_tile, last_tile
    )
    slope_axial_one = differ(next_pad[2:-2], 1, layers)
    slope_around_one = differ(next_pad[:, 2:-2], 0, layers)
    section_one = fields + time_step * rate(
        padded_zero, shock_height, slope_axial, slope_around, speed_first
    )
    padded_one = padded_fields(section_one)
    speed_second = spread(shock_speed(section_one[:, -1], behind_shock), "wn", top_layer)
    second_rate = rate(padded_one, height_one, slope_axial_one, slope_around_one, speed_second)
    fields_next = 0.5 * (fields + section_one + time_step * second_rate)
    height_next = 0.5 * (shock_height + height_one + time_step * speed_second)
    return (fields_next, height_next)


def solution(mesh):
    in_specs = (P(None, "wn", "az", "sx"), P("az", "sx"), P(None, "az", "sx"))
    out_specs = (P(None, "wn", "az", "sx"), P("az", "sx"))
    return jax.shard_map(
        per_device, mesh=mesh, in_specs=in_specs, out_specs=out_specs, check_vma=False
    )
```

profile of v0, /device:TPU:12, one launch (start us, length us, event | category | flops | bytes accessed | tf_op | source)
XLA Modules:
  0.0 143.9 jit_solution(10705477431052719541)
XLA Ops:
  0.6 1.2 fusion.105
  1.8 11.6 %collective-permute-start.1 = (f32[5,16,2,128]{3,2,1,0:T(2,128)S(1)}, f32[5,16,2,128]{3,2,1,0:T(2,128)S(1)}, u32[]{:S(2)}, u32[]{:S(2)}) collective-permute-start(f32[5,16,2,128]{3,2,1,0:T(2,128)S(1)} %get-tuple-element.79), channel_id=1, source_target_pairs={{1,0},{2,1},{3,2},{4,3},{5,4},{6,5},{7,6},{8,7},{9,8},{10,9},{11,1... | collective-permute-start | bytes 245768 | tf_op jit(solution)/shard_map/ppermute | solution.py:18
  13.4 1.9 %collective-permute-start = (f32[5,16,2,128]{3,2,1,0:T(2,128)S(1)}, f32[5,16,2,128]{3,2,1,0:T(2,128)S(1)}, u32[]{:S(2)}, u32[]{:S(2)}) collective-permute-start(f32[5,16,2,128]{3,2,1,0:T(2,128)S(1)} %get-tuple-element.78), channel_id=1, source_target_pairs={{0,1},{1,2},{2,3},{3,4},{4,5},{5,6},{6,7},{7,8},{8,9},{9,10},{10,1... | collective-permute-start | bytes 245768 | tf_op jit(solution)/shard_map/ppermute | solution.py:17
  15.3 0.8 fusion.107
  16.2 2.3 %collective-permute-start.7 = (f32[8,2]{1,0:T(8,128)S(1)}, f32[8,2]{1,0:T(8,128)S(1)}, u32[]{:S(2)}, u32[]{:S(2)}) collective-permute-start(f32[8,2]{1,0:T(8,128)S(1)} %get-tuple-element.98), channel_id=1, source_target_pairs={{16,0},{32,16},{48,32},{64,48},{80,64},{96,80},{112,96},{0,112},{1... | collective-permute-start | bytes 200 | tf_op jit(solution)/shard_map/ppermute | solution.py:18
  18.5 3.5 %collective-permute-start.6 = (f32[8,2]{1,0:T(8,128)S(1)}, f32[8,2]{1,0:T(8,128)S(1)}, u32[]{:S(2)}, u32[]{:S(2)}) collective-permute-start(f32[8,2]{1,0:T(8,128)S(1)} %get-tuple-element.97), channel_id=1, source_target_pairs={{0,16},{16,32},{32,48},{48,64},{64,80},{80,96},{96,112},{112,0},{1... | collective-permute-start | bytes 200 | tf_op jit(solution)/shard_map/ppermute | solution.py:17
  23.4 7.1 %psum.14 = f32[8,128]{1,0:T(8,128)S(1)} all-reduce(f32[8,128]{1,0:T(8,128)S(1)} %get-tuple-element.27), channel_id=1, replica_groups=mesh['wn'=4,'sx'=8,'az'=16] {'wn'}, use_global_device_ids=true, to_apply=%region_0.1 | all-reduce | flops 1024 | bytes 8192 | tf_op jit(solution)/shard_map/psum | solution.py:25
  31.3 6.0 %collective-permute-start.9 = (f32[2,132]{1,0:T(2,128)S(1)}, f32[2,132]{1,0:T(2,128)S(1)}, u32[]{:S(2)}, u32[]{:S(2)}) collective-permute-start(f32[2,132]{1,0:T(2,128)S(1)} %get-tuple-element.87), channel_id=1, source_target_pairs={{1,0},{2,1},{3,2},{4,3},{5,4},{6,5},{7,6},{8,7},{9,8},{10,9},{11,1... | collective-permute-start | bytes 3176 | tf_op jit(solution)/shard_map/ppermute | solution.py:18
  37.3 1.9 %collective-permute-start.8 = (f32[2,132]{1,0:T(2,128)S(1)}, f32[2,132]{1,0:T(2,128)S(1)}, u32[]{:S(2)}, u32[]{:S(2)}) collective-permute-start(f32[2,132]{1,0:T(2,128)S(1)} %get-tuple-element.86), channel_id=1, source_target_pairs={{0,1},{1,2},{2,3},{3,4},{4,5},{5,6},{6,7},{7,8},{8,9},{9,10},{10,1... | collective-permute-start | bytes 3176 | tf_op jit(solution)/shard_map/ppermute | solution.py:17
  39.3 1.1 copy.103
  40.4 1.1 copy.102
  41.6 3.3 %collective-permute-done.8 = f32[2,132]{1,0:T(2,128)S(1)} collective-permute-done((f32[2,132]{1,0:T(2,128)S(1)}, f32[2,132]{1,0:T(2,128)S(1)}, u32[]{:S(2)}, u32[]{:S(2)}) %collective-permute-start.8) | collective-permute-done | bytes 1088 | tf_op jit(solution)/shard_map/ppermute | solution.py:17
  45.2 0.7 broadcast_multiply_fusion.5
  45.9 0.7 broadcast_multiply_fusion.1
  47.4 1.9 %collective-permute-start.3 = (f32[5,2,12,128]{3,2,1,0:T(8,128)S(1)}, f32[5,2,12,128]{3,2,1,0:T(8,128)S(1)}, u32[]{:S(2)}, u32[]{:S(2)}) collective-permute-start(f32[5,2,12,128]{3,2,1,0:T(8,128)S(1)} %get-tuple-element.59), channel_id=1, source_target_pairs={{128,0},{256,128},{384,256},{129,1},{257,129},{385,257},{130,2},{2... | collective-permute-start | bytes 184328 | tf_op jit(solution)/shard_map/ppermute | solution.py:18
  49.3 2.4 %collective-permute-start.2 = (f32[5,2,12,128]{3,2,1,0:T(8,128)S(1)}, f32[5,2,12,128]{3,2,1,0:T(8,128)S(1)}, u32[]{:S(2)}, u32[]{:S(2)}) collective-permute-start(f32[5,2,12,128]{3,2,1,0:T(8,128)S(1)} %get-tuple-element.58), channel_id=1, source_target_pairs={{0,128},{128,256},{256,384},{1,129},{129,257},{257,385},{2,130},{1... | collective-permute-start | bytes 184328 | tf_op jit(solution)/shard_map/ppermute | solution.py:17
  52.1 4.5 %collective-permute-done.2 = f32[5,2,12,128]{3,2,1,0:T(8,128)S(1)} collective-permute-done((f32[5,2,12,128]{3,2,1,0:T(8,128)S(1)}, f32[5,2,12,128]{3,2,1,0:T(8,128)S(1)}, u32[]{:S(2)}, u32[]{:S(2)}) %collective-permute-start.2) | collective-permute-done | bytes 61472 | tf_op jit(solution)/shard_map/ppermute | solution.py:17
  58.9 1.2 fusion.101
  60.0 2.2 %copy.84 = f32[5,20,12,2]{1,3,2,0:T(2,128)} copy(f32[5,20,12,2]{3,2,1,0:T(8,128)} %get-tuple-element.47) | data formatting | bytes 19200 | tf_op jit(solution)/shard_map/slice | solution.py:16
  62.2 3.8 %collective-permute-start.5 = (f32[5,20,12,2]{1,3,2,0:T(2,128)}, f32[5,20,12,2]{1,3,2,0:T(2,128)}, u32[]{:S(2)}, u32[]{:S(2)}) collective-permute-start(f32[5,20,12,2]{1,3,2,0:T(2,128)} %copy.84), channel_id=1, source_target_pairs={{16,0},{32,16},{48,32},{64,48},{80,64},{96,80},{112,96},{17,1},{33... | collective-permute-start | bytes 28808 | tf_op jit(solution)/shard_map/ppermute | solution.py:18
  66.0 1.1 copy.80
  67.1 2.0 %collective-permute-start.4 = (f32[5,20,12,2]{1,3,2,0:T(2,128)}, f32[5,20,12,2]{1,3,2,0:T(2,128)S(1)}, u32[]{:S(2)}, u32[]{:S(2)}) collective-permute-start(f32[5,20,12,2]{1,3,2,0:T(2,128)} %copy.80), channel_id=1, source_target_pairs={{0,16},{16,32},{32,48},{48,64},{64,80},{80,96},{96,112},{1,17},{17... | collective-permute-start | bytes 28808 | tf_op jit(solution)/shard_map/ppermute | solution.py:17
  69.2 1.0 constant_dynamic-update-slice_fusion.5
  70.1 0.9 slice.832
  71.3 2.1 %collective-permute-done.4 = f32[5,20,12,2]{1,3,2,0:T(2,128)S(1)} collective-permute-done((f32[5,20,12,2]{1,3,2,0:T(2,128)}, f32[5,20,12,2]{1,3,2,0:T(2,128)S(1)}, u32[]{:S(2)}, u32[]{:S(2)}) %collective-permute-start.4) | collective-permute-done | bytes 9632 | tf_op jit(solution)/shard_map/ppermute | solution.py:17
  75.1 0.7 copy-done.9
  77.3 7.3 %psum.15 = f32[8,128]{1,0:T(8,128)S(1)} all-reduce(f32[8,128]{1,0:T(8,128)S(1)} %fusion.98), channel_id=1, replica_groups=mesh['wn'=4,'sx'=8,'az'=16] {'wn'}, use_global_device_ids=true, to_apply=%region_1.2 | all-reduce | flops 1024 | bytes 8192 | tf_op jit(solution)/shard_map/psum | solution.py:25
  85.2 1.9 %collective-permute-start.17 = (f32[8,2]{1,0:T(8,128)S(1)}, f32[8,2]{1,0:T(8,128)S(1)}, u32[]{:S(2)}, u32[]{:S(2)}) collective-permute-start(f32[8,2]{1,0:T(8,128)S(1)} %get-tuple-element.92), channel_id=1, source_target_pairs={{16,0},{32,16},{48,32},{64,48},{80,64},{96,80},{112,96},{0,112},{1... | collective-permute-start | bytes 200 | tf_op jit(solution)/shard_map/ppermute | solution.py:18
  87.2 3.9 %collective-permute-start.16 = (f32[8,2]{1,0:T(8,128)S(1)}, f32[8,2]{1,0:T(8,128)S(1)}, u32[]{:S(2)}, u32[]{:S(2)}) collective-permute-start(f32[8,2]{1,0:T(8,128)S(1)} %get-tuple-element.91), channel_id=1, source_target_pairs={{0,16},{16,32},{32,48},{48,64},{64,80},{80,96},{96,112},{112,0},{1... | collective-permute-start | bytes 200 | tf_op jit(solution)/shard_map/ppermute | solution.py:17
  91.1 3.5 %collective-permute-done.16 = f32[8,2]{1,0:T(8,128)S(1)} collective-permute-done((f32[8,2]{1,0:T(8,128)S(1)}, f32[8,2]{1,0:T(8,128)S(1)}, u32[]{:S(2)}, u32[]{:S(2)}) %collective-permute-start.16) | collective-permute-done | bytes 96 | tf_op jit(solution)/shard_map/ppermute | solution.py:17
  94.7 3.0 %collective-permute-start.19 = (f32[2,132]{1,0:T(2,128)S(1)}, f32[2,132]{1,0:T(2,128)S(1)}, u32[]{:S(2)}, u32[]{:S(2)}) collective-permute-start(f32[2,132]{1,0:T(2,128)S(1)} %get-tuple-element.85), channel_id=1, source_target_pairs={{1,0},{2,1},{3,2},{4,3},{5,4},{6,5},{7,6},{8,7},{9,8},{10,9},{11,1... | collective-permute-start | bytes 3176 | tf_op jit(solution)/shard_map/ppermute | solution.py:18
  97.7 2.8 %collective-permute-start.18 = (f32[2,132]{1,0:T(2,128)S(1)}, f32[2,132]{1,0:T(2,128)S(1)}, u32[]{:S(2)}, u32[]{:S(2)}) collective-permute-start(f32[2,132]{1,0:T(2,128)S(1)} %get-tuple-element.84), channel_id=1, source_target_pairs={{0,1},{1,2},{2,3},{3,4},{4,5},{5,6},{6,7},{7,8},{8,9},{9,10},{10,1... | collective-permute-start | bytes 3176 | tf_op jit(solution)/shard_map/ppermute | solution.py:17
  100.6 5.1 %collective-permute-start.11 = (f32[5,16,2,128]{3,2,1,0:T(2,128)S(1)}, f32[5,16,2,128]{3,2,1,0:T(2,128)S(1)}, u32[]{:S(2)}, u32[]{:S(2)}) collective-permute-start(f32[5,16,2,128]{3,2,1,0:T(2,128)S(1)} %get-tuple-element.75), channel_id=1, source_target_pairs={{1,0},{2,1},{3,2},{4,3},{5,4},{6,5},{7,6},{8,7},{9,8},{10,9},{11,1... | collective-permute-start | bytes 245768 | tf_op jit(solution)/shard_map/ppermute | solution.py:18
  105.7 1.9 %collective-permute-start.10 = (f32[5,16,2,128]{3,2,1,0:T(2,128)S(1)}, f32[5,16,2,128]{3,2,1,0:T(2,128)S(1)}, u32[]{:S(2)}, u32[]{:S(2)}) collective-permute-start(f32[5,16,2,128]{3,2,1,0:T(2,128)S(1)} %get-tuple-element.74), channel_id=1, source_target_pairs={{0,1},{1,2},{2,3},{3,4},{4,5},{5,6},{6,7},{7,8},{8,9},{9,10},{10,1... | collective-permute-start | bytes 245768 | tf_op jit(solution)/shard_map/ppermute | solution.py:17
  107.6 1.2 copy.95
  110.6 3.6 %collective-permute-done.10 = f32[5,16,2,128]{3,2,1,0:T(2,128)S(1)} collective-permute-done((f32[5,16,2,128]{3,2,1,0:T(2,128)S(1)}, f32[5,16,2,128]{3,2,1,0:T(2,128)S(1)}, u32[]{:S(2)}, u32[]{:S(2)}) %collective-permute-start.10) | collective-permute-done | bytes 81952 | tf_op jit(solution)/shard_map/ppermute | solution.py:17
  114.2 1.9 %collective-permute-start.13 = (f32[5,2,12,128]{3,2,1,0:T(8,128)S(1)}, f32[5,2,12,128]{3,2,1,0:T(8,128)S(1)}, u32[]{:S(2)}, u32[]{:S(2)}) collective-permute-start(f32[5,2,12,128]{3,2,1,0:T(8,128)S(1)} %get-tuple-element.53), channel_id=1, source_target_pairs={{128,0},{256,128},{384,256},{129,1},{257,129},{385,257},{130,2},{2... | collective-permute-start | bytes 184328 | tf_op jit(solution)/shard_map/ppermute | solution.py:18
  116.1 2.4 %collective-permute-start.12 = (f32[5,2,12,128]{3,2,1,0:T(8,128)S(1)}, f32[5,2,12,128]{3,2,1,0:T(8,128)S(1)}, u32[]{:S(2)}, u32[]{:S(2)}) collective-permute-start(f32[5,2,12,128]{3,2,1,0:T(8,128)S(1)} %get-tuple-element.52), channel_id=1, source_target_pairs={{0,128},{128,256},{256,384},{1,129},{129,257},{257,385},{2,130},{1... | collective-permute-start | bytes 184328 | tf_op jit(solution)/shard_map/ppermute | solution.py:17
  118.9 4.5 %collective-permute-done.12 = f32[5,2,12,128]{3,2,1,0:T(8,128)S(1)} collective-permute-done((f32[5,2,12,128]{3,2,1,0:T(8,128)S(1)}, f32[5,2,12,128]{3,2,1,0:T(8,128)S(1)}, u32[]{:S(2)}, u32[]{:S(2)}) %collective-permute-start.12) | collective-permute-done | bytes 61472 | tf_op jit(solution)/shard_map/ppermute | solution.py:17
  123.9 1.2 fusion.100
  125.1 2.2 %copy.92 = f32[5,20,12,2]{1,3,2,0:T(2,128)} copy(f32[5,20,12,2]{3,2,1,0:T(8,128)} %get-tuple-element.45) | data formatting | bytes 19200 | tf_op jit(solution)/shard_map/slice | solution.py:16
  127.3 5.1 %collective-permute-start.15 = (f32[5,20,12,2]{1,3,2,0:T(2,128)}, f32[5,20,12,2]{1,3,2,0:T(2,128)}, u32[]{:S(2)}, u32[]{:S(2)}) collective-permute-start(f32[5,20,12,2]{1,3,2,0:T(2,128)} %copy.92), channel_id=1, source_target_pairs={{16,0},{32,16},{48,32},{64,48},{80,64},{96,80},{112,96},{17,1},{33... | collective-permute-start | bytes 28808 | tf_op jit(solution)/shard_map/ppermute | solution.py:18
  132.4 1.1 copy.88
  133.5 1.9 %collective-permute-start.14 = (f32[5,20,12,2]{1,3,2,0:T(2,128)}, f32[5,20,12,2]{1,3,2,0:T(2,128)S(1)}, u32[]{:S(2)}, u32[]{:S(2)}) collective-permute-start(f32[5,20,12,2]{1,3,2,0:T(2,128)} %copy.88), channel_id=1, source_target_pairs={{0,16},{16,32},{32,48},{48,64},{64,80},{80,96},{96,112},{1,17},{17... | collective-permute-start | bytes 28808 | tf_op jit(solution)/shard_map/ppermute | solution.py:17
  135.5 0.9 slice.886
  136.7 3.2 %collective-permute-done.14 = f32[5,20,12,2]{1,3,2,0:T(2,128)S(1)} collective-permute-done((f32[5,20,12,2]{1,3,2,0:T(2,128)}, f32[5,20,12,2]{1,3,2,0:T(2,128)S(1)}, u32[]{:S(2)}, u32[]{:S(2)}) %collective-permute-start.14) | collective-permute-done | bytes 9632 | tf_op jit(solution)/shard_map/ppermute | solution.py:17
  141.5 1.0 copy-done.5
  142.5 1.4 fusion.10
  (148 shorter events, 14.4 us)
Async XLA Ops:
  0.6 21.4 %copy-start = (f32[5,16,8,128]{3,2,1,0:T(8,128)S(1)}, f32[5,16,8,128]{3,2,1,0:T(8,128)}, u32[]{:S(2)}) copy-start(f32[5,16,8,128]{3,2,1,0:T(8,128)} %param.4) | copy-start | bytes 983044
  1.8 45.5 %collective-permute-start.1 = (f32[5,16,2,128]{3,2,1,0:T(2,128)S(1)}, f32[5,16,2,128]{3,2,1,0:T(2,128)S(1)}, u32[]{:S(2)}, u32[]{:S(2)}) collective-permute-start(f32[5,16,2,128]{3,2,1,0:T(2,128)S(1)} %get-tuple-element.79), channel_id=1, source_target_pairs={{1,0},{2,1},{3,2},{4,3},{5,4},{6,5},{7,6},{8,7},{9,8},{10,9},{11,1... | collective-permute-start | bytes 245768 | tf_op jit(solution)/shard_map/ppermute | solution.py:18
  13.4 34.0 %collective-permute-start = (f32[5,16,2,128]{3,2,1,0:T(2,128)S(1)}, f32[5,16,2,128]{3,2,1,0:T(2,128)S(1)}, u32[]{:S(2)}, u32[]{:S(2)}) collective-permute-start(f32[5,16,2,128]{3,2,1,0:T(2,128)S(1)} %get-tuple-element.78), channel_id=1, source_target_pairs={{0,1},{1,2},{2,3},{3,4},{4,5},{5,6},{6,7},{7,8},{8,9},{9,10},{10,1... | collective-permute-start | bytes 245768 | tf_op jit(solution)/shard_map/ppermute | solution.py:17
  16.2 14.9 %collective-permute-start.7 = (f32[8,2]{1,0:T(8,128)S(1)}, f32[8,2]{1,0:T(8,128)S(1)}, u32[]{:S(2)}, u32[]{:S(2)}) collective-permute-start(f32[8,2]{1,0:T(8,128)S(1)} %get-tuple-element.98), channel_id=1, source_target_pairs={{16,0},{32,16},{48,32},{64,48},{80,64},{96,80},{112,96},{0,112},{1... | collective-permute-start | bytes 200 | tf_op jit(solution)/shard_map/ppermute | solution.py:18
  18.5 12.6 %collective-permute-start.6 = (f32[8,2]{1,0:T(8,128)S(1)}, f32[8,2]{1,0:T(8,128)S(1)}, u32[]{:S(2)}, u32[]{:S(2)}) collective-permute-start(f32[8,2]{1,0:T(8,128)S(1)} %get-tuple-element.97), channel_id=1, source_target_pairs={{0,16},{16,32},{32,48},{48,64},{64,80},{80,96},{96,112},{112,0},{1... | collective-permute-start | bytes 200 | tf_op jit(solution)/shard_map/ppermute | solution.py:17
  22.0 0.7 copy-start.11
  30.5 0.7 copy-start.15
  31.3 10.3 %collective-permute-start.9 = (f32[2,132]{1,0:T(2,128)S(1)}, f32[2,132]{1,0:T(2,128)S(1)}, u32[]{:S(2)}, u32[]{:S(2)}) collective-permute-start(f32[2,132]{1,0:T(2,128)S(1)} %get-tuple-element.87), channel_id=1, source_target_pairs={{1,0},{2,1},{3,2},{4,3},{5,4},{6,5},{7,6},{8,7},{9,8},{10,9},{11,1... | collective-permute-start | bytes 3176 | tf_op jit(solution)/shard_map/ppermute | solution.py:18
  37.3 7.6 %collective-permute-start.8 = (f32[2,132]{1,0:T(2,128)S(1)}, f32[2,132]{1,0:T(2,128)S(1)}, u32[]{:S(2)}, u32[]{:S(2)}) collective-permute-start(f32[2,132]{1,0:T(2,128)S(1)} %get-tuple-element.86), channel_id=1, source_target_pairs={{0,1},{1,2},{2,3},{3,4},{4,5},{5,6},{6,7},{7,8},{8,9},{9,10},{10,1... | collective-permute-start | bytes 3176 | tf_op jit(solution)/shard_map/ppermute | solution.py:17
  39.3 6.7 %copy-start.22 = (f32[16]{0:T(128)}, f32[16]{0:T(128)S(1)}, u32[]{:S(2)}) copy-start(f32[16]{0:T(128)S(1)} %add_multiply_fusion.1) | copy-start | bytes 196
  47.4 4.7 %collective-permute-start.3 = (f32[5,2,12,128]{3,2,1,0:T(8,128)S(1)}, f32[5,2,12,128]{3,2,1,0:T(8,128)S(1)}, u32[]{:S(2)}, u32[]{:S(2)}) collective-permute-start(f32[5,2,12,128]{3,2,1,0:T(8,128)S(1)} %get-tuple-element.59), channel_id=1, source_target_pairs={{128,0},{256,128},{384,256},{129,1},{257,129},{385,257},{130,2},{2... | collective-permute-start | bytes 184328 | tf_op jit(solution)/shard_map/ppermute | solution.py:18
  49.3 7.3 %collective-permute-start.2 = (f32[5,2,12,128]{3,2,1,0:T(8,128)S(1)}, f32[5,2,12,128]{3,2,1,0:T(8,128)S(1)}, u32[]{:S(2)}, u32[]{:S(2)}) collective-permute-start(f32[5,2,12,128]{3,2,1,0:T(8,128)S(1)} %get-tuple-element.58), channel_id=1, source_target_pairs={{0,128},{128,256},{256,384},{1,129},{129,257},{257,385},{2,130},{1... | collective-permute-start | bytes 184328 | tf_op jit(solution)/shard_map/ppermute | solution.py:17
  52.0 4.6 %copy-start.1 = (f32[5,16,8,128]{3,2,1,0:T(8,128)S(1)}, f32[5,16,8,128]{3,2,1,0:T(8,128)}, u32[]{:S(2)}) copy-start(f32[5,16,8,128]{3,2,1,0:T(8,128)} %param.4) | copy-start | bytes 983044
  52.1 4.5 %slice-start = ((f32[5,16,8,128]{3,2,1,0:T(8,128)}), f32[5,2,8,128]{3,2,1,0:T(8,128)S(1)}, s32[]{:S(2)}) async-start(f32[5,16,8,128]{3,2,1,0:T(8,128)} %param.4), calls=%async_computation | async-start | bytes 81920 | tf_op jit(solution)/shard_map/slice | solution.py:117
  52.1 4.5 %copy-start.20 = (f32[5]{0:T(128)S(1)}, f32[5]{0:T(128)}, u32[]{:S(2)}) copy-start(f32[5]{0:T(128)} %constant.57.clone) | copy-start | bytes 64
  56.7 0.6 copy-start.8
  57.4 0.6 copy-start.6
  58.1 0.6 copy-start.7
  62.2 7.9 %collective-permute-start.5 = (f32[5,20,12,2]{1,3,2,0:T(2,128)}, f32[5,20,12,2]{1,3,2,0:T(2,128)}, u32[]{:S(2)}, u32[]{:S(2)}) collective-permute-start(f32[5,20,12,2]{1,3,2,0:T(2,128)} %copy.84), channel_id=1, source_target_pairs={{16,0},{32,16},{48,32},{64,48},{80,64},{96,80},{112,96},{17,1},{33... | collective-permute-start | bytes 28808 | tf_op jit(solution)/shard_map/ppermute | solution.py:18
  67.1 6.3 %collective-permute-start.4 = (f32[5,20,12,2]{1,3,2,0:T(2,128)}, f32[5,20,12,2]{1,3,2,0:T(2,128)S(1)}, u32[]{:S(2)}, u32[]{:S(2)}) collective-permute-start(f32[5,20,12,2]{1,3,2,0:T(2,128)} %copy.80), channel_id=1, source_target_pairs={{0,16},{16,32},{32,48},{48,64},{64,80},{80,96},{96,112},{1,17},{17... | collective-permute-start | bytes 28808 | tf_op jit(solution)/shard_map/ppermute | solution.py:17
  73.5 0.8 copy-start.12
  73.6 0.8 copy-start.14
  75.1 0.8 copy-start.9
  75.1 0.9 copy-start.10
  75.1 0.8 copy-start.17
  75.1 0.8 copy-start.18
  75.1 0.8 copy-start.16
  76.6 42.0 %copy-start.2 = (f32[5,16,8,128]{3,2,1,0:T(8,128)}, f32[5,16,8,128]{3,2,1,0:T(8,128)S(1)}, u32[]{:S(2)}) copy-start(f32[5,16,8,128]{3,2,1,0:T(8,128)S(1)} %fusion.22) | copy-start | bytes 983044
  76.6 0.7 copy-start.19
  85.2 5.8 %collective-permute-start.17 = (f32[8,2]{1,0:T(8,128)S(1)}, f32[8,2]{1,0:T(8,128)S(1)}, u32[]{:S(2)}, u32[]{:S(2)}) collective-permute-start(f32[8,2]{1,0:T(8,128)S(1)} %get-tuple-element.92), channel_id=1, source_target_pairs={{16,0},{32,16},{48,32},{64,48},{80,64},{96,80},{112,96},{0,112},{1... | collective-permute-start | bytes 200 | tf_op jit(solution)/shard_map/ppermute | solution.py:18
  87.2 7.5 %collective-permute-start.16 = (f32[8,2]{1,0:T(8,128)S(1)}, f32[8,2]{1,0:T(8,128)S(1)}, u32[]{:S(2)}, u32[]{:S(2)}) collective-permute-start(f32[8,2]{1,0:T(8,128)S(1)} %get-tuple-element.91), channel_id=1, source_target_pairs={{0,16},{16,32},{32,48},{48,64},{64,80},{80,96},{96,112},{112,0},{1... | collective-permute-start | bytes 200 | tf_op jit(solution)/shard_map/ppermute | solution.py:17
  94.7 14.6 %collective-permute-start.19 = (f32[2,132]{1,0:T(2,128)S(1)}, f32[2,132]{1,0:T(2,128)S(1)}, u32[]{:S(2)}, u32[]{:S(2)}) collective-permute-start(f32[2,132]{1,0:T(2,128)S(1)} %get-tuple-element.85), channel_id=1, source_target_pairs={{1,0},{2,1},{3,2},{4,3},{5,4},{6,5},{7,6},{8,7},{9,8},{10,9},{11,1... | collective-permute-start | bytes 3176 | tf_op jit(solution)/shard_map/ppermute | solution.py:18
  97.7 11.6 %collective-permute-start.18 = (f32[2,132]{1,0:T(2,128)S(1)}, f32[2,132]{1,0:T(2,128)S(1)}, u32[]{:S(2)}, u32[]{:S(2)}) collective-permute-start(f32[2,132]{1,0:T(2,128)S(1)} %get-tuple-element.84), channel_id=1, source_target_pairs={{0,1},{1,2},{2,3},{3,4},{4,5},{5,6},{6,7},{7,8},{8,9},{9,10},{10,1... | collective-permute-start | bytes 3176 | tf_op jit(solution)/shard_map/ppermute | solution.py:17
  100.6 10.0 %collective-permute-start.11 = (f32[5,16,2,128]{3,2,1,0:T(2,128)S(1)}, f32[5,16,2,128]{3,2,1,0:T(2,128)S(1)}, u32[]{:S(2)}, u32[]{:S(2)}) collective-permute-start(f32[5,16,2,128]{3,2,1,0:T(2,128)S(1)} %get-tuple-element.75), channel_id=1, source_target_pairs={{1,0},{2,1},{3,2},{4,3},{5,4},{6,5},{7,6},{8,7},{9,8},{10,9},{11,1... | collective-permute-start | bytes 245768 | tf_op jit(solution)/shard_map/ppermute | solution.py:18
  105.7 8.4 %collective-permute-start.10 = (f32[5,16,2,128]{3,2,1,0:T(2,128)S(1)}, f32[5,16,2,128]{3,2,1,0:T(2,128)S(1)}, u32[]{:S(2)}, u32[]{:S(2)}) collective-permute-start(f32[5,16,2,128]{3,2,1,0:T(2,128)S(1)} %get-tuple-element.74), channel_id=1, source_target_pairs={{0,1},{1,2},{2,3},{3,4},{4,5},{5,6},{6,7},{7,8},{8,9},{9,10},{10,1... | collective-permute-start | bytes 245768 | tf_op jit(solution)/shard_map/ppermute | solution.py:17
  109.8 0.6 copy-start.23
  114.2 4.7 %collective-permute-start.13 = (f32[5,2,12,128]{3,2,1,0:T(8,128)S(1)}, f32[5,2,12,128]{3,2,1,0:T(8,128)S(1)}, u32[]{:S(2)}, u32[]{:S(2)}) collective-permute-start(f32[5,2,12,128]{3,2,1,0:T(8,128)S(1)} %get-tuple-element.53), channel_id=1, source_target_pairs={{128,0},{256,128},{384,256},{129,1},{257,129},{385,257},{130,2},{2... | collective-permute-start | bytes 184328 | tf_op jit(solution)/shard_map/ppermute | solution.py:18
  116.1 7.3 %collective-permute-start.12 = (f32[5,2,12,128]{3,2,1,0:T(8,128)S(1)}, f32[5,2,12,128]{3,2,1,0:T(8,128)S(1)}, u32[]{:S(2)}, u32[]{:S(2)}) collective-permute-start(f32[5,2,12,128]{3,2,1,0:T(8,128)S(1)} %get-tuple-element.52), channel_id=1, source_target_pairs={{0,128},{128,256},{256,384},{1,129},{129,257},{257,385},{2,130},{1... | collective-permute-start | bytes 184328 | tf_op jit(solution)/shard_map/ppermute | solution.py:17
  118.8 4.6 %copy-start.3 = (f32[5,16,8,128]{3,2,1,0:T(8,128)S(1)}, f32[5,16,8,128]{3,2,1,0:T(8,128)}, u32[]{:S(2)}) copy-start(f32[5,16,8,128]{3,2,1,0:T(8,128)} %copy-done.2) | copy-start | bytes 983044
  118.9 4.7 %copy-start.4 = (f32[5,16,12,128]{3,2,1,0:T(8,128)}, f32[5,16,12,128]{3,2,1,0:T(8,128)S(1)}, u32[]{:S(2)}) copy-start(f32[5,16,12,128]{3,2,1,0:T(8,128)S(1)} %multiply_dynamic-update-slice_fusion) | copy-start | bytes 1474564
  118.9 4.5 %slice-start.1 = ((f32[5,16,8,128]{3,2,1,0:T(8,128)}), f32[5,2,8,128]{3,2,1,0:T(8,128)S(1)}, s32[]{:S(2)}) async-start(f32[5,16,8,128]{3,2,1,0:T(8,128)} %copy-done.2), calls=%async_computation.1 | async-start | bytes 81920 | tf_op jit(solution)/shard_map/slice | solution.py:117
  118.9 4.5 %copy-start.21 = (f32[5]{0:T(128)S(1)}, f32[5]{0:T(128)}, u32[]{:S(2)}) copy-start(f32[5]{0:T(128)} %constant.57.clone) | copy-start | bytes 64
  127.3 8.2 %collective-permute-start.15 = (f32[5,20,12,2]{1,3,2,0:T(2,128)}, f32[5,20,12,2]{1,3,2,0:T(2,128)}, u32[]{:S(2)}, u32[]{:S(2)}) collective-permute-start(f32[5,20,12,2]{1,3,2,0:T(2,128)} %copy.92), channel_id=1, source_target_pairs={{16,0},{32,16},{48,32},{64,48},{80,64},{96,80},{112,96},{17,1},{33... | collective-permute-start | bytes 28808 | tf_op jit(solution)/shard_map/ppermute | solution.py:18
  133.5 6.3 %collective-permute-start.14 = (f32[5,20,12,2]{1,3,2,0:T(2,128)}, f32[5,20,12,2]{1,3,2,0:T(2,128)S(1)}, u32[]{:S(2)}, u32[]{:S(2)}) collective-permute-start(f32[5,20,12,2]{1,3,2,0:T(2,128)} %copy.88), channel_id=1, source_target_pairs={{0,16},{16,32},{32,48},{48,64},{64,80},{80,96},{96,112},{1,17},{17... | collective-permute-start | bytes 28808 | tf_op jit(solution)/shard_map/ppermute | solution.py:17
  139.9 0.8 copy-start.13
  141.4 1.1 copy-start.5
where the time goes:
time: 145 us; the launch traced here: 144 us
  starting transfers between devices  67.5 us (47%)
  local copies, waits for them, and re-layouts  25.5 us (18%)
  waiting for transfers between devices  24.6 us (17%)
  blocking collectives  14.4 us (10%)
  other arithmetic  10.4 us (7%)
  between operations  1.49 us (1%)
    ppermute x10, starting transfers between devices, extended(): after = lax.ppermute(initial, axis, down)  42.7 us
    ppermute x10, starting transfers between devices, extended(): before = lax.ppermute(last, axis, up)  24.8 us
    ppermute x10, waiting for transfers between devices, extended(): before = lax.ppermute(last, axis, up)  24.6 us
    psum x2, blocking collectives, spread(): return lax.psum(kept, axis)  14.4 us
    unnamed x58, local copies, waits for them, and re-layouts  7.62 us
    slice x8, local copies, waits for them, and re-layouts, extended(): last = lax.slice_in_dim(x, length - width, length, axis=dim)  6.65 us
    slice x2, local copies, waits for them, and re-layouts, extended(): initial = lax.slice_in_dim(x, 0, width, axis=dim)  4.43 us
  transfers between devices with their start and end apart: 20, of which 7 were waited for; matrix products, arithmetic and copies ran while one was open for 11% of the time, Pallas kernels for 0%

commit v1 on v0

v1 whole, which is shorter than its diff:
```python
import functools

import jax
import jax.numpy as jnp
from jax import lax
from jax.experimental import pallas as pl
from jax.experimental.pallas import tpu as pltpu
from jax.sharding import PartitionSpec as P

GAMMA = 1.4
CFL_STEP = 0.08
LAYERS = 64
NL = 16
NP = 86
HALF = 43
SCALE = LAYERS / 12.0
STEP = CFL_STEP / LAYERS
C = CFL_STEP / 12.0
VM = pl.BlockSpec(memory_space=pltpu.VMEM)
F32 = jnp.float32
MIRROR = (1.0, -1.0, -1.0, -1.0, 1.0)


def lane():
    return lax.broadcasted_iota(jnp.int32, (8, 128), 1)


def row():
    return lax.broadcasted_iota(jnp.int32, (8, 128), 0)


def rl(x, shift):
    return pltpu.roll(x, shift % 128, 1) if shift % 128 else x


def rs(x, shift):
    return pltpu.roll(x, shift % 8, 0) if shift % 8 else x


def d_lane(x):
    return (rl(x, 2) - rl(x, -2)) + 8.0 * (rl(x, -1) - rl(x, 1))


def strip_patch(d):
    off = lane() & 15
    return jnp.where((off == 12) | (off == 13), rl(d, 8), d)


def strip_ends(x):
    off = lane() & 15
    return jnp.where((off == 10) | (off == 11), rl(x, 8), x)


def d_ends(x, e):
    ln = lane()
    p1 = rl(jnp.where(ln < 1, e, x), -1)
    p2 = rl(jnp.where(ln < 2, e, x), -2)
    m1 = rl(jnp.where(ln >= 127, e, x), 1)
    m2 = rl(jnp.where(ln >= 126, e, x), 2)
    return (m2 - p2) + 8.0 * (p1 - m1)


def patched(d, patch):
    ln = lane()
    return jnp.where((ln < 2) | (ln >= 126), patch, d)


def ring(x, z, shift):
    keep = row() >= shift if shift > 0 else row() < 8 + shift
    a, b = rs(x, shift), rs(z, shift)
    return jnp.where(keep, a, b), jnp.where(keep, b, a)


def d_ring(x, z):
    m2, m1, p1, p2 = ring(x, z, 2), ring(x, z, 1), ring(x, z, -1), ring(x, z, -2)
    return tuple((m2[i] - p2[i]) + 8.0 * (p1[i] - m1[i]) for i in (0, 1))


def spread(x, group):
    ln = lane()
    x = rl(x, -16 * group)
    x = jnp.where(ln < 16, x, rl(x, 16))
    x = jnp.where(ln < 32, x, rl(x, 32))
    return jnp.where(ln < 64, x, rl(x, 64))


def pressure(q):
    kinetic = (q[1] * q[1] + q[2] * q[2] + q[3] * q[3]) / q[0]
    return (GAMMA - 1.0) * (q[4] - 0.5 * kinetic)


def speed(q, b):
    behind = pressure(b)
    return (pressure(q) - behind) / jnp.sqrt(GAMMA * behind * b[0])


def fluxes(q, want=(1, 2, 3)):
    inv = 1.0 / q[0]
    v = [None, q[1] * inv, q[2] * inv, q[3] * inv]
    q11, q22, q33 = q[1] * v[1], q[2] * v[2], q[3] * v[3]
    p = (GAMMA - 1.0) * (q[4] - 0.5 * (q11 + q22 + q33))
    e = q[4] + p
    out = []
    if 1 in want:
        out.append([q[1], q11 + p, q[2] * v[1], q[3] * v[1], e * v[1]])
    if 2 in want:
        out.append([q[2], q[1] * v[2], q22 + p, q[3] * v[2], e * v[2]])
    if 3 in want:
        out.append([q[3], q[1] * v[3], q[2] * v[3], q33 + p, e * v[3]])
    return out


def moving(f1, f3, q, hx, hz, w):
    return [hx * f1[f] + hz * f3[f] + w * q[f] for f in range(5)]


def slopes(h, hz, hs, hsz):
    ds, dsz = d_lane(hs), d_lane(hsz)
    x = SCALE * patched(d_lane(h), rl(strip_patch(ds), -12))
    xz = SCALE * patched(d_lane(hz), rl(strip_patch(dsz), -12))
    a, az = d_ring(h, hz)
    s, _ = d_ring(hs, hsz)
    return (x, SCALE * a), (xz, SCALE * az), (SCALE * ds, SCALE * s)


def plane_of(q, h, b):
    def get(i):
        if i < 80:
            return q[i // NL, i % NL]
        return h[...] if i == 80 else b[i - 81]

    return get


def pack_rows(q, h, b, up, dn):
    get = plane_of(q, h, b)
    high = row() >= 4
    for i in range(HALF):
        x, y = get(i), rs(get(i + HALF), 4)
        up[i] = jnp.where(high, x, y)
        dn[i] = jnp.where(high, y, x)


def pack_columns(q, h, b, u, d, z, right, left):
    get = plane_of(q, h, b)
    high = row() >= 4
    ln = lane()
    for i in range(HALF):
        x, y = u[i], d[i]
        z[i] = jnp.where(high, x, y)
        z[i + HALF] = rs(jnp.where(high, y, x), 4)
    for v in range(6):
        r_acc = jnp.zeros((8, 128), F32)
        l_acc = jnp.zeros((8, 128), F32)
        slots = (
            [(j, t, v * NL + j + 8 * (t & 1), t >= 2) for j in range(8) for t in range(4)]
            if v < 5
            else [(j, t, 80 + j, t >= 2) for j in range(6) for t in (0, 2)]
        )
        for j, t, i, halo in slots:
            at = 16 * j + 4 * t
            x = rl(z[i] if halo else get(i), at + 4)
            r_acc = jnp.where((ln >= at) & (ln < at + 4), x, r_acc)
            at = (at + 4) % 128
            l_acc = jnp.where((ln >= at) & (ln < at + 4), x, l_acc)
        right[v] = r_acc
        left[v] = rl(l_acc, -4)


def pack_layers(first, last, q, h, b, z, right, left, lh_ref, rh_ref, hi, lo, w, strips):
    ln, rw = lane(), row()
    m = ln & 3
    quad = (ln >> 2) & 3
    for v in range(6):
        lm, rm = left[v], right[v]
        end_l = jnp.where(m == 0, lm, jnp.where(m == 1, rl(lm, 1), jnp.where(m == 2, rl(lm, 2), rl(lm, 3))))
        end_r = jnp.where(m == 3, rm, jnp.where(m == 2, rl(rm, -1), jnp.where(m == 1, rl(rm, -2), rl(rm, -3))))
        lh = jnp.where(first, end_l, lh_ref[v])
        rh = jnp.where(last, end_r, rh_ref[v])
        for t in range(4) if v < 5 else (0, 2):
            parts = [rl(x, 4 * (i - t)) for i, x in enumerate((lh, lm, rm, rh))]
            strips[4 * v + t if v < 5 else 20 + t // 2] = jnp.where(
                quad < 2, jnp.where(quad == 0, parts[0], parts[1]), jnp.where(quad == 2, parts[2], parts[3])
            )
    surf, surf_z = strips[20], strips[21]
    own, bq = [q[f, 15] for f in range(5)], [b[f] for f in range(5)]
    zq, bz = [z[f * NL + 15] for f in range(5)], [z[81 + f] for f in range(5)]
    sq = [strips[4 * f + 1] for f in range(5)]
    w0 = speed(own, bq)
    w0z = speed(zq, bz)
    w0s = spread(speed(sq, [rl(surf, 16 * (6 - f)) for f in range(5)]), 7)
    (hx, hz), _, _ = slopes(h[...], z[80], spread(surf, 0), spread(surf_z, 0))
    (s1,) = fluxes(sq, (1,))
    (z3,) = fluxes(zq, (3,))
    near = []
    for x in ([q[f, 13] for f in range(5)], [q[f, 14] for f in range(5)], own, bq):
        f1, f2, f3 = fluxes(x)
        near.append((f1, f2, f3, moving(f1, f3, x, hx, hz, w0)))
    eta = (LAYERS - 0.5) / LAYERS
    ih = 1.0 / h[...]
    top = []
    for f in range(5):
        dx = patched(d_lane(near[2][0][f]), rl(strip_patch(d_lane(s1[f])), -124))
        da, _ = d_ring(near[2][2][f], z3[f])
        dn, dg = ((near[0][k][f] - 8.0 * near[1][k][f]) + 7.0 * near[3][k][f] for k in (1, 3))
        top.append(own[f] + C * (ih * (eta * dg - dn) - (dx + da)))
    w1 = speed(top, bq)
    speeds = (w0, w0z, w0s, w1)
    for k in range(4):
        w[k] = speeds[k]
        hi[27 + k] = speeds[k]
        lo[27 + k] = speeds[k]
    near_rows = (rw < 2) | (rw >= 6)
    hi_s = strips[4 * 4 + 1]
    lo_s = strips[4 * 4]
    hi[26] = hi_s
    lo[26] = lo_s
    for f in range(5):
        for k in range(4):
            hi[4 * f + k] = q[f, 12 + k]
            lo[4 * f + k] = q[f, k]
        hi[20 + f] = jnp.where(near_rows, z[f * NL + 14], rs(z[f * NL + 15], 4))
        lo[20 + f] = jnp.where(near_rows, z[f * NL], rs(z[f * NL + 1], 4))
        if f < 4:
            inside = (ln >= 32 * f) & (ln < 32 * f + 32)
            hi_s = jnp.where(inside, rl(strips[4 * f + 1], 32 * f + 32), hi_s)
            lo_s = jnp.where(inside, rl(strips[4 * f], 32 * f), lo_s)
    hi[25] = hi_s
    lo[25] = lo_s


def advance(wn, first, last, q, h, b, z, strips, w, below, above, cross, out, h_out, *scratch):
    qx, qz, f1x, f2x, f3x, gx, f1z, f2z, f3z, gz, sx, sz, pt, ptz = scratch
    ln, rw = lane(), row()
    group, off = ln >> 4, ln & 15
    bottom, top = wn == 0, wn == 3
    near_rows = (rw < 2) | (rw >= 6)

    speeds = []
    for k in range(4):
        a = jnp.where(bottom, below[27 + k], cross[k])
        c = jnp.where(top, w[k], above[27 + k])
        speeds.append(jnp.where(wn < 2, a, c))
    w0, w0z, w0s, w1 = speeds

    surf, surf_z = strips[20], strips[21]
    strip_q = []
    for f in range(5):
        sign = MIRROR[f]
        bq, bz = b[f], z[81 + f]
        for k in range(NL):
            qx[f, 4 + k] = q[f, k]
            qz[f, 2 + k] = z[f * NL + k]
        for k in range(4):
            qx[f, k] = jnp.where(bottom, sign * q[f, 3 - k], below[4 * f + k])
            qx[f, 20 + k] = jnp.where(top, bq, above[4 * f + k])
        zb, za = below[20 + f], above[20 + f]
        qz[f, 0] = jnp.where(bottom, sign * z[f * NL + 1], zb)
        qz[f, 1] = jnp.where(bottom, sign * z[f * NL], rs(zb, 4))
        qz[f, 18] = jnp.where(top, bz, za)
        qz[f, 19] = jnp.where(top, bz, rs(za, 4))
        s_lo, s_hi = strips[4 * f], strips[4 * f + 1]
        if f < 4:
            sb, sa = rl(below[25], 96 - 32 * f), rl(above[25], -32 * f)
        else:
            sb, sa = below[26], above[26]
        sb = jnp.where(bottom, sign * jnp.where(group == 7, rl(s_lo, -16), rl(s_lo, 80)), sb)
        sa = jnp.where(top, spread(surf, 1 + f), sa)
        strip_q.append((s_lo, s_hi, jnp.where(ln < 64, sa, sb)))

    h0, h0z = h[...], z[80]
    h0s, h0sz = spread(surf, 0), spread(surf_z, 0)
    (hx, hz), (hxz, hzz), (hxs, hzs) = slopes(h0, h0z, h0s, h0sz)
    ih, ihz, ihs = 1.0 / h0, 1.0 / h0z, 1.0 / h0s
    base = wn * NL

    parts = []
    for v in range(3):
        x = [strip_q[f][v] for f in range(5)]
        f1, f2, f3 = fluxes(x)
        d1 = [d_lane(f1[f]) for f in range(5)]
        for f in range(5):
            pt[f, v] = strip_patch(d1[f])
        parts.append((d1, f2, f3, moving(f1, f3, x, hxs, hzs, w0s)))
    halo3 = []
    for v in range(2):
        x = [strips[4 * f + 2 + v] for f in range(5)]
        z1, z3 = fluxes(x, (1, 3))
        for f in range(5):
            ptz[f, v] = strip_patch(d_lane(z1[f]))
        halo3.append(z3)

    def layer_shift(x, v, k):
        a = rl(x[v], -16 * k)
        c = rl(x[(v + (1 if k > 0 else -1)) % 3], -16 * k)
        return jnp.where(ln < 128 - 16 * k if k > 0 else ln >= -16 * k, a, c)

    strip_s = []
    for v in range(2):
        eta = ((base + 8 * v + group).astype(F32) + 0.5) / LAYERS
        done = []
        for f in range(5):
            dn, dg = (
                (layer_shift(x, v, -2) - layer_shift(x, v, 2)) + 8.0 * (layer_shift(x, v, 1) - layer_shift(x, v, -1))
                for x in ([parts[i][k][f] for i in range(3)] for k in (1, 3))
            )
            da, _ = d_ring(parts[v][2][f], halo3[v][f])
            s = strip_q[f][v] + C * (ihs * (eta * dg - dn) - (parts[v][0][f] + da))
            s = jnp.where(first & ((off == 2) | (off == 3)), jnp.where(off == 3, rl(s, -1), rl(s, -2)), s)
            s = jnp.where(last & ((off == 12) | (off == 13)), jnp.where(off == 12, rl(s, 1), rl(s, 2)), s)
            done.append(s)
        strip_s.append(done)

    def own_flux(l, _):
        x = [qx[f, l] for f in range(5)]
        f1, f2, f3 = fluxes(x)
        g = moving(f1, f3, x, hx, hz, w0)
        for f in range(5):
            f1x[f, l], f2x[f, l], f3x[f, l], gx[f, l] = f1[f], f2[f], f3[f], g[f]
        return 0

    def halo_flux(l, _):
        x = [qz[f, l] for f in range(5)]
        f1, f2, f3 = fluxes(x)
        g = moving(f1, f3, x, hxz, hzz, w0z)
        for f in range(5):
            f1z[f, l], f2z[f, l], f3z[f, l], gz[f, l] = f1[f], f2[f], f3[f], g[f]
        return 0

    lax.fori_loop(0, 24, own_flux, 0, unroll=2)
    lax.fori_loop(0, 20, halo_flux, 0, unroll=2)

    def d_normal(ref, f, l):
        return (ref[f, l - 2] - ref[f, l + 2]) + 8.0 * (ref[f, l + 1] - ref[f, l - 1])

    def eta_of(l):
        return ((base + l).astype(F32) + 0.5) / LAYERS

    def patch_shift(l):
        return 116 - 16 * (l & 7)

    def own_edge(l):
        eta = eta_of(l)
        for f in range(5):
            dx = patched(d_lane(f1x[f, l + 4]), pltpu.roll(pt[f, 2], patch_shift(l), 1))
            da, _ = d_ring(f3x[f, l + 4], f3z[f, l + 2])
            dn, dg = d_normal(f2x, f, l + 4), d_normal(gx, f, l + 4)
            sx[f, l + 2] = qx[f, l + 4] + C * (ih * (eta * dg - dn) - (dx + da))

    def section(l, _):
        eta = eta_of(l)
        half = l >> 3
        shift = patch_shift(l)
        for f in range(5):
            dx = patched(d_lane(f1x[f, l + 4]), pltpu.roll(pt[f, half], shift, 1))
            dxz = patched(d_lane(f1z[f, l + 2]), pltpu.roll(ptz[f, half], shift, 1))
            da, daz = d_ring(f3x[f, l + 4], f3z[f, l + 2])
            dn, dg = d_normal(f2x, f, l + 4), d_normal(gx, f, l + 4)
            sx[f, l + 2] = qx[f, l + 4] + C * (ih * (eta * dg - dn) - (dx + da))
            dn, dg = d_normal(f2z, f, l + 2), d_normal(gz, f, l + 2)
            sz[f, l] = qz[f, l + 2] + C * (ihz * (eta * dg - dn) - (dxz + daz))
        return 0

    lax.fori_loop(0, NL, section, 0)
    for l in (-2, -1, 16, 17):
        own_edge(l)
    for f in range(5):
        for k in range(2):
            sx[f, k] = jnp.where(bottom, MIRROR[f] * sx[f, 3 - k], sx[f, k])
            sx[f, 18 + k] = jnp.where(top, b[f], sx[f, 18 + k])

    h1, h1z, h1s = h0 + STEP * w0, h0z + STEP * w0z, h0s + STEP * w0s
    hx1 = SCALE * d_ends(h1, rl(strip_ends(h1s), -12))
    hz1 = SCALE * d_ring(h1, h1z)[0]
    ih1 = 1.0 / h1
    h_out[...] = 0.5 * (h0 + h1 + STEP * w1)
    for v in range(2):
        (f1,) = fluxes(strip_s[v], (1,))
        for f in range(5):
            pt[f, v] = strip_ends(f1[f])

    def own_flux_two(l, _):
        x = [sx[f, l] for f in range(5)]
        f1, f2, f3 = fluxes(x)
        g = moving(f1, f3, x, hx1, hz1, w1)
        for f in range(5):
            f1x[f, l], f2x[f, l], f3x[f, l], gx[f, l] = f1[f], f2[f], f3[f], g[f]
        return 0

    def halo_flux_two(l, _):
        (f3,) = fluxes([sz[f, l] for f in range(5)], (3,))
        for f in range(5):
            f3z[f, l] = f3[f]
        return 0

    lax.fori_loop(0, 20, own_flux_two, 0, unroll=2)
    lax.fori_loop(0, NL, halo_flux_two, 0, unroll=2)

    def final(l, _):
        eta = eta_of(l)
        half = l >> 3
        shift = patch_shift(l)
        for f in range(5):
            dx = d_ends(f1x[f, l + 2], pltpu.roll(pt[f, half], shift, 1))
            da, _ = d_ring(f3x[f, l + 2], f3z[f, l])
            dn, dg = d_normal(f2x, f, l + 2), d_normal(gx, f, l + 2)
            rate = ih1 * (eta * dg - dn) - (dx + da)
            out[f, l] = 0.5 * (qx[f, l + 4] + sx[f, l + 2] + C * rate)
        return 0

    lax.fori_loop(0, NL, final, 0)


def call(body, ins, outs, scratch=()):
    shapes = tuple(jax.ShapeDtypeStruct(s, F32) for s in outs)
    return pl.pallas_call(
        body,
        out_shape=shapes,
        in_specs=[VM] * len(ins),
        out_specs=tuple([VM] * len(shapes)),
        scratch_shapes=[pltpu.VMEM(s, F32) for s in scratch],
        compiler_params=pltpu.CompilerParams(vmem_limit_bytes=40 * 1024 * 1024),
    )(*ins)


def stage_layers(*refs):
    tile, tiles = lax.axis_index("sx"), lax.axis_size("sx")
    pack_layers(tile == 0, tile == tiles - 1, *refs)


def stage_advance(*refs):
    tile, tiles = lax.axis_index("sx"), lax.axis_size("sx")
    advance(lax.axis_index("wn"), tile == 0, tile == tiles - 1, *refs)


def per_device(fields, height, behind):
    around = lax.axis_size("az")
    tiles = lax.axis_size("sx")
    own = (fields, height, behind)
    up, dn = call(pack_rows, own, [(HALF, 8, 128)] * 2)
    from_low = lax.ppermute(up, "az", [(i, (i + 1) % around) for i in range(around)])
    from_high = lax.ppermute(dn, "az", [((i + 1) % around, i) for i in range(around)])
    halo, right, left = call(
        pack_columns, (*own, from_low, from_high), [(NP, 8, 128), (6, 8, 128), (6, 8, 128)]
    )
    from_left = lax.ppermute(right, "sx", [(i, i + 1) for i in range(tiles - 1)])
    from_right = lax.ppermute(left, "sx", [(i + 1, i) for i in range(tiles - 1)])
    hi, lo, w, strips = call(
        stage_layers,
        (*own, halo, right, left, from_left, from_right),
        [(31, 8, 128), (31, 8, 128), (4, 8, 128), (22, 8, 128)],
    )
    below = lax.ppermute(hi, "wn", [(0, 1), (1, 2), (2, 3), (3, 0)])
    above = lax.ppermute(lo, "wn", [(1, 0), (2, 1), (3, 2)])
    cross = lax.ppermute(w, "wn", [(3, 1)])
    return call(
        stage_advance,
        (*own, halo, strips, w, below, above, cross),
        [(5, NL, 8, 128), (8, 128)],
        [(5, 24, 8, 128), (5, 20, 8, 128)]
        + [(5, 24, 8, 128)] * 4
        + [(5, 20, 8, 128)] * 4
        + [(5, 20, 8, 128), (5, NL, 8, 128), (5, 3, 8, 128), (5, 2, 8, 128)],
    )


def solution(mesh):
    in_specs = (P(None, "wn", "az", "sx"), P("az", "sx"), P(None, "az", "sx"))
    out_specs = (P(None, "wn", "az", "sx"), P("az", "sx"))
    return jax.shard_map(
        per_device, mesh=mesh, in_specs=in_specs, out_specs=out_specs, check_vma=False
    )
```

time: 145 us -> 54.3 us (0.37)
  the two profiles are of different devices: /device:TPU:12 before, /device:TPU:25 now
where the time goes in v1:
time: 54.3 us; the launch traced here: 53.9 us
  starting transfers between devices  30.3 us (56%)
  waiting for transfers between devices  11.7 us (22%)
  Pallas kernels  8.91 us (16%)
  local copies, waits for them, and re-layouts  2.38 us (4%)
  between operations  0.72 us (1%)
    ppermute x1, starting transfers between devices, per_device(): lax.ppermute(dn, 'az', [((i + 1) % around, i) for i in range(around)])  10.4 us
    pallas_call x4, Pallas kernels, call(): pl.pallas_call(body, out_shape=shapes, in_specs=[VM] * len(ins), out_spec...  8.91 us
    ppermute x1, starting transfers between devices, per_device(): below = lax.ppermute(hi, 'wn', [(0, 1), (1, 2), (2, 3), (3, 0)])  7.22 us
    ppermute x1, waiting for transfers between devices, per_device(): cross = lax.ppermute(w, 'wn', [(3, 1)])  4.69 us
    ppermute x1, starting transfers between devices, per_device(): lax.ppermute(right, 'sx', [(i, i + 1) for i in range(tiles - 1)])  4.41 us
    ppermute x1, waiting for transfers between devices, per_device(): lax.ppermute(left, 'sx', [(i + 1, i) for i in range(tiles - 1)])  3.84 us
    ppermute x1, starting transfers between devices, per_device(): lax.ppermute(up, 'az', [(i, (i + 1) % around) for i in range(around)])  3.12 us
    unnamed x6, local copies, waits for them, and re-layouts  2.38 us
  transfers between devices with their start and end apart: 7, of which 4 were waited for; matrix products, arithmetic and copies ran while one was open for 0% of the time, Pallas kernels for 0%

profile of v1, /device:TPU:25, one launch (start us, length us, event | category | flops | bytes accessed | tf_op | source)
XLA Modules:
  0.0 53.9 jit_solution(3321176442659570189)
XLA Ops:
  0.6 0.0 copy-start
  0.6 1.0 %copy-done = f32[5,16,8,128]{3,2,1,0:T(8,128)S(1)} copy-done((f32[5,16,8,128]{3,2,1,0:T(8,128)S(1)}, f32[5,16,8,128]{3,2,1,0:T(8,128)}, u32[]{:S(2)}) %copy-start) | copy-done | bytes 327704
  1.6 0.0 copy-start.1
  1.6 0.7 %copy-done.1 = f32[5,8,128]{2,1,0:T(8,128)S(1)} copy-done((f32[5,8,128]{2,1,0:T(8,128)S(1)}, f32[5,8,128]{2,1,0:T(8,128)}, u32[]{:S(2)}) %copy-start.1) | copy-done | bytes 20504
  2.3 0.0 copy-start.2
  2.3 0.7 %copy-done.2 = f32[8,128]{1,0:T(8,128)S(1)} copy-done((f32[8,128]{1,0:T(8,128)S(1)}, f32[8,128]{1,0:T(8,128)}, u32[]{:S(2)}) %copy-start.2) | copy-done | bytes 4120
  3.0 3.1 %collective-permute-start = (f32[43,8,128]{2,1,0:T(8,128)S(1)}, f32[43,8,128]{2,1,0:T(8,128)S(1)}, u32[]{:S(2)}, u32[]{:S(2)}) collective-permute-start(f32[43,8,128]{2,1,0:T(8,128)S(1)} %get-tuple-element.11), channel_id=1, source_target_pairs={{0,1},{1,2},{2,3},{3,4},{4,5},{5,6},{6,7},{7,8},{8,9},{9,10},{10,1... | collective-permute-start | bytes 528392 | tf_op jit(solution)/shard_map/ppermute | solution.py:441
  6.2 10.4 %collective-permute-start.1 = (f32[43,8,128]{2,1,0:T(8,128)S(1)}, f32[43,8,128]{2,1,0:T(8,128)S(1)}, u32[]{:S(2)}, u32[]{:S(2)}) collective-permute-start(f32[43,8,128]{2,1,0:T(8,128)S(1)} %get-tuple-element.12), channel_id=1, source_target_pairs={{1,0},{2,1},{3,2},{4,3},{5,4},{6,5},{7,6},{8,7},{9,8},{10,9},{11,1... | collective-permute-start | bytes 528392 | tf_op jit(solution)/shard_map/ppermute | solution.py:442
  16.6 2.2 %collective-permute-done.u = f32[43,8,128]{2,1,0:T(8,128)S(1)} collective-permute-done((f32[43,8,128]{2,1,0:T(8,128)S(1)}, f32[43,8,128]{2,1,0:T(8,128)S(1)}, u32[]{:S(2)}, u32[]{:S(2)}) %collective-permute-start) | collective-permute-done | bytes 176160 | tf_op jit(solution)/shard_map/ppermute | solution.py:441
  18.8 0.9 %collective-permute-done.1.d = f32[43,8,128]{2,1,0:T(8,128)S(1)} collective-permute-done((f32[43,8,128]{2,1,0:T(8,128)S(1)}, f32[43,8,128]{2,1,0:T(8,128)S(1)}, u32[]{:S(2)}, u32[]{:S(2)}) %collective-permute-start.1) | collective-permute-done | bytes 176160 | tf_op jit(solution)/shard_map/ppermute | solution.py:442
  19.7 0.4 shard_map.51
  20.0 4.4 %collective-permute-start.2 = (f32[6,8,128]{2,1,0:T(8,128)S(1)}, f32[6,8,128]{2,1,0:T(8,128)S(1)}, u32[]{:S(2)}, u32[]{:S(2)}) collective-permute-start(f32[6,8,128]{2,1,0:T(8,128)S(1)} %get-tuple-element.14.refs_4_), channel_id=1, source_target_pairs={{0,16},{16,32},{32,48},{48,64},{64,80},{80,96},{96,112},{1,17},{17... | collective-permute-start | bytes 73736 | tf_op jit(solution)/shard_map/ppermute | solution.py:446
  24.5 1.9 %collective-permute-start.3 = (f32[6,8,128]{2,1,0:T(8,128)S(1)}, f32[6,8,128]{2,1,0:T(8,128)S(1)}, u32[]{:S(2)}, u32[]{:S(2)}) collective-permute-start(f32[6,8,128]{2,1,0:T(8,128)S(1)} %get-tuple-element.15.refs_5_), channel_id=1, source_target_pairs={{16,0},{32,16},{48,32},{64,48},{80,64},{96,80},{112,96},{17,1},{33... | collective-permute-start | bytes 73736 | tf_op jit(solution)/shard_map/ppermute | solution.py:447
  26.4 0.0 collective-permute-done.2.refs_6_
  26.4 3.8 %collective-permute-done.3.refs_7_ = f32[6,8,128]{2,1,0:T(8,128)S(1)} collective-permute-done((f32[6,8,128]{2,1,0:T(8,128)S(1)}, f32[6,8,128]{2,1,0:T(8,128)S(1)}, u32[]{:S(2)}, u32[]{:S(2)}) %collective-permute-start.3) | collective-permute-done | bytes 24608 | tf_op jit(solution)/shard_map/ppermute | solution.py:447
  30.2 0.6 %shard_map.52 = (f32[31,8,128]{2,1,0:T(8,128)S(1)}, f32[31,8,128]{2,1,0:T(8,128)S(1)}, f32[4,8,128]{2,1,0:T(8,128)S(1)}, f32[22,8,128]{2,1,0:T(8,128)S(1)}) custom-call(f32[5,16,8,128]{3,2,1,0:T(8,128)S(1)} %copy-done, f32[8,128]{1,0:T(8,128)S(1)} %copy-done.2, f32[5,8,128]{2,1,0:T(8,128)S(1)} %copy-done.1, f32[86,8,128]{2,1,0:T(8,128)S(1)} %get-tuple-element.13.refs_3_, ...), custom_call_target="tpu_custom_call" | custom-call | tf_op jit(solution)/shard_map/pallas_call | solution.py:416
  30.9 7.2 %collective-permute-start.4 = (f32[31,8,128]{2,1,0:T(8,128)S(1)}, f32[31,8,128]{2,1,0:T(8,128)S(1)}, u32[]{:S(2)}, u32[]{:S(2)}) collective-permute-start(f32[31,8,128]{2,1,0:T(8,128)S(1)} %get-tuple-element.18), channel_id=1, source_target_pairs={{0,128},{128,256},{256,384},{384,0},{1,129},{129,257},{257,385},{3... | collective-permute-start | bytes 380936 | tf_op jit(solution)/shard_map/ppermute | solution.py:453
  38.1 1.9 %collective-permute-start.5 = (f32[31,8,128]{2,1,0:T(8,128)S(1)}, f32[31,8,128]{2,1,0:T(8,128)S(1)}, u32[]{:S(2)}, u32[]{:S(2)}) collective-permute-start(f32[31,8,128]{2,1,0:T(8,128)S(1)} %get-tuple-element.19), channel_id=1, source_target_pairs={{128,0},{256,128},{384,256},{129,1},{257,129},{385,257},{130,2},{2... | collective-permute-start | bytes 380936 | tf_op jit(solution)/shard_map/ppermute | solution.py:454
  40.0 1.3 %collective-permute-start.6 = (f32[4,8,128]{2,1,0:T(8,128)S(1)}, f32[4,8,128]{2,1,0:T(8,128)S(1)}, u32[]{:S(2)}, u32[]{:S(2)}) collective-permute-start(f32[4,8,128]{2,1,0:T(8,128)S(1)} %get-tuple-element.17.refs_5_), channel_id=1, source_target_pairs={{384,128},{385,129},{386,130},{387,131},{388,132},{389,133},{390,1... | collective-permute-start | bytes 49160 | tf_op jit(solution)/shard_map/ppermute | solution.py:455
  41.3 4.7 %collective-permute-done.6.refs_8_ = f32[4,8,128]{2,1,0:T(8,128)S(1)} collective-permute-done((f32[4,8,128]{2,1,0:T(8,128)S(1)}, f32[4,8,128]{2,1,0:T(8,128)S(1)}, u32[]{:S(2)}, u32[]{:S(2)}) %collective-permute-start.6) | collective-permute-done | bytes 16416 | tf_op jit(solution)/shard_map/ppermute | solution.py:455
  46.0 0.0 collective-permute-done.4.refs_6_
  46.0 0.0 collective-permute-done.5.refs_7_
  46.0 7.9 %shard_map.53 = (f32[5,16,8,128]{3,2,1,0:T(8,128)}, f32[8,128]{1,0:T(8,128)}) custom-call(f32[5,16,8,128]{3,2,1,0:T(8,128)S(1)} %copy-done, f32[8,128]{1,0:T(8,128)S(1)} %copy-done.2, f32[5,8,128]{2,1,0:T(8,128)S(1)} %copy-done.1, f32[86,8,128]{2,1,0:T(8,128)S(1)} %get-tuple-element.13.refs_3_, f32[22,8,128]{2,1,0:T(8,128)S(1)} %get-tuple-element.16.refs_4_, ...), custom_call_target="tpu_custom_call" | custom-call | tf_op jit(solution)/shard_map/pallas_call | solution.py:416
  (1 shorter events, 0.0 us)
Async XLA Ops:
  0.6 1.0 %copy-start = (f32[5,16,8,128]{3,2,1,0:T(8,128)S(1)}, f32[5,16,8,128]{3,2,1,0:T(8,128)}, u32[]{:S(2)}) copy-start(f32[5,16,8,128]{3,2,1,0:T(8,128)} %refs_0_.3) | copy-start | bytes 983044
  1.6 0.7 %copy-start.1 = (f32[5,8,128]{2,1,0:T(8,128)S(1)}, f32[5,8,128]{2,1,0:T(8,128)}, u32[]{:S(2)}) copy-start(f32[5,8,128]{2,1,0:T(8,128)} %refs_2_.3) | copy-start | bytes 61444
  2.3 0.7 %copy-start.2 = (f32[8,128]{1,0:T(8,128)S(1)}, f32[8,128]{1,0:T(8,128)}, u32[]{:S(2)}) copy-start(f32[8,128]{1,0:T(8,128)} %refs_1_.3) | copy-start | bytes 12292
  3.0 15.8 %collective-permute-start = (f32[43,8,128]{2,1,0:T(8,128)S(1)}, f32[43,8,128]{2,1,0:T(8,128)S(1)}, u32[]{:S(2)}, u32[]{:S(2)}) collective-permute-start(f32[43,8,128]{2,1,0:T(8,128)S(1)} %get-tuple-element.11), channel_id=1, source_target_pairs={{0,1},{1,2},{2,3},{3,4},{4,5},{5,6},{6,7},{7,8},{8,9},{9,10},{10,1... | collective-permute-start | bytes 528392 | tf_op jit(solution)/shard_map/ppermute | solution.py:441
  6.2 13.5 %collective-permute-start.1 = (f32[43,8,128]{2,1,0:T(8,128)S(1)}, f32[43,8,128]{2,1,0:T(8,128)S(1)}, u32[]{:S(2)}, u32[]{:S(2)}) collective-permute-start(f32[43,8,128]{2,1,0:T(8,128)S(1)} %get-tuple-element.12), channel_id=1, source_target_pairs={{1,0},{2,1},{3,2},{4,3},{5,4},{6,5},{7,6},{8,7},{9,8},{10,9},{11,1... | collective-permute-start | bytes 528392 | tf_op jit(solution)/shard_map/ppermute | solution.py:442
  20.0 6.3 %collective-permute-start.2 = (f32[6,8,128]{2,1,0:T(8,128)S(1)}, f32[6,8,128]{2,1,0:T(8,128)S(1)}, u32[]{:S(2)}, u32[]{:S(2)}) collective-permute-start(f32[6,8,128]{2,1,0:T(8,128)S(1)} %get-tuple-element.14.refs_4_), channel_id=1, source_target_pairs={{0,16},{16,32},{32,48},{48,64},{64,80},{80,96},{96,112},{1,17},{17... | collective-permute-start | bytes 73736 | tf_op jit(solution)/shard_map/ppermute | solution.py:446
  24.5 5.8 %collective-permute-start.3 = (f32[6,8,128]{2,1,0:T(8,128)S(1)}, f32[6,8,128]{2,1,0:T(8,128)S(1)}, u32[]{:S(2)}, u32[]{:S(2)}) collective-permute-start(f32[6,8,128]{2,1,0:T(8,128)S(1)} %get-tuple-element.15.refs_5_), channel_id=1, source_target_pairs={{16,0},{32,16},{48,32},{64,48},{80,64},{96,80},{112,96},{17,1},{33... | collective-permute-start | bytes 73736 | tf_op jit(solution)/shard_map/ppermute | solution.py:447
  30.9 15.2 %collective-permute-start.4 = (f32[31,8,128]{2,1,0:T(8,128)S(1)}, f32[31,8,128]{2,1,0:T(8,128)S(1)}, u32[]{:S(2)}, u32[]{:S(2)}) collective-permute-start(f32[31,8,128]{2,1,0:T(8,128)S(1)} %get-tuple-element.18), channel_id=1, source_target_pairs={{0,128},{128,256},{256,384},{384,0},{1,129},{129,257},{257,385},{3... | collective-permute-start | bytes 380936 | tf_op jit(solution)/shard_map/ppermute | solution.py:453
  38.1 7.9 %collective-permute-start.5 = (f32[31,8,128]{2,1,0:T(8,128)S(1)}, f32[31,8,128]{2,1,0:T(8,128)S(1)}, u32[]{:S(2)}, u32[]{:S(2)}) collective-permute-start(f32[31,8,128]{2,1,0:T(8,128)S(1)} %get-tuple-element.19), channel_id=1, source_target_pairs={{128,0},{256,128},{384,256},{129,1},{257,129},{385,257},{130,2},{2... | collective-permute-start | bytes 380936 | tf_op jit(solution)/shard_map/ppermute | solution.py:454
  40.0 6.0 %collective-permute-start.6 = (f32[4,8,128]{2,1,0:T(8,128)S(1)}, f32[4,8,128]{2,1,0:T(8,128)S(1)}, u32[]{:S(2)}, u32[]{:S(2)}) collective-permute-start(f32[4,8,128]{2,1,0:T(8,128)S(1)} %get-tuple-element.17.refs_5_), channel_id=1, source_target_pairs={{384,128},{385,129},{386,130},{387,131},{388,132},{389,133},{390,1... | collective-permute-start | bytes 49160 | tf_op jit(solution)/shard_map/ppermute | solution.py:455

commit v2 on v1

v2 whole, which is shorter than its diff:
```python
import functools

import jax
import jax.numpy as jnp
from jax import lax
from jax.experimental import pallas as pl
from jax.experimental.pallas import tpu as pltpu
from jax.sharding import PartitionSpec as P

GAMMA = 1.4
CFL_STEP = 0.08
LAYERS = 64
NL = 16
NP = 86
HALF = 43
UNITS = 11
SCALE = LAYERS / 12.0
STEP = CFL_STEP / LAYERS
C = CFL_STEP / 12.0
VM = pl.BlockSpec(memory_space=pltpu.VMEM)
F32 = jnp.float32
MIRROR = (1.0, -1.0, -1.0, -1.0, 1.0)


def lane():
    return lax.broadcasted_iota(jnp.int32, (8, 128), 1)


def row():
    return lax.broadcasted_iota(jnp.int32, (8, 128), 0)


def rl(x, shift):
    return pltpu.roll(x, shift % 128, 1) if shift % 128 else x


def rs(x, shift):
    return pltpu.roll(x, shift % 8, 0) if shift % 8 else x


def d_lane(x):
    return (rl(x, 2) - rl(x, -2)) + 8.0 * (rl(x, -1) - rl(x, 1))


def strip_patch(d):
    off = lane() & 15
    return jnp.where((off == 12) | (off == 13), rl(d, 8), d)


def strip_ends(x):
    off = lane() & 15
    return jnp.where((off == 10) | (off == 11), rl(x, 8), x)


def d_ends(x, e):
    ln = lane()
    p1 = rl(jnp.where(ln < 1, e, x), -1)
    p2 = rl(jnp.where(ln < 2, e, x), -2)
    m1 = rl(jnp.where(ln >= 127, e, x), 1)
    m2 = rl(jnp.where(ln >= 126, e, x), 2)
    return (m2 - p2) + 8.0 * (p1 - m1)


def patched(d, patch):
    ln = lane()
    return jnp.where((ln < 2) | (ln >= 126), patch, d)


def ring(x, z, shift):
    keep = row() >= shift if shift > 0 else row() < 8 + shift
    a, b = rs(x, shift), rs(z, shift)
    return jnp.where(keep, a, b), jnp.where(keep, b, a)


def d_ring(x, z):
    m2, m1, p1, p2 = ring(x, z, 2), ring(x, z, 1), ring(x, z, -1), ring(x, z, -2)
    return tuple((m2[i] - p2[i]) + 8.0 * (p1[i] - m1[i]) for i in (0, 1))


def spread(x, group):
    ln = lane()
    x = rl(x, -16 * group)
    x = jnp.where(ln < 16, x, rl(x, 16))
    x = jnp.where(ln < 32, x, rl(x, 32))
    return jnp.where(ln < 64, x, rl(x, 64))


def pressure(q):
    kinetic = (q[1] * q[1] + q[2] * q[2] + q[3] * q[3]) / q[0]
    return (GAMMA - 1.0) * (q[4] - 0.5 * kinetic)


def speed(q, b):
    behind = pressure(b)
    return (pressure(q) - behind) / jnp.sqrt(GAMMA * behind * b[0])


def fluxes(q, want=(1, 2, 3)):
    inv = 1.0 / q[0]
    v = [None, q[1] * inv, q[2] * inv, q[3] * inv]
    q11, q22, q33 = q[1] * v[1], q[2] * v[2], q[3] * v[3]
    p = (GAMMA - 1.0) * (q[4] - 0.5 * (q11 + q22 + q33))
    e = q[4] + p
    out = []
    if 1 in want:
        out.append([q[1], q11 + p, q[2] * v[1], q[3] * v[1], e * v[1]])
    if 2 in want:
        out.append([q[2], q[1] * v[2], q22 + p, q[3] * v[2], e * v[2]])
    if 3 in want:
        out.append([q[3], q[1] * v[3], q[2] * v[3], q33 + p, e * v[3]])
    return out


def moving(f1, f3, q, hx, hz, w):
    return [hx * f1[f] + hz * f3[f] + w * q[f] for f in range(5)]


def slopes(h, hz, hs, hsz):
    ds, dsz = d_lane(hs), d_lane(hsz)
    x = SCALE * patched(d_lane(h), rl(strip_patch(ds), -12))
    xz = SCALE * patched(d_lane(hz), rl(strip_patch(dsz), -12))
    a, az = d_ring(h, hz)
    s, _ = d_ring(hs, hsz)
    return (x, SCALE * a), (xz, SCALE * az), (SCALE * ds, SCALE * s)


def plane_of(q, h, b):
    def get(i):
        if i < 80:
            return q[i // NL, i % NL]
        return h[...] if i == 80 else b[i - 81]

    return get


def unit_planes(u):
    return [8 * u + j for j in range(8)] if u < 10 else [80 + j for j in range(6)]


def columns(get, right, left):
    ln = lane()
    for v in range(3):
        r_acc = jnp.zeros((8, 128), F32)
        l_acc = jnp.zeros((8, 128), F32)
        for u in range(4 * v, min(4 * v + 4, UNITS)):
            for j, i in enumerate(unit_planes(u)):
                at = 16 * j + 4 * (u - 4 * v)
                x = rl(get(i), at + 4)
                r_acc = jnp.where((ln >= at) & (ln < at + 4), x, r_acc)
                at = (at + 4) % 128
                l_acc = jnp.where((ln >= at) & (ln < at + 4), x, l_acc)
        right[v] = r_acc
        left[v] = rl(l_acc, -4)


def to_pairs(even, right, left, one, two):
    for v in range(3):
        one[v] = jnp.where(even, right[v], left[v])
        two[v] = jnp.where(even, left[v], right[v])


def build_strips(tile, tiles, right, left, one, two, put):
    m = lane() & 3
    quad = (lane() >> 2) & 3
    even = tile % 2 == 0
    for v in range(3):
        lm, rm = left[v], right[v]
        end_l = jnp.where(m == 0, lm, jnp.where(m == 1, rl(lm, 1), jnp.where(m == 2, rl(lm, 2), rl(lm, 3))))
        end_r = jnp.where(m == 3, rm, jnp.where(m == 2, rl(rm, -1), jnp.where(m == 1, rl(rm, -2), rl(rm, -3))))
        lh = jnp.where(tile == 0, end_l, jnp.where(even, two[v], one[v]))
        rh = jnp.where(tile == tiles - 1, end_r, jnp.where(even, one[v], two[v]))
        for t in range(min(4, UNITS - 4 * v)):
            a, b, c, d = (rl(x, 4 * (i - t)) for i, x in enumerate((lh, lm, rm, rh)))
            put(4 * v + t, jnp.where(quad < 2, jnp.where(quad == 0, a, b), jnp.where(quad == 2, c, d)))


def pack_rows(odd, q_hbm, h_hbm, b_hbm, q, h, b, one, two, sems):
    copies = [
        pltpu.make_async_copy(x, y, sems.at[i]) for i, (x, y) in enumerate(((q_hbm, q), (h_hbm, h), (b_hbm, b)))
    ]
    for c in copies:
        c.start()
    for c in copies:
        c.wait()
    get = plane_of(q, h, b)
    mask = (row() >= 4) ^ odd
    for i in range(HALF):
        x, y = get(i), rs(get(i + HALF), 4)
        one[i] = jnp.where(mask, x, y)
        two[i] = jnp.where(mask, y, x)


def pack_columns(even, q, h, b, right, left, one, two):
    columns(plane_of(q, h, b), right, left)
    to_pairs(even, right, left, one, two)


def pack_second(odd, wn, tile, tiles, q, h, b, a1, a2, right, left, s1, s2, *outs):
    z, strips, w, near, far, z_right, z_left, z_one, z_two, hi, lo = outs
    ln, rw = lane(), row()
    mask = (rw >= 4) ^ odd
    for i in range(HALF):
        x, y = a2[i], a1[i]
        z[i] = jnp.where(mask, x, y)
        z[i + HALF] = rs(jnp.where(mask, y, x), 4)

    def put(u, x):
        strips[u] = x

    build_strips(tile, tiles, right, left, s1, s2, put)
    surf = strips[10]
    own, bq = [q[f, 15] for f in range(5)], [b[f] for f in range(5)]
    zq, bz = [z[f * NL + 15] for f in range(5)], [z[81 + f] for f in range(5)]
    sq = [strips[2 * f + 1] for f in range(5)]
    w0 = speed(own, bq)
    w0z = speed(zq, bz)
    w0s = spread(speed(sq, [rl(surf, 16 * (6 - f)) for f in range(5)]), 7)
    hx = SCALE * patched(d_lane(h[...]), rl(strip_patch(d_lane(surf)), -12))
    hz = SCALE * d_ring(h[...], z[80])[0]
    (f1s,) = fluxes(sq, (1,))
    (f3z,) = fluxes(zq, (3,))
    levels = []
    for x in ([q[f, 13] for f in range(5)], [q[f, 14] for f in range(5)], own, bq):
        f1, f2, f3 = fluxes(x)
        levels.append((f1, f2, f3, moving(f1, f3, x, hx, hz, w0)))
    eta = (LAYERS - 0.5) / LAYERS
    ih = 1.0 / h[...]
    top = []
    for f in range(5):
        dx = patched(d_lane(levels[2][0][f]), rl(strip_patch(d_lane(f1s[f])), -124))
        da, _ = d_ring(levels[2][2][f], f3z[f])
        dn, dg = ((levels[0][k][f] - 8.0 * levels[1][k][f]) + 7.0 * levels[3][k][f] for k in (1, 3))
        top.append(own[f] + C * (ih * (eta * dg - dn) - (dx + da)))
    speeds = (w0, w0z, w0s, speed(top, bq))
    for k in range(4):
        w[k] = speeds[k]
        near[27 + k] = speeds[k]
        far[27 + k] = speeds[k]
    near_rows = (rw < 2) | (rw >= 6)
    hi_s = hi[26] = strips[9]
    lo_s = lo[26] = strips[8]
    for f in range(5):
        for k in range(4):
            hi[4 * f + k] = q[f, 12 + k]
            lo[4 * f + k] = q[f, k]
        hi[20 + f] = jnp.where(near_rows, z[f * NL + 14], rs(z[f * NL + 15], 4))
        lo[20 + f] = jnp.where(near_rows, z[f * NL], rs(z[f * NL + 1], 4))
        if f < 4:
            inside = (ln >= 32 * f) & (ln < 32 * f + 32)
            hi_s = jnp.where(inside, rl(strips[2 * f + 1], 32 * f + 32), hi_s)
            lo_s = jnp.where(inside, rl(strips[2 * f], 32 * f), lo_s)
    hi[25] = hi_s
    lo[25] = lo_s
    for i in range(27):
        near[i] = jnp.where(wn % 2 == 0, hi[i], lo[i])
        far[i] = jnp.where(wn == 1, hi[i], lo[i])
    columns(lambda i: z[i], z_right, z_left)
    to_pairs(tile % 2 == 0, z_right, z_left, z_one, z_two)


def advance(wn, tile, tiles, q, h, b, z, strips, w, near, far, cross, z_right, z_left, z_one, z_two, *rest):
    out, h_out, qx, qz, f1x, f2x, gx, f1z, f2z, gz, f3, sx, sz, pt, ptz, zst = rest
    first, last = tile == 0, tile == tiles - 1

    def put_strip(u, x):
        zst[u] = x

    build_strips(tile, tiles, z_right, z_left, z_one, z_two, put_strip)
    odd = wn % 2 == 1

    def below(i):
        return jnp.where(odd, near[i], far[i])

    def above(i):
        return jnp.where(odd, far[i], near[i])

    ln, rw = lane(), row()
    group, off = ln >> 4, ln & 15
    bottom, top = wn == 0, wn == 3
    near_rows = (rw < 2) | (rw >= 6)

    speeds = []
    for k in range(4):
        a = jnp.where(bottom, far[27 + k], cross[k])
        c = jnp.where(top, w[k], near[27 + k])
        speeds.append(jnp.where(wn < 2, a, c))
    w0, w0z, w0s, w1 = speeds

    surf, surf_z = strips[10], zst[10]
    strip_q = []
    for f in range(5):
        sign = MIRROR[f]
        bq, bz = b[f], z[81 + f]
        for k in range(NL):
            qx[f, 4 + k] = q[f, k]
            qz[f, 2 + k] = z[f * NL + k]
        for k in range(4):
            qx[f, k] = jnp.where(bottom, sign * q[f, 3 - k], below(4 * f + k))
            qx[f, 20 + k] = jnp.where(top, bq, above(4 * f + k))
        zb, za = below(20 + f), above(20 + f)
        qz[f, 0] = jnp.where(bottom, sign * z[f * NL + 1], zb)
        qz[f, 1] = jnp.where(bottom, sign * z[f * NL], rs(zb, 4))
        qz[f, 18] = jnp.where(top, bz, za)
        qz[f, 19] = jnp.where(top, bz, rs(za, 4))
        s_lo, s_hi = strips[2 * f], strips[2 * f + 1]
        if f < 4:
            sb, sa = rl(below(25), 96 - 32 * f), rl(above(25), -32 * f)
        else:
            sb, sa = below(26), above(26)
        sb = jnp.where(bottom, sign * jnp.where(group == 7, rl(s_lo, -16), rl(s_lo, 80)), sb)
        sa = jnp.where(top, spread(surf, 1 + f), sa)
        strip_q.append((s_lo, s_hi, jnp.where(ln < 64, sa, sb)))

    h0, h0z = h[...], z[80]
    h0s, h0sz = spread(surf, 0), spread(surf_z, 0)
    (hx, hz), (hxz, hzz), (hxs, hzs) = slopes(h0, h0z, h0s, h0sz)
    ih, ihz, ihs = 1.0 / h0, 1.0 / h0z, 1.0 / h0s
    base = wn * NL

    parts = []
    for v in range(3):
        x = [strip_q[f][v] for f in range(5)]
        a1, a2, a3 = fluxes(x)
        d1 = [d_lane(a1[f]) for f in range(5)]
        for f in range(5):
            pt[f, v] = strip_patch(d1[f])
        parts.append((d1, a2, a3, moving(a1, a3, x, hxs, hzs, w0s)))
    halo3 = []
    for v in range(2):
        x = [zst[2 * f + v] for f in range(5)]
        z1, z3 = fluxes(x, (1, 3))
        for f in range(5):
            ptz[f, v] = strip_patch(d_lane(z1[f]))
        halo3.append(z3)

    def layer_shift(x, v, k):
        a = rl(x[v], -16 * k)
        c = rl(x[(v + (1 if k > 0 else -1)) % 3], -16 * k)
        return jnp.where(ln < 128 - 16 * k if k > 0 else ln >= -16 * k, a, c)

    strip_s = []
    for v in range(2):
        eta = ((base + 8 * v + group).astype(F32) + 0.5) / LAYERS
        done = []
        for f in range(5):
            dn, dg = (
                (layer_shift(x, v, -2) - layer_shift(x, v, 2)) + 8.0 * (layer_shift(x, v, 1) - layer_shift(x, v, -1))
                for x in ([parts[i][k][f] for i in range(3)] for k in (1, 3))
            )
            da, _ = d_ring(parts[v][2][f], halo3[v][f])
            s = strip_q[f][v] + C * (ihs * (eta * dg - dn) - (parts[v][0][f] + da))
            s = jnp.where(first & ((off == 2) | (off == 3)), jnp.where(off == 3, rl(s, -1), rl(s, -2)), s)
            s = jnp.where(last & ((off == 12) | (off == 13)), jnp.where(off == 12, rl(s, 1), rl(s, 2)), s)
            done.append(s)
        strip_s.append(done)

    def d_rows(ref, f, l, at):
        m2, m1, p1, p2 = (ref[f, l, pl.ds(at + k, 8)] for k in (-2, -1, 1, 2))
        return (m2 - p2) + 8.0 * (p1 - m1)

    def d_around(f, l):
        return d_rows(f3, f, l, 16)

    def d_around_halo(f, l):
        return jnp.where(rw < 4, d_rows(f3, f, l, 24), d_rows(f3, f, l, 8))

    def put_halo(f, l, x):
        f3[f, l, 24:32] = x
        f3[f, l, 8:16] = x

    def own_flux(l, _):
        x = [qx[f, l] for f in range(5)]
        a1, a2, a3 = fluxes(x)
        g = moving(a1, a3, x, hx, hz, w0)
        for f in range(5):
            f1x[f, l], f2x[f, l], gx[f, l] = a1[f], a2[f], g[f]
            f3[f, l, 16:24] = a3[f]
        return 0

    def halo_flux(l, _):
        x = [qz[f, l] for f in range(5)]
        a1, a2, a3 = fluxes(x)
        g = moving(a1, a3, x, hxz, hzz, w0z)
        for f in range(5):
            f1z[f, l], f2z[f, l], gz[f, l] = a1[f], a2[f], g[f]
            put_halo(f, l + 2, a3[f])
        return 0

    lax.fori_loop(0, 24, own_flux, 0, unroll=8)
    lax.fori_loop(0, 20, halo_flux, 0, unroll=10)

    def d_normal(ref, f, l):
        return (ref[f, l - 2] - ref[f, l + 2]) + 8.0 * (ref[f, l + 1] - ref[f, l - 1])

    def eta_of(l):
        return ((base + l).astype(F32) + 0.5) / LAYERS

    def patch_shift(l):
        return 116 - 16 * (l & 7)

    def own_edge(l):
        eta = eta_of(l)
        for f in range(5):
            dx = patched(d_lane(f1x[f, l + 4]), pltpu.roll(pt[f, 2], patch_shift(l), 1))
            da = d_around(f, l + 4)
            dn, dg = d_normal(f2x, f, l + 4), d_normal(gx, f, l + 4)
            sx[f, l + 2] = qx[f, l + 4] + C * (ih * (eta * dg - dn) - (dx + da))

    def section(l, _):
        eta = eta_of(l)
        half = l >> 3
        shift = patch_shift(l)
        for f in range(5):
            dx = patched(d_lane(f1x[f, l + 4]), pltpu.roll(pt[f, half], shift, 1))
            dxz = patched(d_lane(f1z[f, l + 2]), pltpu.roll(ptz[f, half], shift, 1))
            da, daz = d_around(f, l + 4), d_around_halo(f, l + 4)
            dn, dg = d_normal(f2x, f, l + 4), d_normal(gx, f, l + 4)
            sx[f, l + 2] = qx[f, l + 4] + C * (ih * (eta * dg - dn) - (dx + da))
            dn, dg = d_normal(f2z, f, l + 2), d_normal(gz, f, l + 2)
            sz[f, l] = qz[f, l + 2] + C * (ihz * (eta * dg - dn) - (dxz + daz))
        return 0

    lax.fori_loop(0, NL, section, 0, unroll=8)
    for l in (-2, -1, 16, 17):
        own_edge(l)
    for f in range(5):
        for k in range(2):
            sx[f, k] = jnp.where(bottom, MIRROR[f] * sx[f, 3 - k], sx[f, k])
            sx[f, 18 + k] = jnp.where(top, b[f], sx[f, 18 + k])

    h1, h1z, h1s = h0 + STEP * w0, h0z + STEP * w0z, h0s + STEP * w0s
    hx1 = SCALE * d_ends(h1, rl(strip_ends(h1s), -12))
    hz1 = SCALE * d_ring(h1, h1z)[0]
    ih1 = 1.0 / h1
    h_out[...] = 0.5 * (h0 + h1 + STEP * w1)
    for v in range(2):
        (a1,) = fluxes(strip_s[v], (1,))
        for f in range(5):
            pt[f, v] = strip_ends(a1[f])

    def own_flux_two(l, _):
        x = [sx[f, l] for f in range(5)]
        a1, a2, a3 = fluxes(x)
        g = moving(a1, a3, x, hx1, hz1, w1)
        for f in range(5):
            f1x[f, l], f2x[f, l], gx[f, l] = a1[f], a2[f], g[f]
            f3[f, l, 16:24] = a3[f]
        return 0

    def halo_flux_two(l, _):
        (a3,) = fluxes([sz[f, l] for f in range(5)], (3,))
        for f in range(5):
            put_halo(f, l + 2, a3[f])
        return 0

    lax.fori_loop(0, 20, own_flux_two, 0, unroll=10)
    lax.fori_loop(0, NL, halo_flux_two, 0, unroll=8)

    def final(l, _):
        eta = eta_of(l)
        half = l >> 3
        shift = patch_shift(l)
        for f in range(5):
            dx = d_ends(f1x[f, l + 2], pltpu.roll(pt[f, half], shift, 1))
            da = d_around(f, l + 2)
            dn, dg = d_normal(f2x, f, l + 2), d_normal(gx, f, l + 2)
            rate = ih1 * (eta * dg - dn) - (dx + da)
            out[f, l] = 0.5 * (qx[f, l + 4] + sx[f, l + 2] + C * rate)
        return 0

    lax.fori_loop(0, NL, final, 0, unroll=8)


def call(body, ins, outs, scratch=(), sems=0, space=VM):
    shapes = tuple(jax.ShapeDtypeStruct(s, F32) for s in outs)
    return pl.pallas_call(
        body,
        out_shape=shapes,
        in_specs=[space] * len(ins),
        out_specs=tuple([VM] * len(shapes)),
        scratch_shapes=[pltpu.VMEM(s, F32) for s in scratch] + [pltpu.SemaphoreType.DMA((sems,))] * (sems > 0),
        compiler_params=pltpu.CompilerParams(vmem_limit_bytes=40 * 1024 * 1024),
    )(*ins)


def where_am_i():
    return lax.axis_index("sx"), lax.axis_size("sx")


def stage_rows(*refs):
    pack_rows(lax.axis_index("az") % 2 == 1, *refs)


def stage_columns(*refs):
    pack_columns(lax.axis_index("sx") % 2 == 0, *refs)


def stage_second(*refs):
    pack_second(lax.axis_index("az") % 2 == 1, lax.axis_index("wn"), *where_am_i(), *refs)


def stage_advance(*refs):
    advance(lax.axis_index("wn"), *where_am_i(), *refs)


def swaps(size, start, wrap):
    pairs = [(i, (i + 1) % size) for i in range(start, size if wrap else size - 1, 2)]
    return pairs + [(j, i) for i, j in pairs]


def per_device(fields, height, behind):
    around = lax.axis_size("az")
    tiles = lax.axis_size("sx")
    plane = (8, 128)
    *own, one, two = call(
        stage_rows,
        [pltpu.with_memory_space_constraint(x, pltpu.HBM) for x in (fields, height, behind)],
        [fields.shape, height.shape, behind.shape] + [(HALF, *plane)] * 2,
        sems=3,
        space=pl.BlockSpec(memory_space=pltpu.HBM),
    )
    a2 = lax.ppermute(two, "az", swaps(around, 1, True))
    a1 = lax.ppermute(one, "az", swaps(around, 0, True))
    right, left, one, two = call(stage_columns, own, [(3, *plane)] * 4)
    s2 = lax.ppermute(two, "sx", swaps(tiles, 1, False))
    s1 = lax.ppermute(one, "sx", swaps(tiles, 0, False))
    halo, strips, w, near, far, z_right, z_left, one, two = call(
        stage_second,
        (*own, a1, a2, right, left, s1, s2),
        [(NP, *plane), (UNITS, *plane), (4, *plane)] + [(31, *plane)] * 2 + [(3, *plane)] * 4,
        [(27, *plane)] * 2,
    )
    cross = lax.ppermute(w, "wn", [(3, 1)])
    far = lax.ppermute(far, "wn", [(1, 2), (2, 1), (3, 0)])
    s2 = lax.ppermute(two, "sx", swaps(tiles, 1, False))
    s1 = lax.ppermute(one, "sx", swaps(tiles, 0, False))
    near = lax.ppermute(near, "wn", [(0, 1), (1, 0), (2, 3), (3, 2)])
    return call(
        stage_advance,
        (*own, halo, strips, w, near, far, cross, z_right, z_left, s1, s2),
        [(5, NL, 8, 128), (8, 128)],
        [(5, 24, 8, 128), (5, 20, 8, 128)]
        + [(5, 24, 8, 128)] * 3
        + [(5, 20, 8, 128)] * 3
        + [(5, 24, 40, 128)]
        + [(5, 20, 8, 128), (5, NL, 8, 128), (5, 3, 8, 128), (5, 2, 8, 128), (UNITS, 8, 128)],
    )


def solution(mesh):
    in_specs = (P(None, "wn", "az", "sx"), P("az", "sx"), P(None, "az", "sx"))
    out_specs = (P(None, "wn", "az", "sx"), P("az", "sx"))
    return jax.shard_map(
        per_device, mesh=mesh, in_specs=in_specs, out_specs=out_specs, check_vma=False
    )
```

time: 54.3 us -> 49.3 us (0.908)
  the two profiles are of different devices: /device:TPU:25 before, /device:TPU:37 now
where the time goes in v2:
time: 49.3 us; the launch traced here: 49 us
  starting transfers between devices  33.1 us (67%)
  Pallas kernels  7.72 us (16%)
  waiting for transfers between devices  7.45 us (15%)
  between operations  0.72 us (1%)
    ppermute x1, starting transfers between devices, per_device(): a2 = lax.ppermute(two, 'az', swaps(around, 1, True))  10.9 us
    pallas_call x4, Pallas kernels, call(): pl.pallas_call(body, out_shape=shapes, in_specs=[space] * len(ins), out_s...  7.72 us
    ppermute x2, waiting for transfers between devices, per_device(): s2 = lax.ppermute(two, 'sx', swaps(tiles, 1, False))  6.07 us
    ppermute x1, starting transfers between devices, per_device(): cross = lax.ppermute(w, 'wn', [(3, 1)])  4.65 us
    ppermute x1, starting transfers between devices, per_device(): near = lax.ppermute(near, 'wn', [(0, 1), (1, 0), (2, 3), (3, 2)])  4.58 us
    ppermute x2, starting transfers between devices, per_device(): s1 = lax.ppermute(one, 'sx', swaps(tiles, 0, False))  4.21 us
    ppermute x2, starting transfers between devices, per_device(): s2 = lax.ppermute(two, 'sx', swaps(tiles, 1, False))  3.84 us
    ppermute x1, starting transfers between devices, per_device(): a1 = lax.ppermute(one, 'az', swaps(around, 0, True))  2.83 us
  transfers between devices with their start and end apart: 9, of which 4 were waited for; matrix products, arithmetic and copies ran while one was open for 0% of the time, Pallas kernels for 0%

profile of v2, /device:TPU:37, one launch (start us, length us, event | category | flops | bytes accessed | tf_op | source)
XLA Modules:
  0.0 49.0 jit_solution(14145711822434688528)
XLA Ops:
  0.6 1.0 %shard_map.50 = (f32[5,16,8,128]{3,2,1,0:T(8,128)S(1)}, f32[8,128]{1,0:T(8,128)S(1)}, f32[5,8,128]{2,1,0:T(8,128)S(1)}, f32[43,8,128]{2,1,0:T(8,128)S(1)}, f32[43,8,128]{2,1,0:T(8,128)S(1)}) custom-call(f32[5,16,8,128]{3,2,1,0:T(8,128)} %refs_0_.1, f32[8,128]{1,0:T(8,128)} %refs_1_.1, f32[5,8,128]{2,1,0:T(8,128)} %refs_2_.1), custom_call_target="tpu_custom_call" | custom-call | tf_op jit(solution)/shard_map/pallas_call | solution.py:476
  1.7 2.8 %collective-permute-start = (f32[43,8,128]{2,1,0:T(8,128)S(1)}, f32[43,8,128]{2,1,0:T(8,128)S(1)}, u32[]{:S(2)}, u32[]{:S(2)}) collective-permute-start(f32[43,8,128]{2,1,0:T(8,128)S(1)} %get-tuple-element.23), channel_id=1, source_target_pairs={{0,1},{2,3},{4,5},{6,7},{8,9},{10,11},{12,13},{14,15},{1,0},{3,2},... | collective-permute-start | bytes 528392 | tf_op jit(solution)/shard_map/ppermute | solution.py:523
  4.5 10.9 %collective-permute-start.1 = (f32[43,8,128]{2,1,0:T(8,128)S(1)}, f32[43,8,128]{2,1,0:T(8,128)S(1)}, u32[]{:S(2)}, u32[]{:S(2)}) collective-permute-start(f32[43,8,128]{2,1,0:T(8,128)S(1)} %get-tuple-element.24), channel_id=1, source_target_pairs={{1,2},{3,4},{5,6},{7,8},{9,10},{11,12},{13,14},{15,0},{2,1},{4,3},... | collective-permute-start | bytes 528392 | tf_op jit(solution)/shard_map/ppermute | solution.py:522
  15.4 0.2 shard_map.51
  15.7 2.3 %collective-permute-start.2 = (f32[3,8,128]{2,1,0:T(8,128)S(1)}, f32[3,8,128]{2,1,0:T(8,128)S(1)}, u32[]{:S(2)}, u32[]{:S(2)}) collective-permute-start(f32[3,8,128]{2,1,0:T(8,128)S(1)} %get-tuple-element.27), channel_id=1, source_target_pairs={{0,16},{32,48},{64,80},{96,112},{16,0},{48,32},{80,64},{112,96},{1... | collective-permute-start | bytes 36872 | tf_op jit(solution)/shard_map/ppermute | solution.py:526
  18.0 1.9 %collective-permute-start.3 = (f32[3,8,128]{2,1,0:T(8,128)S(1)}, f32[3,8,128]{2,1,0:T(8,128)S(1)}, u32[]{:S(2)}, u32[]{:S(2)}) collective-permute-start(f32[3,8,128]{2,1,0:T(8,128)S(1)} %get-tuple-element.28), channel_id=1, source_target_pairs={{16,32},{48,64},{80,96},{32,16},{64,48},{96,80},{17,33},{49,65},{8... | collective-permute-start | bytes 36872 | tf_op jit(solution)/shard_map/ppermute | solution.py:525
  19.9 0.5 %collective-permute-done.2.refs_7_ = f32[3,8,128]{2,1,0:T(8,128)S(1)} collective-permute-done((f32[3,8,128]{2,1,0:T(8,128)S(1)}, f32[3,8,128]{2,1,0:T(8,128)S(1)}, u32[]{:S(2)}, u32[]{:S(2)}) %collective-permute-start.2) | collective-permute-done | bytes 12320 | tf_op jit(solution)/shard_map/ppermute | solution.py:526
  20.4 3.2 %collective-permute-done.3.refs_8_ = f32[3,8,128]{2,1,0:T(8,128)S(1)} collective-permute-done((f32[3,8,128]{2,1,0:T(8,128)S(1)}, f32[3,8,128]{2,1,0:T(8,128)S(1)}, u32[]{:S(2)}, u32[]{:S(2)}) %collective-permute-start.3) | collective-permute-done | bytes 12320 | tf_op jit(solution)/shard_map/ppermute | solution.py:525
  23.6 0.0 collective-permute-done.refs_3_
  23.6 0.0 collective-permute-done.1.refs_4_
  23.6 0.5 %shard_map.52 = (f32[86,8,128]{2,1,0:T(8,128)S(1)}, f32[11,8,128]{2,1,0:T(8,128)S(1)}, f32[4,8,128]{2,1,0:T(8,128)S(1)}, f32[31,8,128]{2,1,0:T(8,128)S(1)}, f32[...) custom-call(f32[5,16,8,128]{3,2,1,0:T(8,128)S(1)} %get-tuple-element, ...), custom_call_target="tpu_custom_call" | custom-call | tf_op jit(solution)/shard_map/pallas_call | solution.py:476
  24.2 4.6 %collective-permute-start.4 = (f32[31,8,128]{2,1,0:T(8,128)S(1)}, f32[31,8,128]{2,1,0:T(8,128)S(1)}, u32[]{:S(2)}, u32[]{:S(2)}) collective-permute-start(f32[31,8,128]{2,1,0:T(8,128)S(1)} %get-tuple-element.32), channel_id=1, source_target_pairs={{0,128},{128,0},{256,384},{384,256},{1,129},{129,1},{257,385},{385... | collective-permute-start | bytes 380936 | tf_op jit(solution)/shard_map/ppermute | solution.py:537
  28.8 2.0 %collective-permute-start.5 = (f32[31,8,128]{2,1,0:T(8,128)S(1)}, f32[31,8,128]{2,1,0:T(8,128)S(1)}, u32[]{:S(2)}, u32[]{:S(2)}) collective-permute-start(f32[31,8,128]{2,1,0:T(8,128)S(1)} %get-tuple-element.33), channel_id=1, source_target_pairs={{128,256},{256,128},{384,0},{129,257},{257,129},{385,1},{130,258},... | collective-permute-start | bytes 380936 | tf_op jit(solution)/shard_map/ppermute | solution.py:534
  30.8 4.6 %collective-permute-start.6 = (f32[4,8,128]{2,1,0:T(8,128)S(1)}, f32[4,8,128]{2,1,0:T(8,128)S(1)}, u32[]{:S(2)}, u32[]{:S(2)}) collective-permute-start(f32[4,8,128]{2,1,0:T(8,128)S(1)} %get-tuple-element.31.refs_5_), channel_id=1, source_target_pairs={{384,128},{385,129},{386,130},{387,131},{388,132},{389,133},{390,1... | collective-permute-start | bytes 49160 | tf_op jit(solution)/shard_map/ppermute | solution.py:533
  35.4 1.9 %collective-permute-start.7 = (f32[3,8,128]{2,1,0:T(8,128)S(1)}, f32[3,8,128]{2,1,0:T(8,128)S(1)}, u32[]{:S(2)}, u32[]{:S(2)}) collective-permute-start(f32[3,8,128]{2,1,0:T(8,128)S(1)} %get-tuple-element.36), channel_id=1, source_target_pairs={{0,16},{32,48},{64,80},{96,112},{16,0},{48,32},{80,64},{112,96},{1... | collective-permute-start | bytes 36872 | tf_op jit(solution)/shard_map/ppermute | solution.py:536
  37.4 1.9 %collective-permute-start.8 = (f32[3,8,128]{2,1,0:T(8,128)S(1)}, f32[3,8,128]{2,1,0:T(8,128)S(1)}, u32[]{:S(2)}, u32[]{:S(2)}) collective-permute-start(f32[3,8,128]{2,1,0:T(8,128)S(1)} %get-tuple-element.37), channel_id=1, source_target_pairs={{16,32},{48,64},{80,96},{32,16},{64,48},{96,80},{17,33},{49,65},{8... | collective-permute-start | bytes 36872 | tf_op jit(solution)/shard_map/ppermute | solution.py:535
  39.3 0.9 %collective-permute-done.7.refs_11_ = f32[3,8,128]{2,1,0:T(8,128)S(1)} collective-permute-done((f32[3,8,128]{2,1,0:T(8,128)S(1)}, f32[3,8,128]{2,1,0:T(8,128)S(1)}, u32[]{:S(2)}, u32[]{:S(2)}) %collective-permute-start.7) | collective-permute-done | bytes 12320 | tf_op jit(solution)/shard_map/ppermute | solution.py:536
  40.2 2.8 %collective-permute-done.8.refs_12_ = f32[3,8,128]{2,1,0:T(8,128)S(1)} collective-permute-done((f32[3,8,128]{2,1,0:T(8,128)S(1)}, f32[3,8,128]{2,1,0:T(8,128)S(1)}, u32[]{:S(2)}, u32[]{:S(2)}) %collective-permute-start.8) | collective-permute-done | bytes 12320 | tf_op jit(solution)/shard_map/ppermute | solution.py:535
  43.0 0.0 collective-permute-done.6.refs_8_
  43.0 0.0 collective-permute-done.4.refs_6_
  43.0 0.0 collective-permute-done.5.refs_7_
  43.0 5.9 %shard_map.53 = (f32[5,16,8,128]{3,2,1,0:T(8,128)}, f32[8,128]{1,0:T(8,128)}) custom-call(f32[5,16,8,128]{3,2,1,0:T(8,128)S(1)} %get-tuple-element.20.refs_0_, f32[8,128]{1,0:T(8,128)S(1)} %get-tuple-element.21.refs_1_, f32[5,8,128]{2,1,0:T(8,128)S(1)} %get-tuple-element.22.refs_2_, f32[86,8,128]{2,1,0:T(8,128)S(1)} %get-tuple-element.29.refs_3_, ...), custom_call_target="tpu_custom_call" | custom-call | tf_op jit(solution)/shard_map/pallas_call | solution.py:476
Async XLA Ops:
  1.7 22.0 %collective-permute-start = (f32[43,8,128]{2,1,0:T(8,128)S(1)}, f32[43,8,128]{2,1,0:T(8,128)S(1)}, u32[]{:S(2)}, u32[]{:S(2)}) collective-permute-start(f32[43,8,128]{2,1,0:T(8,128)S(1)} %get-tuple-element.23), channel_id=1, source_target_pairs={{0,1},{2,3},{4,5},{6,7},{8,9},{10,11},{12,13},{14,15},{1,0},{3,2},... | collective-permute-start | bytes 528392 | tf_op jit(solution)/shard_map/ppermute | solution.py:523
  4.5 19.1 %collective-permute-start.1 = (f32[43,8,128]{2,1,0:T(8,128)S(1)}, f32[43,8,128]{2,1,0:T(8,128)S(1)}, u32[]{:S(2)}, u32[]{:S(2)}) collective-permute-start(f32[43,8,128]{2,1,0:T(8,128)S(1)} %get-tuple-element.24), channel_id=1, source_target_pairs={{1,2},{3,4},{5,6},{7,8},{9,10},{11,12},{13,14},{15,0},{2,1},{4,3},... | collective-permute-start | bytes 528392 | tf_op jit(solution)/shard_map/ppermute | solution.py:522
  15.7 4.7 %collective-permute-start.2 = (f32[3,8,128]{2,1,0:T(8,128)S(1)}, f32[3,8,128]{2,1,0:T(8,128)S(1)}, u32[]{:S(2)}, u32[]{:S(2)}) collective-permute-start(f32[3,8,128]{2,1,0:T(8,128)S(1)} %get-tuple-element.27), channel_id=1, source_target_pairs={{0,16},{32,48},{64,80},{96,112},{16,0},{48,32},{80,64},{112,96},{1... | collective-permute-start | bytes 36872 | tf_op jit(solution)/shard_map/ppermute | solution.py:526
  18.0 5.7 %collective-permute-start.3 = (f32[3,8,128]{2,1,0:T(8,128)S(1)}, f32[3,8,128]{2,1,0:T(8,128)S(1)}, u32[]{:S(2)}, u32[]{:S(2)}) collective-permute-start(f32[3,8,128]{2,1,0:T(8,128)S(1)} %get-tuple-element.28), channel_id=1, source_target_pairs={{16,32},{48,64},{80,96},{32,16},{64,48},{96,80},{17,33},{49,65},{8... | collective-permute-start | bytes 36872 | tf_op jit(solution)/shard_map/ppermute | solution.py:525
  24.2 18.9 %collective-permute-start.4 = (f32[31,8,128]{2,1,0:T(8,128)S(1)}, f32[31,8,128]{2,1,0:T(8,128)S(1)}, u32[]{:S(2)}, u32[]{:S(2)}) collective-permute-start(f32[31,8,128]{2,1,0:T(8,128)S(1)} %get-tuple-element.32), channel_id=1, source_target_pairs={{0,128},{128,0},{256,384},{384,256},{1,129},{129,1},{257,385},{385... | collective-permute-start | bytes 380936 | tf_op jit(solution)/shard_map/ppermute | solution.py:537
  28.8 14.3 %collective-permute-start.5 = (f32[31,8,128]{2,1,0:T(8,128)S(1)}, f32[31,8,128]{2,1,0:T(8,128)S(1)}, u32[]{:S(2)}, u32[]{:S(2)}) collective-permute-start(f32[31,8,128]{2,1,0:T(8,128)S(1)} %get-tuple-element.33), channel_id=1, source_target_pairs={{128,256},{256,128},{384,0},{129,257},{257,129},{385,1},{130,258},... | collective-permute-start | bytes 380936 | tf_op jit(solution)/shard_map/ppermute | solution.py:534
  30.8 12.2 %collective-permute-start.6 = (f32[4,8,128]{2,1,0:T(8,128)S(1)}, f32[4,8,128]{2,1,0:T(8,128)S(1)}, u32[]{:S(2)}, u32[]{:S(2)}) collective-permute-start(f32[4,8,128]{2,1,0:T(8,128)S(1)} %get-tuple-element.31.refs_5_), channel_id=1, source_target_pairs={{384,128},{385,129},{386,130},{387,131},{388,132},{389,133},{390,1... | collective-permute-start | bytes 49160 | tf_op jit(solution)/shard_map/ppermute | solution.py:533
  35.4 4.7 %collective-permute-start.7 = (f32[3,8,128]{2,1,0:T(8,128)S(1)}, f32[3,8,128]{2,1,0:T(8,128)S(1)}, u32[]{:S(2)}, u32[]{:S(2)}) collective-permute-start(f32[3,8,128]{2,1,0:T(8,128)S(1)} %get-tuple-element.36), channel_id=1, source_target_pairs={{0,16},{32,48},{64,80},{96,112},{16,0},{48,32},{80,64},{112,96},{1... | collective-permute-start | bytes 36872 | tf_op jit(solution)/shard_map/ppermute | solution.py:536
  37.4 5.7 %collective-permute-start.8 = (f32[3,8,128]{2,1,0:T(8,128)S(1)}, f32[3,8,128]{2,1,0:T(8,128)S(1)}, u32[]{:S(2)}, u32[]{:S(2)}) collective-permute-start(f32[3,8,128]{2,1,0:T(8,128)S(1)} %get-tuple-element.37), channel_id=1, source_target_pairs={{16,32},{48,64},{80,96},{32,16},{64,48},{96,80},{17,33},{49,65},{8... | collective-permute-start | bytes 36872 | tf_op jit(solution)/shard_map/ppermute | solution.py:535

commit v3 on v2

--- a/solution.py
+++ b/solution.py
@@ -95,24 +95,26 @@
     return (pressure(q) - behind) / jnp.sqrt(GAMMA * behind * b[0])
 
 
-def fluxes(q, want=(1, 2, 3)):
+def fluxes(q, want=(1, 2, 3), move=None):
     inv = 1.0 / q[0]
-    v = [None, q[1] * inv, q[2] * inv, q[3] * inv]
-    q11, q22, q33 = q[1] * v[1], q[2] * v[2], q[3] * v[3]
+    v1, v2, v3 = q[1] * inv, q[2] * inv, q[3] * inv
+    q11, q22, q33 = q[1] * v1, q[2] * v2, q[3] * v3
     p = (GAMMA - 1.0) * (q[4] - 0.5 * (q11 + q22 + q33))
     e = q[4] + p
+    q12, q13, q23 = q[1] * v2, q[1] * v3, q[2] * v3
     out = []
     if 1 in want:
-        out.append([q[1], q11 + p, q[2] * v[1], q[3] * v[1], e * v[1]])
+        out.append([q[1], q11 + p, q12, q13, e * v1])
     if 2 in want:
-        out.append([q[2], q[1] * v[2], q22 + p, q[3] * v[2], e * v[2]])
+        out.append([q[2], q12, q22 + p, q23, e * v2])
     if 3 in want:
-        out.append([q[3], q[1] * v[3], q[2] * v[3], q33 + p, e * v[3]])
+        out.append([q[3], q13, q23, q33 + p, e * v3])
+    if move is not None:
+        hx, hz, w = move
+        s = hx * v1 + hz * v3
+        t = s + w
+        out.append([q[0] * t, q[1] * t + p * hx, q[2] * t, q[3] * t + p * hz, q[4] * t + p * s])
     return out
-
-
-def moving(f1, f3, q, hx, hz, w):
-    return [hx * f1[f] + hz * f3[f] + w * q[f] for f in range(5)]
 
 
 def slopes(h, hz, hs, hsz):
@@ -221,8 +223,7 @@
     (f3z,) = fluxes(zq, (3,))
     levels = []
     for x in ([q[f, 13] for f in range(5)], [q[f, 14] for f in range(5)], own, bq):
-        f1, f2, f3 = fluxes(x)
-        levels.append((f1, f2, f3, moving(f1, f3, x, hx, hz, w0)))
+        levels.append(fluxes(x, move=(hx, hz, w0)))
     eta = (LAYERS - 0.5) / LAYERS
     ih = 1.0 / h[...]
     top = []
@@ -234,7 +235,6 @@
     speeds = (w0, w0z, w0s, speed(top, bq))
     for k in range(4):
         w[k] = speeds[k]
-        near[27 + k] = speeds[k]
         far[27 + k] = speeds[k]
     near_rows = (rw < 2) | (rw >= 6)
     hi_s = hi[26] = strips[9]
@@ -258,15 +258,25 @@
     to_pairs(tile % 2 == 0, z_right, z_left, z_one, z_two)
 
 
-def advance(wn, tile, tiles, q, h, b, z, strips, w, near, far, cross, z_right, z_left, z_one, z_two, *rest):
-    out, h_out, qx, qz, f1x, f2x, gx, f1z, f2z, gz, f3, sx, sz, pt, ptz, zst = rest
+def pack_near(wn, near, w, far, _one, _two, out):
+    for i in range(27):
+        out[i] = near[i]
+    for k in range(4):
+        out[27 + k] = jnp.where(wn == 0, far[27 + k], w[k])
+
+
+def advance(wn, tile, tiles, q, h, b, z, strips, w, near, far, z_right, z_left, z_one, z_two, *rest):
+    out, h_out, qh, zh, f1x, f2x, gx, f1z, f2z, gz, f3, sx, sz, zst = rest
+    ln, rw = lane(), row()
+    group, off = ln >> 4, ln & 15
+    bottom, top, odd = wn == 0, wn == 3, wn % 2 == 1
     first, last = tile == 0, tile == tiles - 1
+    base = (wn * NL).astype(F32) + 0.5
 
     def put_strip(u, x):
         zst[u] = x
 
     build_strips(tile, tiles, z_right, z_left, z_one, z_two, put_strip)
-    odd = wn % 2 == 1
 
     def below(i):
         return jnp.where(odd, near[i], far[i])
@@ -274,16 +284,7 @@
     def above(i):
         return jnp.where(odd, far[i], near[i])
 
-    ln, rw = lane(), row()
-    group, off = ln >> 4, ln & 15
-    bottom, top = wn == 0, wn == 3
-    near_rows = (rw < 2) | (rw >= 6)
-
-    speeds = []
-    for k in range(4):
-        a = jnp.where(bottom, far[27 + k], cross[k])
-        c = jnp.where(top, w[k], near[27 + k])
-        speeds.append(jnp.where(wn < 2, a, c))
+    speeds = [jnp.where(top, w[k], jnp.where(bottom, far[27 + k], near[27 + k])) for k in range(4)]
     w0, w0z, w0s, w1 = speeds
 
     surf, surf_z = strips[10], zst[10]
@@ -291,17 +292,14 @@
     for f in range(5):
         sign = MIRROR[f]
         bq, bz = b[f], z[81 + f]
-        for k in range(NL):
-            qx[f, 4 + k] = q[f, k]
-            qz[f, 2 + k] = z[f * NL + k]
         for k in range(4):
-            qx[f, k] = jnp.where(bottom, sign * q[f, 3 - k], below(4 * f + k))
-            qx[f, 20 + k] = jnp.where(top, bq, above(4 * f + k))
+            qh[f, k] = jnp.where(bottom, sign * q[f, 3 - k], below(4 * f + k))
+            qh[f, 4 + k] = jnp.where(top, bq, above(4 * f + k))
         zb, za = below(20 + f), above(20 + f)
-        qz[f, 0] = jnp.where(bottom, sign * z[f * NL + 1], zb)
-        qz[f, 1] = jnp.where(bottom, sign * z[f * NL], rs(zb, 4))
-        qz[f, 18] = jnp.where(top, bz, za)
-        qz[f, 19] = jnp.where(top, bz, rs(za, 4))
+        zh[f, 0] = jnp.where(bottom, sign * z[f * NL + 1], zb)
+        zh[f, 1] = jnp.where(bottom, sign * z[f * NL], rs(zb, 4))
+        zh[f, 2] = jnp.where(top, bz, za)
+        zh[f, 3] = jnp.where(top, bz, rs(za, 4))
         s_lo, s_hi = strips[2 * f], strips[2 * f + 1]
         if f < 4:
             sb, sa = rl(below(25), 96 - 32 * f), rl(above(25), -32 * f)
@@ -311,26 +309,27 @@
         sa = jnp.where(top, spread(surf, 1 + f), sa)
         strip_q.append((s_lo, s_hi, jnp.where(ln < 64, sa, sb)))
 
+    def own_q(f, l):
+        return q[f, l] if 0 <= l < NL else qh[f, l + 4 if l < 0 else l - 12]
+
+    def halo_q(f, l):
+        return z[f * NL + l] if 0 <= l < NL else zh[f, l + 2 if l < 0 else l - 14]
+
     h0, h0z = h[...], z[80]
     h0s, h0sz = spread(surf, 0), spread(surf_z, 0)
     (hx, hz), (hxz, hzz), (hxs, hzs) = slopes(h0, h0z, h0s, h0sz)
     ih, ihz, ihs = 1.0 / h0, 1.0 / h0z, 1.0 / h0s
-    base = wn * NL
-
-    parts = []
+
+    parts, patch = [], []
     for v in range(3):
-        x = [strip_q[f][v] for f in range(5)]
-        a1, a2, a3 = fluxes(x)
+        a1, a2, a3, g = fluxes([strip_q[f][v] for f in range(5)], move=(hxs, hzs, w0s))
         d1 = [d_lane(a1[f]) for f in range(5)]
-        for f in range(5):
-            pt[f, v] = strip_patch(d1[f])
-        parts.append((d1, a2, a3, moving(a1, a3, x, hxs, hzs, w0s)))
-    halo3 = []
+        patch.append([strip_patch(d1[f]) for f in range(5)])
+        parts.append((d1, a2, a3, g))
+    halo3, patch_z = [], []
     for v in range(2):
-        x = [zst[2 * f + v] for f in range(5)]
-        z1, z3 = fluxes(x, (1, 3))
-        for f in range(5):
-            ptz[f, v] = strip_patch(d_lane(z1[f]))
+        z1, z3 = fluxes([zst[2 * f + v] for f in range(5)], (1, 3))
+        patch_z.append([strip_patch(d_lane(z1[f])) for f in range(5)])
         halo3.append(z3)
 
     def layer_shift(x, v, k):
@@ -340,7 +339,7 @@
 
     strip_s = []
     for v in range(2):
-        eta = ((base + 8 * v + group).astype(F32) + 0.5) / LAYERS
+        eta = (base + (8 * v + group).astype(F32)) / LAYERS
         done = []
         for f in range(5):
             dn, dg = (
@@ -354,75 +353,63 @@
             done.append(s)
         strip_s.append(done)
 
-    def d_rows(ref, f, l, at):
-        m2, m1, p1, p2 = (ref[f, l, pl.ds(at + k, 8)] for k in (-2, -1, 1, 2))
+    def d_rows(f, l, at):
+        m2, m1, p1, p2 = (f3[f, l, at + k : at + k + 8] for k in (-2, -1, 1, 2))
         return (m2 - p2) + 8.0 * (p1 - m1)
 
-    def d_around(f, l):
-        return d_rows(f3, f, l, 16)
-
-    def d_around_halo(f, l):
-        return jnp.where(rw < 4, d_rows(f3, f, l, 24), d_rows(f3, f, l, 8))
+    def d_normal(ref, f, l):
+        return (ref[f, l - 2] - ref[f, l + 2]) + 8.0 * (ref[f, l + 1] - ref[f, l - 1])
+
+    def eta_of(l):
+        return (base + l) / LAYERS
+
+    def patch_shift(l):
+        return 116 - 16 * (l & 7)
+
+    def own_flux(l):
+        a1, a2, a3, g = fluxes([own_q(f, l) for f in range(5)], move=(hx, hz, w0))
+        for f in range(5):
+            f2x[f, l + 4], gx[f, l + 4] = a2[f], g[f]
+            if -2 <= l < 18:
+                f1x[f, l + 4] = a1[f]
+                f3[f, l + 4, 16:24] = a3[f]
 
     def put_halo(f, l, x):
         f3[f, l, 24:32] = x
         f3[f, l, 8:16] = x
 
-    def own_flux(l, _):
-        x = [qx[f, l] for f in range(5)]
-        a1, a2, a3 = fluxes(x)
-        g = moving(a1, a3, x, hx, hz, w0)
-        for f in range(5):
-            f1x[f, l], f2x[f, l], gx[f, l] = a1[f], a2[f], g[f]
-            f3[f, l, 16:24] = a3[f]
-        return 0
-
-    def halo_flux(l, _):
-        x = [qz[f, l] for f in range(5)]
-        a1, a2, a3 = fluxes(x)
-        g = moving(a1, a3, x, hxz, hzz, w0z)
-        for f in range(5):
-            f1z[f, l], f2z[f, l], gz[f, l] = a1[f], a2[f], g[f]
-            put_halo(f, l + 2, a3[f])
-        return 0
-
-    lax.fori_loop(0, 24, own_flux, 0, unroll=8)
-    lax.fori_loop(0, 20, halo_flux, 0, unroll=10)
-
-    def d_normal(ref, f, l):
-        return (ref[f, l - 2] - ref[f, l + 2]) + 8.0 * (ref[f, l + 1] - ref[f, l - 1])
-
-    def eta_of(l):
-        return ((base + l).astype(F32) + 0.5) / LAYERS
-
-    def patch_shift(l):
-        return 116 - 16 * (l & 7)
-
-    def own_edge(l):
-        eta = eta_of(l)
-        for f in range(5):
-            dx = patched(d_lane(f1x[f, l + 4]), pltpu.roll(pt[f, 2], patch_shift(l), 1))
-            da = d_around(f, l + 4)
+    def halo_flux(l):
+        a1, a2, a3, g = fluxes([halo_q(f, l) for f in range(5)], move=(hxz, hzz, w0z))
+        for f in range(5):
+            f2z[f, l + 2], gz[f, l + 2] = a2[f], g[f]
+            put_halo(f, l + 4, a3[f])
+            if 0 <= l < NL:
+                f1z[f, l] = a1[f]
+
+    def section(l):
+        eta, shift = eta_of(l), patch_shift(l)
+        own, halo = [], []
+        for f in range(5):
+            dx = patched(d_lane(f1x[f, l + 4]), rl(patch[(l >> 3) % 3][f], shift))
+            da = d_rows(f, l + 4, 16)
             dn, dg = d_normal(f2x, f, l + 4), d_normal(gx, f, l + 4)
-            sx[f, l + 2] = qx[f, l + 4] + C * (ih * (eta * dg - dn) - (dx + da))
-
-    def section(l, _):
-        eta = eta_of(l)
-        half = l >> 3
-        shift = patch_shift(l)
-        for f in range(5):
-            dx = patched(d_lane(f1x[f, l + 4]), pltpu.roll(pt[f, half], shift, 1))
-            dxz = patched(d_lane(f1z[f, l + 2]), pltpu.roll(ptz[f, half], shift, 1))
-            da, daz = d_around(f, l + 4), d_around_halo(f, l + 4)
-            dn, dg = d_normal(f2x, f, l + 4), d_normal(gx, f, l + 4)
-            sx[f, l + 2] = qx[f, l + 4] + C * (ih * (eta * dg - dn) - (dx + da))
-            dn, dg = d_normal(f2z, f, l + 2), d_normal(gz, f, l + 2)
-            sz[f, l] = qz[f, l + 2] + C * (ihz * (eta * dg - dn) - (dxz + daz))
-        return 0
-
-    lax.fori_loop(0, NL, section, 0, unroll=8)
-    for l in (-2, -1, 16, 17):
-        own_edge(l)
+            own.append(own_q(f, l) + C * (ih * (eta * dg - dn) - (dx + da)))
+            if 0 <= l < NL:
+                dx = patched(d_lane(f1z[f, l]), rl(patch_z[l >> 3][f], shift))
+                da = jnp.where(rw < 4, d_rows(f, l + 4, 24), d_rows(f, l + 4, 8))
+                dn, dg = d_normal(f2z, f, l + 2), d_normal(gz, f, l + 2)
+                halo.append(halo_q(f, l) + C * (ihz * (eta * dg - dn) - (dx + da)))
+        for f in range(5):
+            sx[f, l + 2] = own[f]
+            if halo:
+                sz[f, l] = halo[f]
+
+    for l in range(-4, 20):
+        own_flux(l)
+        if -2 <= l < 18:
+            halo_flux(l)
+        if l - 2 >= -2:
+            section(l - 2)
     for f in range(5):
         for k in range(2):
             sx[f, k] = jnp.where(bottom, MIRROR[f] * sx[f, 3 - k], sx[f, k])
@@ -433,42 +420,42 @@
     hz1 = SCALE * d_ring(h1, h1z)[0]
     ih1 = 1.0 / h1
     h_out[...] = 0.5 * (h0 + h1 + STEP * w1)
+    ends = []
     for v in range(2):
         (a1,) = fluxes(strip_s[v], (1,))
-        for f in range(5):
-            pt[f, v] = strip_ends(a1[f])
-
-    def own_flux_two(l, _):
-        x = [sx[f, l] for f in range(5)]
-        a1, a2, a3 = fluxes(x)
-        g = moving(a1, a3, x, hx1, hz1, w1)
-        for f in range(5):
-            f1x[f, l], f2x[f, l], gx[f, l] = a1[f], a2[f], g[f]
-            f3[f, l, 16:24] = a3[f]
-        return 0
-
-    def halo_flux_two(l, _):
+        ends.append([strip_ends(a1[f]) for f in range(5)])
+
+    def own_flux_two(l):
+        a1, a2, a3, g = fluxes([sx[f, l + 2] for f in range(5)], move=(hx1, hz1, w1))
+        for f in range(5):
+            f2x[f, l + 4], gx[f, l + 4] = a2[f], g[f]
+            if 0 <= l < NL:
+                f1x[f, l + 4] = a1[f]
+                f3[f, l + 4, 16:24] = a3[f]
+
+    def halo_flux_two(l):
         (a3,) = fluxes([sz[f, l] for f in range(5)], (3,))
         for f in range(5):
-            put_halo(f, l + 2, a3[f])
-        return 0
-
-    lax.fori_loop(0, 20, own_flux_two, 0, unroll=10)
-    lax.fori_loop(0, NL, halo_flux_two, 0, unroll=8)
-
-    def final(l, _):
-        eta = eta_of(l)
-        half = l >> 3
-        shift = patch_shift(l)
-        for f in range(5):
-            dx = d_ends(f1x[f, l + 2], pltpu.roll(pt[f, half], shift, 1))
-            da = d_around(f, l + 2)
-            dn, dg = d_normal(f2x, f, l + 2), d_normal(gx, f, l + 2)
+            put_halo(f, l + 4, a3[f])
+
+    def final(l):
+        eta, shift = eta_of(l), patch_shift(l)
+        done = []
+        for f in range(5):
+            dx = d_ends(f1x[f, l + 4], rl(ends[l >> 3][f], shift))
+            da = d_rows(f, l + 4, 16)
+            dn, dg = d_normal(f2x, f, l + 4), d_normal(gx, f, l + 4)
             rate = ih1 * (eta * dg - dn) - (dx + da)
-            out[f, l] = 0.5 * (qx[f, l + 4] + sx[f, l + 2] + C * rate)
-        return 0
-
-    lax.fori_loop(0, NL, final, 0, unroll=8)
+            done.append(0.5 * (q[f, l] + sx[f, l + 2] + C * rate))
+        for f in range(5):
+            out[f, l] = done[f]
+
+    for l in range(-2, 18):
+        own_flux_two(l)
+        if 0 <= l < NL:
+            halo_flux_two(l)
+        if l - 2 >= 0:
+            final(l - 2)
 
 
 def call(body, ins, outs, scratch=(), sems=0, space=VM):
@@ -497,6 +484,10 @@
 
 def stage_second(*refs):
     pack_second(lax.axis_index("az") % 2 == 1, lax.axis_index("wn"), *where_am_i(), *refs)
+
+
+def stage_near(*refs):
+    pack_near(lax.axis_index("wn"), *refs)
 
 
 def stage_advance(*refs):
@@ -527,23 +518,24 @@
     halo, strips, w, near, far, z_right, z_left, one, two = call(
         stage_second,
         (*own, a1, a2, right, left, s1, s2),
-        [(NP, *plane), (UNITS, *plane), (4, *plane)] + [(31, *plane)] * 2 + [(3, *plane)] * 4,
+        [(NP, *plane), (UNITS, *plane), (4, *plane), (27, *plane), (31, *plane)] + [(3, *plane)] * 4,
         [(27, *plane)] * 2,
     )
-    cross = lax.ppermute(w, "wn", [(3, 1)])
     far = lax.ppermute(far, "wn", [(1, 2), (2, 1), (3, 0)])
     s2 = lax.ppermute(two, "sx", swaps(tiles, 1, False))
     s1 = lax.ppermute(one, "sx", swaps(tiles, 0, False))
+    (near,) = call(stage_near, (near, w, far, s1, s2), [(31, *plane)])
     near = lax.ppermute(near, "wn", [(0, 1), (1, 0), (2, 3), (3, 2)])
     return call(
         stage_advance,
-        (*own, halo, strips, w, near, far, cross, z_right, z_left, s1, s2),
+        (*own, halo, strips, w, near, far, z_right, z_left, s1, s2),
         [(5, NL, 8, 128), (8, 128)],
-        [(5, 24, 8, 128), (5, 20, 8, 128)]
+        [(5, 8, 8, 128), (5, 4, 8, 128)]
         + [(5, 24, 8, 128)] * 3
-        + [(5, 20, 8, 128)] * 3
+        + [(5, NL, 8, 128)]
+        + [(5, 20, 8, 128)] * 2
         + [(5, 24, 40, 128)]
-        + [(5, 20, 8, 128), (5, NL, 8, 128), (5, 3, 8, 128), (5, 2, 8, 128), (UNITS, 8, 128)],
+        + [(5, 20, 8, 128), (5, NL, 8, 128), (UNITS, 8, 128)],
     )
 
 

time: 49.3 us -> 50.3 us (1.020)
  the two profiles are of different devices: /device:TPU:37 before, /device:TPU:33 now
where the time goes in v3:
time: 50.3 us; the launch traced here: 50 us
  starting transfers between devices  30.9 us (61%)
  Pallas kernels  9.56 us (19%)
  waiting for transfers between devices  8.75 us (17%)
  between operations  0.71 us (1%)
    ppermute x1, starting transfers between devices, per_device(): a2 = lax.ppermute(two, 'az', swaps(around, 1, True))  10.6 us
    pallas_call x5, Pallas kernels, call(): pl.pallas_call(body, out_shape=shapes, in_specs=[space] * len(ins), out_s...  9.56 us
    ppermute x1, starting transfers between devices, per_device(): far = lax.ppermute(far, 'wn', [(1, 2), (2, 1), (3, 0)])  7.2 us
    ppermute x2, waiting for transfers between devices, per_device(): s2 = lax.ppermute(two, 'sx', swaps(tiles, 1, False))  6.07 us
    ppermute x2, starting transfers between devices, per_device(): s1 = lax.ppermute(one, 'sx', swaps(tiles, 0, False))  4.21 us
    ppermute x2, starting transfers between devices, per_device(): s2 = lax.ppermute(two, 'sx', swaps(tiles, 1, False))  3.84 us
    ppermute x1, starting transfers between devices, per_device(): a1 = lax.ppermute(one, 'az', swaps(around, 0, True))  3.12 us
    ppermute x1, starting transfers between devices, per_device(): near = lax.ppermute(near, 'wn', [(0, 1), (1, 0), (2, 3), (3, 2)])  1.92 us
  transfers between devices with their start and end apart: 8, of which 5 were waited for; matrix products, arithmetic and copies ran while one was open for 0% of the time, Pallas kernels for 0%

profile of v3, /device:TPU:33, one launch (start us, length us, event | category | flops | bytes accessed | tf_op | source)
XLA Modules:
  0.0 50.0 jit_solution(108915960950804564)
XLA Ops:
  0.6 1.0 %shard_map.50 = (f32[5,16,8,128]{3,2,1,0:T(8,128)S(1)}, f32[8,128]{1,0:T(8,128)S(1)}, f32[5,8,128]{2,1,0:T(8,128)S(1)}, f32[43,8,128]{2,1,0:T(8,128)S(1)}, f32[43,8,128]{2,1,0:T(8,128)S(1)}) custom-call(f32[5,16,8,128]{3,2,1,0:T(8,128)} %refs_0_.1, f32[8,128]{1,0:T(8,128)} %refs_1_.1, f32[5,8,128]{2,1,0:T(8,128)} %refs_2_.1), custom_call_target="tpu_custom_call" | custom-call | tf_op jit(solution)/shard_map/pallas_call | solution.py:463
  1.7 3.1 %collective-permute-start = (f32[43,8,128]{2,1,0:T(8,128)S(1)}, f32[43,8,128]{2,1,0:T(8,128)S(1)}, u32[]{:S(2)}, u32[]{:S(2)}) collective-permute-start(f32[43,8,128]{2,1,0:T(8,128)S(1)} %get-tuple-element.23), channel_id=1, source_target_pairs={{0,1},{2,3},{4,5},{6,7},{8,9},{10,11},{12,13},{14,15},{1,0},{3,2},... | collective-permute-start | bytes 528392 | tf_op jit(solution)/shard_map/ppermute | solution.py:514
  4.8 10.6 %collective-permute-start.1 = (f32[43,8,128]{2,1,0:T(8,128)S(1)}, f32[43,8,128]{2,1,0:T(8,128)S(1)}, u32[]{:S(2)}, u32[]{:S(2)}) collective-permute-start(f32[43,8,128]{2,1,0:T(8,128)S(1)} %get-tuple-element.24), channel_id=1, source_target_pairs={{1,2},{3,4},{5,6},{7,8},{9,10},{11,12},{13,14},{15,0},{2,1},{4,3},... | collective-permute-start | bytes 528392 | tf_op jit(solution)/shard_map/ppermute | solution.py:513
  15.4 0.2 shard_map.51
  15.7 2.3 %collective-permute-start.2 = (f32[3,8,128]{2,1,0:T(8,128)S(1)}, f32[3,8,128]{2,1,0:T(8,128)S(1)}, u32[]{:S(2)}, u32[]{:S(2)}) collective-permute-start(f32[3,8,128]{2,1,0:T(8,128)S(1)} %get-tuple-element.27), channel_id=1, source_target_pairs={{0,16},{32,48},{64,80},{96,112},{16,0},{48,32},{80,64},{112,96},{1... | collective-permute-start | bytes 36872 | tf_op jit(solution)/shard_map/ppermute | solution.py:517
  18.0 1.9 %collective-permute-start.3 = (f32[3,8,128]{2,1,0:T(8,128)S(1)}, f32[3,8,128]{2,1,0:T(8,128)S(1)}, u32[]{:S(2)}, u32[]{:S(2)}) collective-permute-start(f32[3,8,128]{2,1,0:T(8,128)S(1)} %get-tuple-element.28), channel_id=1, source_target_pairs={{16,32},{48,64},{80,96},{32,16},{64,48},{96,80},{17,33},{49,65},{8... | collective-permute-start | bytes 36872 | tf_op jit(solution)/shard_map/ppermute | solution.py:516
  19.9 0.5 collective-permute-done.2.refs_7_
  20.4 3.2 %collective-permute-done.3.refs_8_ = f32[3,8,128]{2,1,0:T(8,128)S(1)} collective-permute-done((f32[3,8,128]{2,1,0:T(8,128)S(1)}, f32[3,8,128]{2,1,0:T(8,128)S(1)}, u32[]{:S(2)}, u32[]{:S(2)}) %collective-permute-start.3) | collective-permute-done | bytes 12320 | tf_op jit(solution)/shard_map/ppermute | solution.py:516
  23.6 0.0 collective-permute-done.refs_3_
  23.6 0.0 collective-permute-done.1.refs_4_
  23.6 0.5 %shard_map.52 = (f32[86,8,128]{2,1,0:T(8,128)S(1)}, f32[11,8,128]{2,1,0:T(8,128)S(1)}, f32[4,8,128]{2,1,0:T(8,128)S(1)}, f32[27,8,128]{2,1,0:T(8,128)S(1)}, f32[...) custom-call(f32[5,16,8,128]{3,2,1,0:T(8,128)S(1)} %get-tuple-element, ...), custom_call_target="tpu_custom_call" | custom-call | tf_op jit(solution)/shard_map/pallas_call | solution.py:463
  24.2 7.2 %collective-permute-start.4 = (f32[31,8,128]{2,1,0:T(8,128)S(1)}, f32[31,8,128]{2,1,0:T(8,128)S(1)}, u32[]{:S(2)}, u32[]{:S(2)}) collective-permute-start(f32[31,8,128]{2,1,0:T(8,128)S(1)} %get-tuple-element.33), channel_id=1, source_target_pairs={{128,256},{256,128},{384,0},{129,257},{257,129},{385,1},{130,258},... | collective-permute-start | bytes 380936 | tf_op jit(solution)/shard_map/ppermute | solution.py:524
  31.4 1.9 %collective-permute-start.5 = (f32[3,8,128]{2,1,0:T(8,128)S(1)}, f32[3,8,128]{2,1,0:T(8,128)S(1)}, u32[]{:S(2)}, u32[]{:S(2)}) collective-permute-start(f32[3,8,128]{2,1,0:T(8,128)S(1)} %get-tuple-element.34), channel_id=1, source_target_pairs={{0,16},{32,48},{64,80},{96,112},{16,0},{48,32},{80,64},{112,96},{1... | collective-permute-start | bytes 36872 | tf_op jit(solution)/shard_map/ppermute | solution.py:526
  33.3 1.9 %collective-permute-start.6 = (f32[3,8,128]{2,1,0:T(8,128)S(1)}, f32[3,8,128]{2,1,0:T(8,128)S(1)}, u32[]{:S(2)}, u32[]{:S(2)}) collective-permute-start(f32[3,8,128]{2,1,0:T(8,128)S(1)} %get-tuple-element.35), channel_id=1, source_target_pairs={{16,32},{48,64},{80,96},{32,16},{64,48},{96,80},{17,33},{49,65},{8... | collective-permute-start | bytes 36872 | tf_op jit(solution)/shard_map/ppermute | solution.py:525
  35.2 0.9 %collective-permute-done.5.refs_3_.refs_10_ = f32[3,8,128]{2,1,0:T(8,128)S(1)} collective-permute-done((f32[3,8,128]{2,1,0:T(8,128)S(1)}, f32[3,8,128]{2,1,0:T(8,128)S(1)}, u32[]{:S(2)}, u32[]{:S(2)}) %collective-permute-start.5) | collective-permute-done | bytes 12320 | tf_op jit(solution)/shard_map/ppermute | solution.py:526
  36.1 2.8 %collective-permute-done.6.refs_4_.refs_11_ = f32[3,8,128]{2,1,0:T(8,128)S(1)} collective-permute-done((f32[3,8,128]{2,1,0:T(8,128)S(1)}, f32[3,8,128]{2,1,0:T(8,128)S(1)}, u32[]{:S(2)}, u32[]{:S(2)}) %collective-permute-start.6) | collective-permute-done | bytes 12320 | tf_op jit(solution)/shard_map/ppermute | solution.py:525
  39.0 0.0 collective-permute-done.4.refs_2_.refs_7_
  39.0 1.9 %collective-permute-start.7 = (f32[31,8,128]{2,1,0:T(8,128)S(1)}, f32[31,8,128]{2,1,0:T(8,128)S(1)}, u32[]{:S(2)}, u32[]{:S(2)}) collective-permute-start(f32[31,8,128]{2,1,0:T(8,128)S(1)} %shard_map.53), channel_id=1, source_target_pairs={{0,128},{128,0},{256,384},{384,256},{1,129},{129,1},{257,385},{385... | collective-permute-start | bytes 380936 | tf_op jit(solution)/shard_map/ppermute | solution.py:528
  40.9 1.3 %collective-permute-done.7.refs_6_ = f32[31,8,128]{2,1,0:T(8,128)S(1)} collective-permute-done((f32[31,8,128]{2,1,0:T(8,128)S(1)}, f32[31,8,128]{2,1,0:T(8,128)S(1)}, u32[]{:S(2)}, u32[]{:S(2)}) %collective-permute-start.7) | collective-permute-done | bytes 127008 | tf_op jit(solution)/shard_map/ppermute | solution.py:528
  42.2 7.8 %shard_map.54 = (f32[5,16,8,128]{3,2,1,0:T(8,128)}, f32[8,128]{1,0:T(8,128)}) custom-call(f32[5,16,8,128]{3,2,1,0:T(8,128)S(1)} %get-tuple-element.20.refs_0_, f32[8,128]{1,0:T(8,128)S(1)} %get-tuple-element.21.refs_1_, f32[5,8,128]{2,1,0:T(8,128)S(1)} %get-tuple-element.22.refs_2_, f32[86,8,128]{2,1,0:T(8,128)S(1)} %get-tuple-element.29.refs_3_, ...), custom_call_target="tpu_custom_call" | custom-call | tf_op jit(solution)/shard_map/pallas_call | solution.py:463
  (1 shorter events, 0.0 us)
Async XLA Ops:
  1.7 22.0 %collective-permute-start = (f32[43,8,128]{2,1,0:T(8,128)S(1)}, f32[43,8,128]{2,1,0:T(8,128)S(1)}, u32[]{:S(2)}, u32[]{:S(2)}) collective-permute-start(f32[43,8,128]{2,1,0:T(8,128)S(1)} %get-tuple-element.23), channel_id=1, source_target_pairs={{0,1},{2,3},{4,5},{6,7},{8,9},{10,11},{12,13},{14,15},{1,0},{3,2},... | collective-permute-start | bytes 528392 | tf_op jit(solution)/shard_map/ppermute | solution.py:514
  4.8 18.8 %collective-permute-start.1 = (f32[43,8,128]{2,1,0:T(8,128)S(1)}, f32[43,8,128]{2,1,0:T(8,128)S(1)}, u32[]{:S(2)}, u32[]{:S(2)}) collective-permute-start(f32[43,8,128]{2,1,0:T(8,128)S(1)} %get-tuple-element.24), channel_id=1, source_target_pairs={{1,2},{3,4},{5,6},{7,8},{9,10},{11,12},{13,14},{15,0},{2,1},{4,3},... | collective-permute-start | bytes 528392 | tf_op jit(solution)/shard_map/ppermute | solution.py:513
  15.7 4.7 %collective-permute-start.2 = (f32[3,8,128]{2,1,0:T(8,128)S(1)}, f32[3,8,128]{2,1,0:T(8,128)S(1)}, u32[]{:S(2)}, u32[]{:S(2)}) collective-permute-start(f32[3,8,128]{2,1,0:T(8,128)S(1)} %get-tuple-element.27), channel_id=1, source_target_pairs={{0,16},{32,48},{64,80},{96,112},{16,0},{48,32},{80,64},{112,96},{1... | collective-permute-start | bytes 36872 | tf_op jit(solution)/shard_map/ppermute | solution.py:517
  18.0 5.7 %collective-permute-start.3 = (f32[3,8,128]{2,1,0:T(8,128)S(1)}, f32[3,8,128]{2,1,0:T(8,128)S(1)}, u32[]{:S(2)}, u32[]{:S(2)}) collective-permute-start(f32[3,8,128]{2,1,0:T(8,128)S(1)} %get-tuple-element.28), channel_id=1, source_target_pairs={{16,32},{48,64},{80,96},{32,16},{64,48},{96,80},{17,33},{49,65},{8... | collective-permute-start | bytes 36872 | tf_op jit(solution)/shard_map/ppermute | solution.py:516
  24.2 14.8 %collective-permute-start.4 = (f32[31,8,128]{2,1,0:T(8,128)S(1)}, f32[31,8,128]{2,1,0:T(8,128)S(1)}, u32[]{:S(2)}, u32[]{:S(2)}) collective-permute-start(f32[31,8,128]{2,1,0:T(8,128)S(1)} %get-tuple-element.33), channel_id=1, source_target_pairs={{128,256},{256,128},{384,0},{129,257},{257,129},{385,1},{130,258},... | collective-permute-start | bytes 380936 | tf_op jit(solution)/shard_map/ppermute | solution.py:524
  31.4 4.7 %collective-permute-start.5 = (f32[3,8,128]{2,1,0:T(8,128)S(1)}, f32[3,8,128]{2,1,0:T(8,128)S(1)}, u32[]{:S(2)}, u32[]{:S(2)}) collective-permute-start(f32[3,8,128]{2,1,0:T(8,128)S(1)} %get-tuple-element.34), channel_id=1, source_target_pairs={{0,16},{32,48},{64,80},{96,112},{16,0},{48,32},{80,64},{112,96},{1... | collective-permute-start | bytes 36872 | tf_op jit(solution)/shard_map/ppermute | solution.py:526
  33.3 5.7 %collective-permute-start.6 = (f32[3,8,128]{2,1,0:T(8,128)S(1)}, f32[3,8,128]{2,1,0:T(8,128)S(1)}, u32[]{:S(2)}, u32[]{:S(2)}) collective-permute-start(f32[3,8,128]{2,1,0:T(8,128)S(1)} %get-tuple-element.35), channel_id=1, source_target_pairs={{16,32},{48,64},{80,96},{32,16},{64,48},{96,80},{17,33},{49,65},{8... | collective-permute-start | bytes 36872 | tf_op jit(solution)/shard_map/ppermute | solution.py:525
  39.0 3.2 %collective-permute-start.7 = (f32[31,8,128]{2,1,0:T(8,128)S(1)}, f32[31,8,128]{2,1,0:T(8,128)S(1)}, u32[]{:S(2)}, u32[]{:S(2)}) collective-permute-start(f32[31,8,128]{2,1,0:T(8,128)S(1)} %shard_map.53), channel_id=1, source_target_pairs={{0,128},{128,0},{256,384},{384,256},{1,129},{129,1},{257,385},{385... | collective-permute-start | bytes 380936 | tf_op jit(solution)/shard_map/ppermute | solution.py:528

commit v4 on v2

--- a/solution.py
+++ b/solution.py
@@ -95,24 +95,26 @@
     return (pressure(q) - behind) / jnp.sqrt(GAMMA * behind * b[0])
 
 
-def fluxes(q, want=(1, 2, 3)):
+def fluxes(q, want=(1, 2, 3), move=None):
     inv = 1.0 / q[0]
-    v = [None, q[1] * inv, q[2] * inv, q[3] * inv]
-    q11, q22, q33 = q[1] * v[1], q[2] * v[2], q[3] * v[3]
+    v1, v2, v3 = q[1] * inv, q[2] * inv, q[3] * inv
+    q11, q22, q33 = q[1] * v1, q[2] * v2, q[3] * v3
     p = (GAMMA - 1.0) * (q[4] - 0.5 * (q11 + q22 + q33))
     e = q[4] + p
+    q12, q13, q23 = q[1] * v2, q[1] * v3, q[2] * v3
     out = []
     if 1 in want:
-        out.append([q[1], q11 + p, q[2] * v[1], q[3] * v[1], e * v[1]])
+        out.append([q[1], q11 + p, q12, q13, e * v1])
     if 2 in want:
-        out.append([q[2], q[1] * v[2], q22 + p, q[3] * v[2], e * v[2]])
+        out.append([q[2], q12, q22 + p, q23, e * v2])
     if 3 in want:
-        out.append([q[3], q[1] * v[3], q[2] * v[3], q33 + p, e * v[3]])
+        out.append([q[3], q13, q23, q33 + p, e * v3])
+    if move is not None:
+        hx, hz, w = move
+        s = hx * v1 + hz * v3
+        t = s + w
+        out.append([q[0] * t, q[1] * t + p * hx, q[2] * t, q[3] * t + p * hz, q[4] * t + p * s])
     return out
-
-
-def moving(f1, f3, q, hx, hz, w):
-    return [hx * f1[f] + hz * f3[f] + w * q[f] for f in range(5)]
 
 
 def slopes(h, hz, hs, hsz):
@@ -221,8 +223,7 @@
     (f3z,) = fluxes(zq, (3,))
     levels = []
     for x in ([q[f, 13] for f in range(5)], [q[f, 14] for f in range(5)], own, bq):
-        f1, f2, f3 = fluxes(x)
-        levels.append((f1, f2, f3, moving(f1, f3, x, hx, hz, w0)))
+        levels.append(fluxes(x, move=(hx, hz, w0)))
     eta = (LAYERS - 0.5) / LAYERS
     ih = 1.0 / h[...]
     top = []
@@ -235,7 +236,6 @@
     for k in range(4):
         w[k] = speeds[k]
         near[27 + k] = speeds[k]
-        far[27 + k] = speeds[k]
     near_rows = (rw < 2) | (rw >= 6)
     hi_s = hi[26] = strips[9]
     lo_s = lo[26] = strips[8]
@@ -258,7 +258,14 @@
     to_pairs(tile % 2 == 0, z_right, z_left, z_one, z_two)
 
 
-def advance(wn, tile, tiles, q, h, b, z, strips, w, near, far, cross, z_right, z_left, z_one, z_two, *rest):
+def pack_far(wn, far, w, near, out):
+    for i in range(27):
+        out[i] = far[i]
+    for k in range(4):
+        out[27 + k] = jnp.where(wn == 2, near[27 + k], w[k])
+
+
+def advance(wn, tile, tiles, q, h, b, z, strips, w, near, far, z_right, z_left, z_one, z_two, *rest):
     out, h_out, qx, qz, f1x, f2x, gx, f1z, f2z, gz, f3, sx, sz, pt, ptz, zst = rest
     first, last = tile == 0, tile == tiles - 1
 
@@ -279,11 +286,7 @@
     bottom, top = wn == 0, wn == 3
     near_rows = (rw < 2) | (rw >= 6)
 
-    speeds = []
-    for k in range(4):
-        a = jnp.where(bottom, far[27 + k], cross[k])
-        c = jnp.where(top, w[k], near[27 + k])
-        speeds.append(jnp.where(wn < 2, a, c))
+    speeds = [jnp.where(top, w[k], jnp.where(wn == 2, near[27 + k], far[27 + k])) for k in range(4)]
     w0, w0z, w0s, w1 = speeds
 
     surf, surf_z = strips[10], zst[10]
@@ -320,11 +323,11 @@
     parts = []
     for v in range(3):
         x = [strip_q[f][v] for f in range(5)]
-        a1, a2, a3 = fluxes(x)
+        a1, a2, a3, g = fluxes(x, move=(hxs, hzs, w0s))
         d1 = [d_lane(a1[f]) for f in range(5)]
         for f in range(5):
             pt[f, v] = strip_patch(d1[f])
-        parts.append((d1, a2, a3, moving(a1, a3, x, hxs, hzs, w0s)))
+        parts.append((d1, a2, a3, g))
     halo3 = []
     for v in range(2):
         x = [zst[2 * f + v] for f in range(5)]
@@ -364,30 +367,37 @@
     def d_around_halo(f, l):
         return jnp.where(rw < 4, d_rows(f3, f, l, 24), d_rows(f3, f, l, 8))
 
+    def batches(first_l, count, size, body):
+        def step(i, _):
+            todo = []
+            for k in range(size):
+                todo += body(first_l + i * size + k)
+            for ref, at, x in todo:
+                ref[at] = x
+            return 0
+
+        lax.fori_loop(0, count // size, step, 0)
+
     def put_halo(f, l, x):
-        f3[f, l, 24:32] = x
-        f3[f, l, 8:16] = x
-
-    def own_flux(l, _):
-        x = [qx[f, l] for f in range(5)]
-        a1, a2, a3 = fluxes(x)
-        g = moving(a1, a3, x, hx, hz, w0)
-        for f in range(5):
-            f1x[f, l], f2x[f, l], gx[f, l] = a1[f], a2[f], g[f]
-            f3[f, l, 16:24] = a3[f]
-        return 0
-
-    def halo_flux(l, _):
-        x = [qz[f, l] for f in range(5)]
-        a1, a2, a3 = fluxes(x)
-        g = moving(a1, a3, x, hxz, hzz, w0z)
-        for f in range(5):
-            f1z[f, l], f2z[f, l], gz[f, l] = a1[f], a2[f], g[f]
-            put_halo(f, l + 2, a3[f])
-        return 0
-
-    lax.fori_loop(0, 24, own_flux, 0, unroll=8)
-    lax.fori_loop(0, 20, halo_flux, 0, unroll=10)
+        return [(f3, (f, l, slice(24, 32)), x), (f3, (f, l, slice(8, 16)), x)]
+
+    def own_flux(l):
+        a1, a2, a3, g = fluxes([qx[f, l + 4] for f in range(5)], move=(hx, hz, w0))
+        todo = []
+        for f in range(5):
+            todo += [(r, (f, l + 4), x[f]) for r, x in ((f1x, a1), (f2x, a2), (gx, g))]
+            todo += [(f3, (f, l + 4, slice(16, 24)), a3[f])]
+        return todo
+
+    def halo_flux(l):
+        a1, a2, a3, g = fluxes([qz[f, l + 2] for f in range(5)], move=(hxz, hzz, w0z))
+        todo = []
+        for f in range(5):
+            todo += [(r, (f, l + 2), x[f]) for r, x in ((f1z, a1), (f2z, a2), (gz, g))] + put_halo(f, l + 4, a3[f])
+        return todo
+
+    batches(-4, 24, 4, own_flux)
+    batches(-2, 20, 4, halo_flux)
 
     def d_normal(ref, f, l):
         return (ref[f, l - 2] - ref[f, l + 2]) + 8.0 * (ref[f, l + 1] - ref[f, l - 1])
@@ -398,31 +408,28 @@
     def patch_shift(l):
         return 116 - 16 * (l & 7)
 
-    def own_edge(l):
-        eta = eta_of(l)
-        for f in range(5):
-            dx = patched(d_lane(f1x[f, l + 4]), pltpu.roll(pt[f, 2], patch_shift(l), 1))
+    def own_section(l):
+        eta, shift, todo = eta_of(l), patch_shift(l), []
+        third = (l + 8) >> 3
+        third = jnp.where((third == 0) | (third == 3), 2, third - 1)
+        for f in range(5):
+            dx = patched(d_lane(f1x[f, l + 4]), pltpu.roll(pt[f, third], shift, 1))
             da = d_around(f, l + 4)
             dn, dg = d_normal(f2x, f, l + 4), d_normal(gx, f, l + 4)
-            sx[f, l + 2] = qx[f, l + 4] + C * (ih * (eta * dg - dn) - (dx + da))
-
-    def section(l, _):
-        eta = eta_of(l)
-        half = l >> 3
-        shift = patch_shift(l)
-        for f in range(5):
-            dx = patched(d_lane(f1x[f, l + 4]), pltpu.roll(pt[f, half], shift, 1))
-            dxz = patched(d_lane(f1z[f, l + 2]), pltpu.roll(ptz[f, half], shift, 1))
-            da, daz = d_around(f, l + 4), d_around_halo(f, l + 4)
-            dn, dg = d_normal(f2x, f, l + 4), d_normal(gx, f, l + 4)
-            sx[f, l + 2] = qx[f, l + 4] + C * (ih * (eta * dg - dn) - (dx + da))
+            todo.append((sx, (f, l + 2), qx[f, l + 4] + C * (ih * (eta * dg - dn) - (dx + da))))
+        return todo
+
+    def halo_section(l):
+        eta, shift, todo = eta_of(l), patch_shift(l), []
+        for f in range(5):
+            dx = patched(d_lane(f1z[f, l + 2]), pltpu.roll(ptz[f, l >> 3], shift, 1))
+            da = d_around_halo(f, l + 4)
             dn, dg = d_normal(f2z, f, l + 2), d_normal(gz, f, l + 2)
-            sz[f, l] = qz[f, l + 2] + C * (ihz * (eta * dg - dn) - (dxz + daz))
-        return 0
-
-    lax.fori_loop(0, NL, section, 0, unroll=8)
-    for l in (-2, -1, 16, 17):
-        own_edge(l)
+            todo.append((sz, (f, l), qz[f, l + 2] + C * (ihz * (eta * dg - dn) - (dx + da))))
+        return todo
+
+    batches(-2, 20, 4, own_section)
+    batches(0, NL, 4, halo_section)
     for f in range(5):
         for k in range(2):
             sx[f, k] = jnp.where(bottom, MIRROR[f] * sx[f, 3 - k], sx[f, k])
@@ -438,37 +445,31 @@
         for f in range(5):
             pt[f, v] = strip_ends(a1[f])
 
-    def own_flux_two(l, _):
-        x = [sx[f, l] for f in range(5)]
-        a1, a2, a3 = fluxes(x)
-        g = moving(a1, a3, x, hx1, hz1, w1)
-        for f in range(5):
-            f1x[f, l], f2x[f, l], gx[f, l] = a1[f], a2[f], g[f]
-            f3[f, l, 16:24] = a3[f]
-        return 0
-
-    def halo_flux_two(l, _):
+    def own_flux_two(l):
+        a1, a2, a3, g = fluxes([sx[f, l + 2] for f in range(5)], move=(hx1, hz1, w1))
+        todo = []
+        for f in range(5):
+            todo += [(r, (f, l + 4), x[f]) for r, x in ((f1x, a1), (f2x, a2), (gx, g))]
+            todo += [(f3, (f, l + 4, slice(16, 24)), a3[f])]
+        return todo
+
+    def halo_flux_two(l):
         (a3,) = fluxes([sz[f, l] for f in range(5)], (3,))
-        for f in range(5):
-            put_halo(f, l + 2, a3[f])
-        return 0
-
-    lax.fori_loop(0, 20, own_flux_two, 0, unroll=10)
-    lax.fori_loop(0, NL, halo_flux_two, 0, unroll=8)
-
-    def final(l, _):
-        eta = eta_of(l)
-        half = l >> 3
-        shift = patch_shift(l)
-        for f in range(5):
-            dx = d_ends(f1x[f, l + 2], pltpu.roll(pt[f, half], shift, 1))
-            da = d_around(f, l + 2)
-            dn, dg = d_normal(f2x, f, l + 2), d_normal(gx, f, l + 2)
+        return [x for f in range(5) for x in put_halo(f, l + 4, a3[f])]
+
+    def final(l):
+        eta, shift, todo = eta_of(l), patch_shift(l), []
+        for f in range(5):
+            dx = d_ends(f1x[f, l + 4], pltpu.roll(pt[f, l >> 3], shift, 1))
+            da = d_around(f, l + 4)
+            dn, dg = d_normal(f2x, f, l + 4), d_normal(gx, f, l + 4)
             rate = ih1 * (eta * dg - dn) - (dx + da)
-            out[f, l] = 0.5 * (qx[f, l + 4] + sx[f, l + 2] + C * rate)
-        return 0
-
-    lax.fori_loop(0, NL, final, 0, unroll=8)
+            todo.append((out, (f, l), 0.5 * (qx[f, l + 4] + sx[f, l + 2] + C * rate)))
+        return todo
+
+    batches(-2, 20, 4, own_flux_two)
+    batches(0, NL, 4, halo_flux_two)
+    batches(0, NL, 4, final)
 
 
 def call(body, ins, outs, scratch=(), sems=0, space=VM):
@@ -497,6 +498,10 @@
 
 def stage_second(*refs):
     pack_second(lax.axis_index("az") % 2 == 1, lax.axis_index("wn"), *where_am_i(), *refs)
+
+
+def stage_far(*refs):
+    pack_far(lax.axis_index("wn"), *refs)
 
 
 def stage_advance(*refs):
@@ -527,17 +532,17 @@
     halo, strips, w, near, far, z_right, z_left, one, two = call(
         stage_second,
         (*own, a1, a2, right, left, s1, s2),
-        [(NP, *plane), (UNITS, *plane), (4, *plane)] + [(31, *plane)] * 2 + [(3, *plane)] * 4,
+        [(NP, *plane), (UNITS, *plane), (4, *plane), (31, *plane), (27, *plane)] + [(3, *plane)] * 4,
         [(27, *plane)] * 2,
     )
-    cross = lax.ppermute(w, "wn", [(3, 1)])
-    far = lax.ppermute(far, "wn", [(1, 2), (2, 1), (3, 0)])
+    near = lax.ppermute(near, "wn", [(0, 1), (1, 0), (2, 3), (3, 2)])
     s2 = lax.ppermute(two, "sx", swaps(tiles, 1, False))
     s1 = lax.ppermute(one, "sx", swaps(tiles, 0, False))
-    near = lax.ppermute(near, "wn", [(0, 1), (1, 0), (2, 3), (3, 2)])
+    (far,) = call(stage_far, (far, w, near), [(31, *plane)])
+    far = lax.ppermute(far, "wn", [(1, 2), (2, 1), (3, 0)])
     return call(
         stage_advance,
-        (*own, halo, strips, w, near, far, cross, z_right, z_left, s1, s2),
+        (*own, halo, strips, w, near, far, z_right, z_left, s1, s2),
         [(5, NL, 8, 128), (8, 128)],
         [(5, 24, 8, 128), (5, 20, 8, 128)]
         + [(5, 24, 8, 128)] * 3

time: 49.3 us -> 47.6 us (0.966)
  the two profiles are of different devices: /device:TPU:37 before, /device:TPU:33 now
where the time goes in v4:
time: 47.6 us; the launch traced here: 47.3 us
  starting transfers between devices  31.3 us (66%)
  waiting for transfers between devices  8.41 us (18%)
  Pallas kernels  6.86 us (14%)
  between operations  0.71 us (1%)
    ppermute x1, starting transfers between devices, per_device(): a2 = lax.ppermute(two, 'az', swaps(around, 1, True))  10.6 us
    pallas_call x5, Pallas kernels, call(): pl.pallas_call(body, out_shape=shapes, in_specs=[space] * len(ins), out_s...  6.86 us
    ppermute x2, waiting for transfers between devices, per_device(): s2 = lax.ppermute(two, 'sx', swaps(tiles, 1, False))  6.07 us
    ppermute x1, starting transfers between devices, per_device(): far = lax.ppermute(far, 'wn', [(1, 2), (2, 1), (3, 0)])  4.9 us
    ppermute x1, starting transfers between devices, per_device(): near = lax.ppermute(near, 'wn', [(0, 1), (1, 0), (2, 3), (3, 2)])  4.57 us
    ppermute x2, starting transfers between devices, per_device(): s1 = lax.ppermute(one, 'sx', swaps(tiles, 0, False))  4.21 us
    ppermute x2, starting transfers between devices, per_device(): s2 = lax.ppermute(two, 'sx', swaps(tiles, 1, False))  3.84 us
    ppermute x1, starting transfers between devices, per_device(): a1 = lax.ppermute(one, 'az', swaps(around, 0, True))  3.12 us
  transfers between devices with their start and end apart: 8, of which 5 were waited for; matrix products, arithmetic and copies ran while one was open for 0% of the time, Pallas kernels for 0%

profile of v4, /device:TPU:33, one launch (start us, length us, event | category | flops | bytes accessed | tf_op | source)
XLA Modules:
  0.0 47.3 jit_solution(10736775164837717838)
XLA Ops:
  0.6 1.0 %shard_map.50 = (f32[5,16,8,128]{3,2,1,0:T(8,128)S(1)}, f32[8,128]{1,0:T(8,128)S(1)}, f32[5,8,128]{2,1,0:T(8,128)S(1)}, f32[43,8,128]{2,1,0:T(8,128)S(1)}, f32[43,8,128]{2,1,0:T(8,128)S(1)}) custom-call(f32[5,16,8,128]{3,2,1,0:T(8,128)} %refs_0_.1, f32[8,128]{1,0:T(8,128)} %refs_1_.1, f32[5,8,128]{2,1,0:T(8,128)} %refs_2_.1), custom_call_target="tpu_custom_call" | custom-call | tf_op jit(solution)/shard_map/pallas_call | solution.py:477
  1.7 3.1 %collective-permute-start = (f32[43,8,128]{2,1,0:T(8,128)S(1)}, f32[43,8,128]{2,1,0:T(8,128)S(1)}, u32[]{:S(2)}, u32[]{:S(2)}) collective-permute-start(f32[43,8,128]{2,1,0:T(8,128)S(1)} %get-tuple-element.23), channel_id=1, source_target_pairs={{0,1},{2,3},{4,5},{6,7},{8,9},{10,11},{12,13},{14,15},{1,0},{3,2},... | collective-permute-start | bytes 528392 | tf_op jit(solution)/shard_map/ppermute | solution.py:528
  4.8 10.6 %collective-permute-start.1 = (f32[43,8,128]{2,1,0:T(8,128)S(1)}, f32[43,8,128]{2,1,0:T(8,128)S(1)}, u32[]{:S(2)}, u32[]{:S(2)}) collective-permute-start(f32[43,8,128]{2,1,0:T(8,128)S(1)} %get-tuple-element.24), channel_id=1, source_target_pairs={{1,2},{3,4},{5,6},{7,8},{9,10},{11,12},{13,14},{15,0},{2,1},{4,3},... | collective-permute-start | bytes 528392 | tf_op jit(solution)/shard_map/ppermute | solution.py:527
  15.4 0.2 shard_map.51
  15.7 2.3 %collective-permute-start.2 = (f32[3,8,128]{2,1,0:T(8,128)S(1)}, f32[3,8,128]{2,1,0:T(8,128)S(1)}, u32[]{:S(2)}, u32[]{:S(2)}) collective-permute-start(f32[3,8,128]{2,1,0:T(8,128)S(1)} %get-tuple-element.27), channel_id=1, source_target_pairs={{0,16},{32,48},{64,80},{96,112},{16,0},{48,32},{80,64},{112,96},{1... | collective-permute-start | bytes 36872 | tf_op jit(solution)/shard_map/ppermute | solution.py:531
  18.0 1.9 %collective-permute-start.3 = (f32[3,8,128]{2,1,0:T(8,128)S(1)}, f32[3,8,128]{2,1,0:T(8,128)S(1)}, u32[]{:S(2)}, u32[]{:S(2)}) collective-permute-start(f32[3,8,128]{2,1,0:T(8,128)S(1)} %get-tuple-element.28), channel_id=1, source_target_pairs={{16,32},{48,64},{80,96},{32,16},{64,48},{96,80},{17,33},{49,65},{8... | collective-permute-start | bytes 36872 | tf_op jit(solution)/shard_map/ppermute | solution.py:530
  19.9 0.5 %collective-permute-done.2.refs_7_ = f32[3,8,128]{2,1,0:T(8,128)S(1)} collective-permute-done((f32[3,8,128]{2,1,0:T(8,128)S(1)}, f32[3,8,128]{2,1,0:T(8,128)S(1)}, u32[]{:S(2)}, u32[]{:S(2)}) %collective-permute-start.2) | collective-permute-done | bytes 12320 | tf_op jit(solution)/shard_map/ppermute | solution.py:531
  20.4 3.2 %collective-permute-done.3.refs_8_ = f32[3,8,128]{2,1,0:T(8,128)S(1)} collective-permute-done((f32[3,8,128]{2,1,0:T(8,128)S(1)}, f32[3,8,128]{2,1,0:T(8,128)S(1)}, u32[]{:S(2)}, u32[]{:S(2)}) %collective-permute-start.3) | collective-permute-done | bytes 12320 | tf_op jit(solution)/shard_map/ppermute | solution.py:530
  23.6 0.0 collective-permute-done.refs_3_
  23.6 0.0 collective-permute-done.1.refs_4_
  23.6 0.5 %shard_map.52 = (f32[86,8,128]{2,1,0:T(8,128)S(1)}, f32[11,8,128]{2,1,0:T(8,128)S(1)}, f32[4,8,128]{2,1,0:T(8,128)S(1)}, f32[31,8,128]{2,1,0:T(8,128)S(1)}, f32[...) custom-call(f32[5,16,8,128]{3,2,1,0:T(8,128)S(1)} %get-tuple-element, ...), custom_call_target="tpu_custom_call" | custom-call | tf_op jit(solution)/shard_map/pallas_call | solution.py:477
  24.2 4.6 %collective-permute-start.4 = (f32[31,8,128]{2,1,0:T(8,128)S(1)}, f32[31,8,128]{2,1,0:T(8,128)S(1)}, u32[]{:S(2)}, u32[]{:S(2)}) collective-permute-start(f32[31,8,128]{2,1,0:T(8,128)S(1)} %get-tuple-element.32), channel_id=1, source_target_pairs={{0,128},{128,0},{256,384},{384,256},{1,129},{129,1},{257,385},{385... | collective-permute-start | bytes 380936 | tf_op jit(solution)/shard_map/ppermute | solution.py:538
  28.7 1.0 %collective-permute-done.4.refs_2_.refs_6_ = f32[31,8,128]{2,1,0:T(8,128)S(1)} collective-permute-done((f32[31,8,128]{2,1,0:T(8,128)S(1)}, f32[31,8,128]{2,1,0:T(8,128)S(1)}, u32[]{:S(2)}, u32[]{:S(2)}) %collective-permute-start.4) | collective-permute-done | bytes 127008 | tf_op jit(solution)/shard_map/ppermute | solution.py:538
  29.7 4.9 %collective-permute-start.5 = (f32[31,8,128]{2,1,0:T(8,128)S(1)}, f32[31,8,128]{2,1,0:T(8,128)S(1)}, u32[]{:S(2)}, u32[]{:S(2)}) collective-permute-start(f32[31,8,128]{2,1,0:T(8,128)S(1)} %shard_map.53), channel_id=1, source_target_pairs={{128,256},{256,128},{384,0},{129,257},{257,129},{385,1},{130,258},... | collective-permute-start | bytes 380936 | tf_op jit(solution)/shard_map/ppermute | solution.py:542
  34.6 1.9 %collective-permute-start.6 = (f32[3,8,128]{2,1,0:T(8,128)S(1)}, f32[3,8,128]{2,1,0:T(8,128)S(1)}, u32[]{:S(2)}, u32[]{:S(2)}) collective-permute-start(f32[3,8,128]{2,1,0:T(8,128)S(1)} %get-tuple-element.36), channel_id=1, source_target_pairs={{0,16},{32,48},{64,80},{96,112},{16,0},{48,32},{80,64},{112,96},{1... | collective-permute-start | bytes 36872 | tf_op jit(solution)/shard_map/ppermute | solution.py:540
  36.6 1.9 %collective-permute-start.7 = (f32[3,8,128]{2,1,0:T(8,128)S(1)}, f32[3,8,128]{2,1,0:T(8,128)S(1)}, u32[]{:S(2)}, u32[]{:S(2)}) collective-permute-start(f32[3,8,128]{2,1,0:T(8,128)S(1)} %get-tuple-element.37), channel_id=1, source_target_pairs={{16,32},{48,64},{80,96},{32,16},{64,48},{96,80},{17,33},{49,65},{8... | collective-permute-start | bytes 36872 | tf_op jit(solution)/shard_map/ppermute | solution.py:539
  38.5 0.9 %collective-permute-done.6.refs_10_ = f32[3,8,128]{2,1,0:T(8,128)S(1)} collective-permute-done((f32[3,8,128]{2,1,0:T(8,128)S(1)}, f32[3,8,128]{2,1,0:T(8,128)S(1)}, u32[]{:S(2)}, u32[]{:S(2)}) %collective-permute-start.6) | collective-permute-done | bytes 12320 | tf_op jit(solution)/shard_map/ppermute | solution.py:540
  39.4 2.8 %collective-permute-done.7.refs_11_ = f32[3,8,128]{2,1,0:T(8,128)S(1)} collective-permute-done((f32[3,8,128]{2,1,0:T(8,128)S(1)}, f32[3,8,128]{2,1,0:T(8,128)S(1)}, u32[]{:S(2)}, u32[]{:S(2)}) %collective-permute-start.7) | collective-permute-done | bytes 12320 | tf_op jit(solution)/shard_map/ppermute | solution.py:539
  42.2 0.0 collective-permute-done.5.refs_7_
  42.2 5.1 %shard_map.54 = (f32[5,16,8,128]{3,2,1,0:T(8,128)}, f32[8,128]{1,0:T(8,128)}) custom-call(f32[5,16,8,128]{3,2,1,0:T(8,128)S(1)} %get-tuple-element.20.refs_0_, f32[8,128]{1,0:T(8,128)S(1)} %get-tuple-element.21.refs_1_, f32[5,8,128]{2,1,0:T(8,128)S(1)} %get-tuple-element.22.refs_2_, f32[86,8,128]{2,1,0:T(8,128)S(1)} %get-tuple-element.29.refs_3_, ...), custom_call_target="tpu_custom_call" | custom-call | tf_op jit(solution)/shard_map/pallas_call | solution.py:477
  (1 shorter events, 0.0 us)
Async XLA Ops:
  1.7 22.0 %collective-permute-start = (f32[43,8,128]{2,1,0:T(8,128)S(1)}, f32[43,8,128]{2,1,0:T(8,128)S(1)}, u32[]{:S(2)}, u32[]{:S(2)}) collective-permute-start(f32[43,8,128]{2,1,0:T(8,128)S(1)} %get-tuple-element.23), channel_id=1, source_target_pairs={{0,1},{2,3},{4,5},{6,7},{8,9},{10,11},{12,13},{14,15},{1,0},{3,2},... | collective-permute-start | bytes 528392 | tf_op jit(solution)/shard_map/ppermute | solution.py:528
  4.8 18.8 %collective-permute-start.1 = (f32[43,8,128]{2,1,0:T(8,128)S(1)}, f32[43,8,128]{2,1,0:T(8,128)S(1)}, u32[]{:S(2)}, u32[]{:S(2)}) collective-permute-start(f32[43,8,128]{2,1,0:T(8,128)S(1)} %get-tuple-element.24), channel_id=1, source_target_pairs={{1,2},{3,4},{5,6},{7,8},{9,10},{11,12},{13,14},{15,0},{2,1},{4,3},... | collective-permute-start | bytes 528392 | tf_op jit(solution)/shard_map/ppermute | solution.py:527
  15.7 4.7 %collective-permute-start.2 = (f32[3,8,128]{2,1,0:T(8,128)S(1)}, f32[3,8,128]{2,1,0:T(8,128)S(1)}, u32[]{:S(2)}, u32[]{:S(2)}) collective-permute-start(f32[3,8,128]{2,1,0:T(8,128)S(1)} %get-tuple-element.27), channel_id=1, source_target_pairs={{0,16},{32,48},{64,80},{96,112},{16,0},{48,32},{80,64},{112,96},{1... | collective-permute-start | bytes 36872 | tf_op jit(solution)/shard_map/ppermute | solution.py:531
  18.0 5.7 %collective-permute-start.3 = (f32[3,8,128]{2,1,0:T(8,128)S(1)}, f32[3,8,128]{2,1,0:T(8,128)S(1)}, u32[]{:S(2)}, u32[]{:S(2)}) collective-permute-start(f32[3,8,128]{2,1,0:T(8,128)S(1)} %get-tuple-element.28), channel_id=1, source_target_pairs={{16,32},{48,64},{80,96},{32,16},{64,48},{96,80},{17,33},{49,65},{8... | collective-permute-start | bytes 36872 | tf_op jit(solution)/shard_map/ppermute | solution.py:530
  24.2 5.5 %collective-permute-start.4 = (f32[31,8,128]{2,1,0:T(8,128)S(1)}, f32[31,8,128]{2,1,0:T(8,128)S(1)}, u32[]{:S(2)}, u32[]{:S(2)}) collective-permute-start(f32[31,8,128]{2,1,0:T(8,128)S(1)} %get-tuple-element.32), channel_id=1, source_target_pairs={{0,128},{128,0},{256,384},{384,256},{1,129},{129,1},{257,385},{385... | collective-permute-start | bytes 380936 | tf_op jit(solution)/shard_map/ppermute | solution.py:538
  29.7 12.5 %collective-permute-start.5 = (f32[31,8,128]{2,1,0:T(8,128)S(1)}, f32[31,8,128]{2,1,0:T(8,128)S(1)}, u32[]{:S(2)}, u32[]{:S(2)}) collective-permute-start(f32[31,8,128]{2,1,0:T(8,128)S(1)} %shard_map.53), channel_id=1, source_target_pairs={{128,256},{256,128},{384,0},{129,257},{257,129},{385,1},{130,258},... | collective-permute-start | bytes 380936 | tf_op jit(solution)/shard_map/ppermute | solution.py:542
  34.6 4.7 %collective-permute-start.6 = (f32[3,8,128]{2,1,0:T(8,128)S(1)}, f32[3,8,128]{2,1,0:T(8,128)S(1)}, u32[]{:S(2)}, u32[]{:S(2)}) collective-permute-start(f32[3,8,128]{2,1,0:T(8,128)S(1)} %get-tuple-element.36), channel_id=1, source_target_pairs={{0,16},{32,48},{64,80},{96,112},{16,0},{48,32},{80,64},{112,96},{1... | collective-permute-start | bytes 36872 | tf_op jit(solution)/shard_map/ppermute | solution.py:540
  36.6 5.7 %collective-permute-start.7 = (f32[3,8,128]{2,1,0:T(8,128)S(1)}, f32[3,8,128]{2,1,0:T(8,128)S(1)}, u32[]{:S(2)}, u32[]{:S(2)}) collective-permute-start(f32[3,8,128]{2,1,0:T(8,128)S(1)} %get-tuple-element.37), channel_id=1, source_target_pairs={{16,32},{48,64},{80,96},{32,16},{64,48},{96,80},{17,33},{49,65},{8... | collective-permute-start | bytes 36872 | tf_op jit(solution)/shard_map/ppermute | solution.py:539

commit v5 on v4

--- a/solution.py
+++ b/solution.py
@@ -265,8 +265,118 @@
         out[27 + k] = jnp.where(wn == 2, near[27 + k], w[k])
 
 
-def advance(wn, tile, tiles, q, h, b, z, strips, w, near, far, z_right, z_left, z_one, z_two, *rest):
-    out, h_out, qx, qz, f1x, f2x, gx, f1z, f2z, gz, f3, sx, sz, pt, ptz, zst = rest
+def d_rows(f3, f, l, at):
+    m2, m1, p1, p2 = (f3[f, l, pl.ds(at + k, 8)] for k in (-2, -1, 1, 2))
+    return (m2 - p2) + 8.0 * (p1 - m1)
+
+
+def d_around(f3, f, l):
+    return d_rows(f3, f, l, 16)
+
+
+def d_around_halo(f3, f, l):
+    return jnp.where(row() < 4, d_rows(f3, f, l, 24), d_rows(f3, f, l, 8))
+
+
+def put_halo(f3, f, l, x):
+    return [(f3, (f, l, slice(24, 32)), x), (f3, (f, l, slice(8, 16)), x)]
+
+
+def d_normal(get, l):
+    return (get(l - 2) - get(l + 2)) + 8.0 * (get(l + 1) - get(l - 1))
+
+
+def plane_at(ref, f):
+    return lambda l: ref[f, l]
+
+
+def patch_shift(l):
+    return 116 - 16 * (l & 7)
+
+
+def edges(patch):
+    return patched(jnp.zeros_like(patch), patch)
+
+
+def batches(first_l, count, size, body):
+    def step(i, _):
+        todo = []
+        for k in range(size):
+            todo += body(first_l + i * size + k)
+        for ref, at, x in todo:
+            ref[at] = x
+        return 0
+
+    lax.fori_loop(0, count // size, step, 0)
+
+
+def prepare(wn, q, h, z, strips, _far, tx, bx, tz, bz, ez, f1x, f2x, gx, f1z, f2z, gz, f3, pt):
+    h0, h0z = h[...], z[80]
+    hx = SCALE * patched(d_lane(h0), rl(strip_patch(d_lane(spread(strips[10], 0))), -12))
+    hz, hzz = (SCALE * x for x in d_ring(h0, h0z))
+    ih, ihz = C / h0, C / h0z
+    base = wn * NL
+    for v in range(2):
+        (a1,) = fluxes([strips[2 * f + v] for f in range(5)], (1,))
+        for f in range(5):
+            pt[f, v] = strip_patch(d_lane(a1[f]))
+
+    def own_flux(l):
+        a1, a2, a3, g = fluxes([q[f, l] for f in range(5)], move=(hx, hz, 0.0))
+        todo = []
+        for f in range(5):
+            todo += [(r, (f, l), x[f]) for r, x in ((f1x, a1), (f2x, a2), (gx, g))]
+            todo += [(f3, (f, l, slice(16, 24)), a3[f])]
+        return todo
+
+    def halo_flux(l):
+        a1, a2, a3 = fluxes([z[f * NL + l] for f in range(5)])
+        todo = []
+        for f in range(5):
+            todo += [(r, (f, l), x) for r, x in ((f1z, a1[f]), (f2z, a2[f]), (gz, hzz * a3[f]))]
+            todo += put_halo(f3, f, l, a3[f])
+        return todo
+
+    batches(0, NL, 4, own_flux)
+    batches(0, NL, 4, halo_flux)
+
+    def own_surface(f, l):
+        dx = patched(d_lane(f1x[f, l]), pltpu.roll(pt[f, l >> 3], patch_shift(l), 1))
+        return q[f, l] - C * (dx + d_around(f3, f, l))
+
+    def halo_surface(f, l):
+        ln = lane()
+        dx = jnp.where((ln < 2) | (ln >= 126), 0.0, d_lane(f1z[f, l]))
+        return z[f * NL + l] - C * (dx + d_around_halo(f3, f, l))
+
+    def own_inner(l):
+        k, todo = ih * (((base + l).astype(F32) + 0.5) / LAYERS), []
+        for f in range(5):
+            t = own_surface(f, l) + (k * d_normal(plane_at(gx, f), l) - ih * d_normal(plane_at(f2x, f), l))
+            todo += [(tx, (f, l), t), (bx, (f, l), k * d_normal(plane_at(q, f), l))]
+        return todo
+
+    def halo_inner(l):
+        k, todo = ihz * (((base + l).astype(F32) + 0.5) / LAYERS), []
+        for f in range(5):
+            t = halo_surface(f, l) + (k * d_normal(plane_at(gz, f), l) - ihz * d_normal(plane_at(f2z, f), l))
+            todo += [(tz, (f, l), t), (bz, (f, l), k * d_normal(lambda i, f=f: z[f * NL + i], l))]
+            todo += [(ez, (f, l), k * d_normal(plane_at(f1z, f), l))]
+        return todo
+
+    def outer(l):
+        return [(tx, (f, l), own_surface(f, l)) for f in range(5)] + [
+            (tz, (f, l), halo_surface(f, l)) for f in range(5)
+        ]
+
+    batches(2, 12, 4, own_inner)
+    batches(2, 12, 4, halo_inner)
+    for l in (0, 14):
+        batches(l, 2, 2, outer)
+
+
+def advance(wn, tile, tiles, q, h, b, z, strips, w, near, far, z_right, z_left, z_one, z_two, tx, bx, tz, bz, ez, *rest):
+    out, h_out, qw, zw, f1w, f2w, gw, f2zw, gzw, f1x, f2x, gx, f3, sx, sz, pt, ptz, zst = rest
     first, last = tile == 0, tile == tiles - 1
 
     def put_strip(u, x):
@@ -293,18 +403,19 @@
     strip_q = []
     for f in range(5):
         sign = MIRROR[f]
-        bq, bz = b[f], z[81 + f]
-        for k in range(NL):
-            qx[f, 4 + k] = q[f, k]
-            qz[f, 2 + k] = z[f * NL + k]
+        bq, bz_ = b[f], z[81 + f]
         for k in range(4):
-            qx[f, k] = jnp.where(bottom, sign * q[f, 3 - k], below(4 * f + k))
-            qx[f, 20 + k] = jnp.where(top, bq, above(4 * f + k))
+            qw[f, k] = jnp.where(bottom, sign * q[f, 3 - k], below(4 * f + k))
+            qw[f, 4 + k] = q[f, k]
+            qw[f, 8 + k] = q[f, 12 + k]
+            qw[f, 12 + k] = jnp.where(top, bq, above(4 * f + k))
+            zw[f, 2 + k] = z[f * NL + k]
+            zw[f, 6 + k] = z[f * NL + 12 + k]
         zb, za = below(20 + f), above(20 + f)
-        qz[f, 0] = jnp.where(bottom, sign * z[f * NL + 1], zb)
-        qz[f, 1] = jnp.where(bottom, sign * z[f * NL], rs(zb, 4))
-        qz[f, 18] = jnp.where(top, bz, za)
-        qz[f, 19] = jnp.where(top, bz, rs(za, 4))
+        zw[f, 0] = jnp.where(bottom, sign * z[f * NL + 1], zb)
+        zw[f, 1] = jnp.where(bottom, sign * z[f * NL], rs(zb, 4))
+        zw[f, 10] = jnp.where(top, bz_, za)
+        zw[f, 11] = jnp.where(top, bz_, rs(za, 4))
         s_lo, s_hi = strips[2 * f], strips[2 * f + 1]
         if f < 4:
             sb, sa = rl(below(25), 96 - 32 * f), rl(above(25), -32 * f)
@@ -357,79 +468,60 @@
             done.append(s)
         strip_s.append(done)
 
-    def d_rows(ref, f, l, at):
-        m2, m1, p1, p2 = (ref[f, l, pl.ds(at + k, 8)] for k in (-2, -1, 1, 2))
-        return (m2 - p2) + 8.0 * (p1 - m1)
-
-    def d_around(f, l):
-        return d_rows(f3, f, l, 16)
-
-    def d_around_halo(f, l):
-        return jnp.where(rw < 4, d_rows(f3, f, l, 24), d_rows(f3, f, l, 8))
-
-    def batches(first_l, count, size, body):
-        def step(i, _):
-            todo = []
-            for k in range(size):
-                todo += body(first_l + i * size + k)
-            for ref, at, x in todo:
-                ref[at] = x
-            return 0
-
-        lax.fori_loop(0, count // size, step, 0)
-
-    def put_halo(f, l, x):
-        return [(f3, (f, l, slice(24, 32)), x), (f3, (f, l, slice(8, 16)), x)]
-
-    def own_flux(l):
-        a1, a2, a3, g = fluxes([qx[f, l + 4] for f in range(5)], move=(hx, hz, w0))
+    def own_flux(k):
+        a1, a2, a3, g = fluxes([qw[f, k] for f in range(5)], move=(hx, hz, w0))
         todo = []
         for f in range(5):
-            todo += [(r, (f, l + 4), x[f]) for r, x in ((f1x, a1), (f2x, a2), (gx, g))]
-            todo += [(f3, (f, l + 4, slice(16, 24)), a3[f])]
-        return todo
-
-    def halo_flux(l):
-        a1, a2, a3, g = fluxes([qz[f, l + 2] for f in range(5)], move=(hxz, hzz, w0z))
-        todo = []
-        for f in range(5):
-            todo += [(r, (f, l + 2), x[f]) for r, x in ((f1z, a1), (f2z, a2), (gz, g))] + put_halo(f, l + 4, a3[f])
-        return todo
-
-    batches(-4, 24, 4, own_flux)
-    batches(-2, 20, 4, halo_flux)
-
-    def d_normal(ref, f, l):
-        return (ref[f, l - 2] - ref[f, l + 2]) + 8.0 * (ref[f, l + 1] - ref[f, l - 1])
+            todo += [(r, (f, k), x[f]) for r, x in ((f1w, a1), (f2w, a2), (gw, g))]
+            todo += [(f3, (f, k, slice(16, 24)), a3[f])]
+        return todo
 
     def eta_of(l):
         return ((base + l).astype(F32) + 0.5) / LAYERS
 
-    def patch_shift(l):
-        return 116 - 16 * (l & 7)
-
-    def own_section(l):
-        eta, shift, todo = eta_of(l), patch_shift(l), []
-        third = (l + 8) >> 3
-        third = jnp.where((third == 0) | (third == 3), 2, third - 1)
-        for f in range(5):
-            dx = patched(d_lane(f1x[f, l + 4]), pltpu.roll(pt[f, third], shift, 1))
-            da = d_around(f, l + 4)
-            dn, dg = d_normal(f2x, f, l + 4), d_normal(gx, f, l + 4)
-            todo.append((sx, (f, l + 2), qx[f, l + 4] + C * (ih * (eta * dg - dn) - (dx + da))))
-        return todo
-
-    def halo_section(l):
-        eta, shift, todo = eta_of(l), patch_shift(l), []
-        for f in range(5):
-            dx = patched(d_lane(f1z[f, l + 2]), pltpu.roll(ptz[f, l >> 3], shift, 1))
-            da = d_around_halo(f, l + 4)
-            dn, dg = d_normal(f2z, f, l + 2), d_normal(gz, f, l + 2)
-            todo.append((sz, (f, l), qz[f, l + 2] + C * (ihz * (eta * dg - dn) - (dx + da))))
-        return todo
-
-    batches(-2, 20, 4, own_section)
-    batches(0, NL, 4, halo_section)
+    batches(0, 16, 4, own_flux)
+    for k in range(12):
+        a2, a3, g = fluxes([zw[f, k] for f in range(5)], (2, 3), move=(hxz, hzz, w0z))
+        for f in range(5):
+            f2zw[f, k], gzw[f, k] = a2[f], g[f]
+            if k in (0, 1, 10, 11):
+                for ref, at, x in put_halo(f3, f, k + 2, a3[f]):
+                    ref[at] = x
+
+    def normal_own(f, k, eta):
+        return ih * (eta * d_normal(plane_at(gw, f), k) - d_normal(plane_at(f2w, f), k))
+
+    def ghost_layer(m):
+        upper = (m >= 2).astype(jnp.int32)
+        k, l, todo = 2 + m + 8 * upper, m - 2 + 16 * upper, []
+        for f in range(5):
+            dx = patched(d_lane(f1w[f, k]), pltpu.roll(pt[f, 2], patch_shift(l), 1))
+            s = qw[f, k] + C * (normal_own(f, k, eta_of(l)) - (dx + d_around(f3, f, k)))
+            todo.append((sx, (f, l + 2), s))
+        return todo
+
+    def outer(m):
+        upper = (m >= 2).astype(jnp.int32)
+        k, kz, l, todo = 4 + m + 4 * upper, 2 + m + 4 * upper, m + 12 * upper, []
+        eta, half, shift = eta_of(l), l >> 3, patch_shift(l)
+        for f in range(5):
+            todo.append((sx, (f, l + 2), tx[f, l] + C * normal_own(f, k, eta)))
+            dn, dg = d_normal(plane_at(f2zw, f), kz), d_normal(plane_at(gzw, f), kz)
+            edge = edges(pltpu.roll(ptz[f, half], shift, 1))
+            todo.append((sz, (f, l), tz[f, l] + C * (ihz * (eta * dg - dn) - edge)))
+        return todo
+
+    def inner(l):
+        half, shift, todo = l >> 3, patch_shift(l), []
+        for f in range(5):
+            todo.append((sx, (f, l + 2), tx[f, l] + w0 * bx[f, l]))
+            edge = edges(pltpu.roll(ptz[f, half], shift, 1))
+            todo.append((sz, (f, l), (tz[f, l] + w0z * bz[f, l]) + (hxz * ez[f, l] - C * edge)))
+        return todo
+
+    batches(0, 4, 2, ghost_layer)
+    batches(0, 4, 2, outer)
+    batches(2, 12, 4, inner)
     for f in range(5):
         for k in range(2):
             sx[f, k] = jnp.where(bottom, MIRROR[f] * sx[f, 3 - k], sx[f, k])
@@ -449,22 +541,22 @@
         a1, a2, a3, g = fluxes([sx[f, l + 2] for f in range(5)], move=(hx1, hz1, w1))
         todo = []
         for f in range(5):
-            todo += [(r, (f, l + 4), x[f]) for r, x in ((f1x, a1), (f2x, a2), (gx, g))]
-            todo += [(f3, (f, l + 4, slice(16, 24)), a3[f])]
+            todo += [(r, (f, l + 2), x[f]) for r, x in ((f1x, a1), (f2x, a2), (gx, g))]
+            todo += [(f3, (f, l + 2, slice(16, 24)), a3[f])]
         return todo
 
     def halo_flux_two(l):
         (a3,) = fluxes([sz[f, l] for f in range(5)], (3,))
-        return [x for f in range(5) for x in put_halo(f, l + 4, a3[f])]
+        return [x for f in range(5) for x in put_halo(f3, f, l + 2, a3[f])]
 
     def final(l):
         eta, shift, todo = eta_of(l), patch_shift(l), []
         for f in range(5):
-            dx = d_ends(f1x[f, l + 4], pltpu.roll(pt[f, l >> 3], shift, 1))
-            da = d_around(f, l + 4)
-            dn, dg = d_normal(f2x, f, l + 4), d_normal(gx, f, l + 4)
+            dx = d_ends(f1x[f, l + 2], pltpu.roll(pt[f, l >> 3], shift, 1))
+            da = d_around(f3, f, l + 2)
+            dn, dg = d_normal(plane_at(f2x, f), l + 2), d_normal(plane_at(gx, f), l + 2)
             rate = ih1 * (eta * dg - dn) - (dx + da)
-            todo.append((out, (f, l), 0.5 * (qx[f, l + 4] + sx[f, l + 2] + C * rate)))
+            todo.append((out, (f, l), 0.5 * (q[f, l] + sx[f, l + 2] + C * rate)))
         return todo
 
     batches(-2, 20, 4, own_flux_two)
@@ -502,6 +594,10 @@
 
 def stage_far(*refs):
     pack_far(lax.axis_index("wn"), *refs)
+
+
+def stage_prepare(*refs):
+    prepare(lax.axis_index("wn"), *refs)
 
 
 def stage_advance(*refs):
@@ -539,16 +635,23 @@
     s2 = lax.ppermute(two, "sx", swaps(tiles, 1, False))
     s1 = lax.ppermute(one, "sx", swaps(tiles, 0, False))
     (far,) = call(stage_far, (far, w, near), [(31, *plane)])
+    parts = call(
+        stage_prepare,
+        (own[0], own[1], halo, strips, far),
+        [(5, NL, *plane)] * 5,
+        [(5, NL, *plane)] * 6 + [(5, NL, 40, 128), (5, 2, *plane)],
+    )
     far = lax.ppermute(far, "wn", [(1, 2), (2, 1), (3, 0)])
     return call(
         stage_advance,
-        (*own, halo, strips, w, near, far, z_right, z_left, s1, s2),
-        [(5, NL, 8, 128), (8, 128)],
-        [(5, 24, 8, 128), (5, 20, 8, 128)]
-        + [(5, 24, 8, 128)] * 3
-        + [(5, 20, 8, 128)] * 3
-        + [(5, 24, 40, 128)]
-        + [(5, 20, 8, 128), (5, NL, 8, 128), (5, 3, 8, 128), (5, 2, 8, 128), (UNITS, 8, 128)],
+        (*own, halo, strips, w, near, far, z_right, z_left, s1, s2, *parts),
+        [(5, NL, *plane), plane],
+        [(5, 16, *plane), (5, 12, *plane)]
+        + [(5, 16, *plane)] * 3
+        + [(5, 12, *plane)] * 2
+        + [(5, 20, *plane)] * 3
+        + [(5, 20, 40, 128)]
+        + [(5, 20, *plane), (5, NL, *plane), (5, 3, *plane), (5, 2, *plane), (UNITS, *plane)],
     )
 
 

time: 47.6 us -> 47.3 us (level)
  the two profiles are of different devices: /device:TPU:33 before, /device:TPU:25 now
where the time goes in v5:
time: 47.3 us; the launch traced here: 47 us
  starting transfers between devices  36.4 us (77%)
  Pallas kernels  7.81 us (17%)
  waiting for transfers between devices  2.03 us (4%)
  between operations  0.75 us (2%)
    ppermute x1, starting transfers between devices, per_device(): a2 = lax.ppermute(two, 'az', swaps(around, 1, True))  10.6 us
    ppermute x2, starting transfers between devices, per_device(): s2 = lax.ppermute(two, 'sx', swaps(tiles, 1, False))  9.21 us
    pallas_call x6, Pallas kernels, call(): pl.pallas_call(body, out_shape=shapes, in_specs=[space] * len(ins), out_s...  7.81 us
    ppermute x1, starting transfers between devices, per_device(): far = lax.ppermute(far, 'wn', [(1, 2), (2, 1), (3, 0)])  4.9 us
    ppermute x1, starting transfers between devices, per_device(): near = lax.ppermute(near, 'wn', [(0, 1), (1, 0), (2, 3), (3, 2)])  4.5 us
    ppermute x2, starting transfers between devices, per_device(): s1 = lax.ppermute(one, 'sx', swaps(tiles, 0, False))  4.06 us
    ppermute x1, starting transfers between devices, per_device(): a1 = lax.ppermute(one, 'az', swaps(around, 0, True))  3.12 us
    ppermute x2, waiting for transfers between devices, per_device(): s2 = lax.ppermute(two, 'sx', swaps(tiles, 1, False))  1.06 us
  transfers between devices with their start and end apart: 8, of which 2 were waited for; matrix products, arithmetic and copies ran while one was open for 0% of the time, Pallas kernels for 5%

profile of v5, /device:TPU:25, one launch (start us, length us, event | category | flops | bytes accessed | tf_op | source)
XLA Modules:
  0.0 47.0 jit_solution(16743166742533437377)
XLA Ops:
  0.6 1.0 %shard_map.50 = (f32[5,16,8,128]{3,2,1,0:T(8,128)S(1)}, f32[8,128]{1,0:T(8,128)S(1)}, f32[5,8,128]{2,1,0:T(8,128)S(1)}, f32[43,8,128]{2,1,0:T(8,128)S(1)}, f32[43,8,128]{2,1,0:T(8,128)S(1)}) custom-call(f32[5,16,8,128]{3,2,1,0:T(8,128)} %refs_0_.1, f32[8,128]{1,0:T(8,128)} %refs_1_.1, f32[5,8,128]{2,1,0:T(8,128)} %refs_2_.1), custom_call_target="tpu_custom_call" | custom-call | tf_op jit(solution)/shard_map/pallas_call | solution.py:569
  1.7 3.1 %collective-permute-start = (f32[43,8,128]{2,1,0:T(8,128)S(1)}, f32[43,8,128]{2,1,0:T(8,128)S(1)}, u32[]{:S(2)}, u32[]{:S(2)}) collective-permute-start(f32[43,8,128]{2,1,0:T(8,128)S(1)} %get-tuple-element.28), channel_id=1, source_target_pairs={{0,1},{2,3},{4,5},{6,7},{8,9},{10,11},{12,13},{14,15},{1,0},{3,2},... | collective-permute-start | bytes 528392 | tf_op jit(solution)/shard_map/ppermute | solution.py:624
  4.8 10.6 %collective-permute-start.1 = (f32[43,8,128]{2,1,0:T(8,128)S(1)}, f32[43,8,128]{2,1,0:T(8,128)S(1)}, u32[]{:S(2)}, u32[]{:S(2)}) collective-permute-start(f32[43,8,128]{2,1,0:T(8,128)S(1)} %get-tuple-element.29), channel_id=1, source_target_pairs={{1,2},{3,4},{5,6},{7,8},{9,10},{11,12},{13,14},{15,0},{2,1},{4,3},... | collective-permute-start | bytes 528392 | tf_op jit(solution)/shard_map/ppermute | solution.py:623
  15.4 0.2 shard_map.51
  15.7 2.1 %collective-permute-start.2 = (f32[3,8,128]{2,1,0:T(8,128)S(1)}, f32[3,8,128]{2,1,0:T(8,128)S(1)}, u32[]{:S(2)}, u32[]{:S(2)}) collective-permute-start(f32[3,8,128]{2,1,0:T(8,128)S(1)} %get-tuple-element.32), channel_id=1, source_target_pairs={{0,16},{32,48},{64,80},{96,112},{16,0},{48,32},{80,64},{112,96},{1... | collective-permute-start | bytes 36872 | tf_op jit(solution)/shard_map/ppermute | solution.py:627
  17.7 4.6 %collective-permute-start.3 = (f32[3,8,128]{2,1,0:T(8,128)S(1)}, f32[3,8,128]{2,1,0:T(8,128)S(1)}, u32[]{:S(2)}, u32[]{:S(2)}) collective-permute-start(f32[3,8,128]{2,1,0:T(8,128)S(1)} %get-tuple-element.33), channel_id=1, source_target_pairs={{16,32},{48,64},{80,96},{32,16},{64,48},{96,80},{17,33},{49,65},{8... | collective-permute-start | bytes 36872 | tf_op jit(solution)/shard_map/ppermute | solution.py:626
  22.4 0.0 collective-permute-done.2.refs_7_
  22.4 1.1 %collective-permute-done.3.refs_8_ = f32[3,8,128]{2,1,0:T(8,128)S(1)} collective-permute-done((f32[3,8,128]{2,1,0:T(8,128)S(1)}, f32[3,8,128]{2,1,0:T(8,128)S(1)}, u32[]{:S(2)}, u32[]{:S(2)}) %collective-permute-start.3) | collective-permute-done | bytes 12320 | tf_op jit(solution)/shard_map/ppermute | solution.py:626
  23.5 0.0 collective-permute-done.refs_3_
  23.5 0.0 collective-permute-done.1.refs_4_
  23.5 0.5 %shard_map.52 = (f32[86,8,128]{2,1,0:T(8,128)S(1)}, f32[11,8,128]{2,1,0:T(8,128)S(1)}, f32[4,8,128]{2,1,0:T(8,128)S(1)}, f32[31,8,128]{2,1,0:T(8,128)S(1)}, f32[...) custom-call(f32[5,16,8,128]{3,2,1,0:T(8,128)S(1)} %get-tuple-element, ...), custom_call_target="tpu_custom_call" | custom-call | tf_op jit(solution)/shard_map/pallas_call | solution.py:569
  24.0 4.5 %collective-permute-start.4 = (f32[31,8,128]{2,1,0:T(8,128)S(1)}, f32[31,8,128]{2,1,0:T(8,128)S(1)}, u32[]{:S(2)}, u32[]{:S(2)}) collective-permute-start(f32[31,8,128]{2,1,0:T(8,128)S(1)} %get-tuple-element.37), channel_id=1, source_target_pairs={{0,128},{128,0},{256,384},{384,256},{1,129},{129,1},{257,385},{385... | collective-permute-start | bytes 380936 | tf_op jit(solution)/shard_map/ppermute | solution.py:634
  28.5 1.0 %collective-permute-done.4.refs_2_.refs_6_ = f32[31,8,128]{2,1,0:T(8,128)S(1)} collective-permute-done((f32[31,8,128]{2,1,0:T(8,128)S(1)}, f32[31,8,128]{2,1,0:T(8,128)S(1)}, u32[]{:S(2)}, u32[]{:S(2)}) %collective-permute-start.4) | collective-permute-done | bytes 127008 | tf_op jit(solution)/shard_map/ppermute | solution.py:634
  29.5 4.9 %collective-permute-start.5 = (f32[31,8,128]{2,1,0:T(8,128)S(1)}, f32[31,8,128]{2,1,0:T(8,128)S(1)}, u32[]{:S(2)}, u32[]{:S(2)}) collective-permute-start(f32[31,8,128]{2,1,0:T(8,128)S(1)} %shard_map.53.refs_4_), channel_id=1, source_target_pairs={{128,256},{256,128},{384,0},{129,257},{257,129},{385,1},{130,258},... | collective-permute-start | bytes 380936 | tf_op jit(solution)/shard_map/ppermute | solution.py:644
  34.4 2.0 %collective-permute-start.6 = (f32[3,8,128]{2,1,0:T(8,128)S(1)}, f32[3,8,128]{2,1,0:T(8,128)S(1)}, u32[]{:S(2)}, u32[]{:S(2)}) collective-permute-start(f32[3,8,128]{2,1,0:T(8,128)S(1)} %get-tuple-element.41), channel_id=1, source_target_pairs={{0,16},{32,48},{64,80},{96,112},{16,0},{48,32},{80,64},{112,96},{1... | collective-permute-start | bytes 36872 | tf_op jit(solution)/shard_map/ppermute | solution.py:636
  36.4 4.6 %collective-permute-start.7 = (f32[3,8,128]{2,1,0:T(8,128)S(1)}, f32[3,8,128]{2,1,0:T(8,128)S(1)}, u32[]{:S(2)}, u32[]{:S(2)}) collective-permute-start(f32[3,8,128]{2,1,0:T(8,128)S(1)} %get-tuple-element.42), channel_id=1, source_target_pairs={{16,32},{48,64},{80,96},{32,16},{64,48},{96,80},{17,33},{49,65},{8... | collective-permute-start | bytes 36872 | tf_op jit(solution)/shard_map/ppermute | solution.py:635
  41.0 2.0 %shard_map.54 = (f32[5,16,8,128]{3,2,1,0:T(8,128)S(1)}, f32[5,16,8,128]{3,2,1,0:T(8,128)S(1)}, f32[5,16,8,128]{3,2,1,0:T(8,128)S(1)}, f32[5,16,8,128]{3,2,1,0:T(8,128)S(1)}, f32[5,16,8,128]{3,2,1,0:T(8,128)S(1)}) custom-call(f32[5,16,8,128]{3,2,1,0:T(8,128)S(1)} %get-tuple-element.25.refs_0_, f32[8,128]{1,0:T(8,128)S(1)} %get-tuple-element.26.refs_1_, ...), custom_call_target="tpu_custom_call" | custom-call | tf_op jit(solution)/shard_map/pallas_call | solution.py:569
  43.0 0.0 collective-permute-done.6.refs_10_
  43.0 0.0 collective-permute-done.7.refs_11_
  43.0 0.0 collective-permute-done.5.refs_7_
  43.0 4.0 %shard_map.55 = (f32[5,16,8,128]{3,2,1,0:T(8,128)}, f32[8,128]{1,0:T(8,128)}) custom-call(f32[5,16,8,128]{3,2,1,0:T(8,128)S(1)} %get-tuple-element.25.refs_0_, f32[8,128]{1,0:T(8,128)S(1)} %get-tuple-element.26.refs_1_, f32[5,8,128]{2,1,0:T(8,128)S(1)} %get-tuple-element.27.refs_2_, f32[86,8,128]{2,1,0:T(8,128)S(1)} %get-tuple-element.34.refs_2_.refs_3_, ...), custom_call_target="tpu_custom_call" | custom-call | tf_op jit(solution)/shard_map/pallas_call | solution.py:569
  (1 shorter events, 0.0 us)
Async XLA Ops:
  1.7 21.8 %collective-permute-start = (f32[43,8,128]{2,1,0:T(8,128)S(1)}, f32[43,8,128]{2,1,0:T(8,128)S(1)}, u32[]{:S(2)}, u32[]{:S(2)}) collective-permute-start(f32[43,8,128]{2,1,0:T(8,128)S(1)} %get-tuple-element.28), channel_id=1, source_target_pairs={{0,1},{2,3},{4,5},{6,7},{8,9},{10,11},{12,13},{14,15},{1,0},{3,2},... | collective-permute-start | bytes 528392 | tf_op jit(solution)/shard_map/ppermute | solution.py:624
  4.8 18.7 %collective-permute-start.1 = (f32[43,8,128]{2,1,0:T(8,128)S(1)}, f32[43,8,128]{2,1,0:T(8,128)S(1)}, u32[]{:S(2)}, u32[]{:S(2)}) collective-permute-start(f32[43,8,128]{2,1,0:T(8,128)S(1)} %get-tuple-element.29), channel_id=1, source_target_pairs={{1,2},{3,4},{5,6},{7,8},{9,10},{11,12},{13,14},{15,0},{2,1},{4,3},... | collective-permute-start | bytes 528392 | tf_op jit(solution)/shard_map/ppermute | solution.py:623
  15.7 6.7 %collective-permute-start.2 = (f32[3,8,128]{2,1,0:T(8,128)S(1)}, f32[3,8,128]{2,1,0:T(8,128)S(1)}, u32[]{:S(2)}, u32[]{:S(2)}) collective-permute-start(f32[3,8,128]{2,1,0:T(8,128)S(1)} %get-tuple-element.32), channel_id=1, source_target_pairs={{0,16},{32,48},{64,80},{96,112},{16,0},{48,32},{80,64},{112,96},{1... | collective-permute-start | bytes 36872 | tf_op jit(solution)/shard_map/ppermute | solution.py:627
  17.7 5.7 %collective-permute-start.3 = (f32[3,8,128]{2,1,0:T(8,128)S(1)}, f32[3,8,128]{2,1,0:T(8,128)S(1)}, u32[]{:S(2)}, u32[]{:S(2)}) collective-permute-start(f32[3,8,128]{2,1,0:T(8,128)S(1)} %get-tuple-element.33), channel_id=1, source_target_pairs={{16,32},{48,64},{80,96},{32,16},{64,48},{96,80},{17,33},{49,65},{8... | collective-permute-start | bytes 36872 | tf_op jit(solution)/shard_map/ppermute | solution.py:626
  24.0 5.5 %collective-permute-start.4 = (f32[31,8,128]{2,1,0:T(8,128)S(1)}, f32[31,8,128]{2,1,0:T(8,128)S(1)}, u32[]{:S(2)}, u32[]{:S(2)}) collective-permute-start(f32[31,8,128]{2,1,0:T(8,128)S(1)} %get-tuple-element.37), channel_id=1, source_target_pairs={{0,128},{128,0},{256,384},{384,256},{1,129},{129,1},{257,385},{385... | collective-permute-start | bytes 380936 | tf_op jit(solution)/shard_map/ppermute | solution.py:634
  29.5 13.5 %collective-permute-start.5 = (f32[31,8,128]{2,1,0:T(8,128)S(1)}, f32[31,8,128]{2,1,0:T(8,128)S(1)}, u32[]{:S(2)}, u32[]{:S(2)}) collective-permute-start(f32[31,8,128]{2,1,0:T(8,128)S(1)} %shard_map.53.refs_4_), channel_id=1, source_target_pairs={{128,256},{256,128},{384,0},{129,257},{257,129},{385,1},{130,258},... | collective-permute-start | bytes 380936 | tf_op jit(solution)/shard_map/ppermute | solution.py:644
  34.4 8.6 %collective-permute-start.6 = (f32[3,8,128]{2,1,0:T(8,128)S(1)}, f32[3,8,128]{2,1,0:T(8,128)S(1)}, u32[]{:S(2)}, u32[]{:S(2)}) collective-permute-start(f32[3,8,128]{2,1,0:T(8,128)S(1)} %get-tuple-element.41), channel_id=1, source_target_pairs={{0,16},{32,48},{64,80},{96,112},{16,0},{48,32},{80,64},{112,96},{1... | collective-permute-start | bytes 36872 | tf_op jit(solution)/shard_map/ppermute | solution.py:636
  36.4 6.6 %collective-permute-start.7 = (f32[3,8,128]{2,1,0:T(8,128)S(1)}, f32[3,8,128]{2,1,0:T(8,128)S(1)}, u32[]{:S(2)}, u32[]{:S(2)}) collective-permute-start(f32[3,8,128]{2,1,0:T(8,128)S(1)} %get-tuple-element.42), channel_id=1, source_target_pairs={{16,32},{48,64},{80,96},{32,16},{64,48},{96,80},{17,33},{49,65},{8... | collective-permute-start | bytes 36872 | tf_op jit(solution)/shard_map/ppermute | solution.py:635

commit v6 on v5

--- a/solution.py
+++ b/solution.py
@@ -18,6 +18,7 @@
 STEP = CFL_STEP / LAYERS
 C = CFL_STEP / 12.0
 VM = pl.BlockSpec(memory_space=pltpu.VMEM)
+HBM = pl.BlockSpec(memory_space=pltpu.HBM)
 F32 = jnp.float32
 MIRROR = (1.0, -1.0, -1.0, -1.0, 1.0)
 
@@ -197,8 +198,13 @@
     to_pairs(even, right, left, one, two)
 
 
-def pack_second(odd, wn, tile, tiles, q, h, b, a1, a2, right, left, s1, s2, *outs):
-    z, strips, w, near, far, z_right, z_left, z_one, z_two, hi, lo = outs
+def pack_corners(even, z, right, left, one, two):
+    columns(lambda i: z[i], right, left)
+    to_pairs(even, right, left, one, two)
+
+
+def pack_second(odd, wn, tile, tiles, q, h, b, a1, a2, right, left, s1, s2, _parts, *outs):
+    z, strips, w, near, far, hi, lo = outs
     ln, rw = lane(), row()
     mask = (rw >= 4) ^ odd
     for i in range(HALF):
@@ -254,11 +260,9 @@
     for i in range(27):
         near[i] = jnp.where(wn % 2 == 0, hi[i], lo[i])
         far[i] = jnp.where(wn == 1, hi[i], lo[i])
-    columns(lambda i: z[i], z_right, z_left)
-    to_pairs(tile % 2 == 0, z_right, z_left, z_one, z_two)
-
-
-def pack_far(wn, far, w, near, out):
+
+
+def pack_far(wn, far, w, near, _corners, out):
     for i in range(27):
         out[i] = far[i]
     for k in range(4):
@@ -298,19 +302,35 @@
     return patched(jnp.zeros_like(patch), patch)
 
 
-def batches(first_l, count, size, body):
+def batches(first_l, count, size, body, after=None):
     def step(i, _):
         todo = []
         for k in range(size):
             todo += body(first_l + i * size + k)
         for ref, at, x in todo:
             ref[at] = x
+        if after is not None:
+            after(i)
         return 0
 
     lax.fori_loop(0, count // size, step, 0)
 
 
-def prepare(wn, q, h, z, strips, _far, tx, bx, tz, bz, ez, f1x, f2x, gx, f1z, f2z, gz, f3, pt):
+def own_parts(q, _right, f1, f3, d1, dn, dq, f2):
+    def flux(l):
+        a1, a2, a3 = fluxes([q[f, l] for f in range(5)])
+        return [(r, (f, l), x[f]) for f in range(5) for r, x in ((f1, a1), (f2, a2), (f3, a3), (d1, [d_lane(y) for y in a1]))]
+
+    def inner(l):
+        return [
+            (r, (f, l), d_normal(plane_at(x, f), l)) for f in range(5) for r, x in ((dn, f2), (dq, q))
+        ]
+
+    batches(0, NL, 4, flux)
+    batches(2, 12, 4, inner)
+
+
+def prepare(wn, q, h, z, strips, f1x, f3x, d1x, dnx, dqx, _far, tx, bx, tz, bz, ez, gx, f1z, f2z, gz, f3, pt):
     h0, h0z = h[...], z[80]
     hx = SCALE * patched(d_lane(h0), rl(strip_patch(d_lane(spread(strips[10], 0))), -12))
     hz, hzz = (SCALE * x for x in d_ring(h0, h0z))
@@ -321,12 +341,11 @@
         for f in range(5):
             pt[f, v] = strip_patch(d_lane(a1[f]))
 
-    def own_flux(l):
-        a1, a2, a3, g = fluxes([q[f, l] for f in range(5)], move=(hx, hz, 0.0))
+    def own_moving(l):
         todo = []
         for f in range(5):
-            todo += [(r, (f, l), x[f]) for r, x in ((f1x, a1), (f2x, a2), (gx, g))]
-            todo += [(f3, (f, l, slice(16, 24)), a3[f])]
+            a = f3x[f, l]
+            todo += [(gx, (f, l), hx * f1x[f, l] + hz * a), (f3, (f, l, slice(16, 24)), a)]
         return todo
 
     def halo_flux(l):
@@ -337,11 +356,11 @@
             todo += put_halo(f3, f, l, a3[f])
         return todo
 
-    batches(0, NL, 4, own_flux)
+    batches(0, NL, 4, own_moving)
     batches(0, NL, 4, halo_flux)
 
     def own_surface(f, l):
-        dx = patched(d_lane(f1x[f, l]), pltpu.roll(pt[f, l >> 3], patch_shift(l), 1))
+        dx = patched(d1x[f, l], pltpu.roll(pt[f, l >> 3], patch_shift(l), 1))
         return q[f, l] - C * (dx + d_around(f3, f, l))
 
     def halo_surface(f, l):
@@ -352,8 +371,8 @@
     def own_inner(l):
         k, todo = ih * (((base + l).astype(F32) + 0.5) / LAYERS), []
         for f in range(5):
-            t = own_surface(f, l) + (k * d_normal(plane_at(gx, f), l) - ih * d_normal(plane_at(f2x, f), l))
-            todo += [(tx, (f, l), t), (bx, (f, l), k * d_normal(plane_at(q, f), l))]
+            t = own_surface(f, l) + (k * d_normal(plane_at(gx, f), l) - ih * dnx[f, l])
+            todo += [(tx, (f, l), t), (bx, (f, l), k * dqx[f, l])]
         return todo
 
     def halo_inner(l):
@@ -376,7 +395,7 @@
 
 
 def advance(wn, tile, tiles, q, h, b, z, strips, w, near, far, z_right, z_left, z_one, z_two, tx, bx, tz, bz, ez, *rest):
-    out, h_out, qw, zw, f1w, f2w, gw, f2zw, gzw, f1x, f2x, gx, f3, sx, sz, pt, ptz, zst = rest
+    out_hbm, h_hbm, qw, zw, f1w, f2w, gw, f2zw, gzw, f1x, f2x, gx, f3, sx, sz, pt, ptz, zst, out, h_out, sems = rest
     first, last = tile == 0, tile == tiles - 1
 
     def put_strip(u, x):
@@ -480,13 +499,15 @@
         return ((base + l).astype(F32) + 0.5) / LAYERS
 
     batches(0, 16, 4, own_flux)
-    for k in range(12):
+
+    def halo_flux(k):
         a2, a3, g = fluxes([zw[f, k] for f in range(5)], (2, 3), move=(hxz, hzz, w0z))
-        for f in range(5):
-            f2zw[f, k], gzw[f, k] = a2[f], g[f]
-            if k in (0, 1, 10, 11):
-                for ref, at, x in put_halo(f3, f, k + 2, a3[f]):
-                    ref[at] = x
+        todo = []
+        for f in range(5):
+            todo += [(r, (f, k), x[f]) for r, x in ((f2zw, a2), (gzw, g))] + put_halo(f3, f, k + 2, a3[f])
+        return todo
+
+    batches(0, 12, 4, halo_flux)
 
     def normal_own(f, k, eta):
         return ih * (eta * d_normal(plane_at(gw, f), k) - d_normal(plane_at(f2w, f), k))
@@ -532,6 +553,8 @@
     hz1 = SCALE * d_ring(h1, h1z)[0]
     ih1 = 1.0 / h1
     h_out[...] = 0.5 * (h0 + h1 + STEP * w1)
+    h_copy = pltpu.make_async_copy(h_out, h_hbm, sems.at[4])
+    h_copy.start()
     for v in range(2):
         (a1,) = fluxes(strip_s[v], (1,))
         for f in range(5):
@@ -561,16 +584,24 @@
 
     batches(-2, 20, 4, own_flux_two)
     batches(0, NL, 4, halo_flux_two)
-    batches(0, NL, 4, final)
-
-
-def call(body, ins, outs, scratch=(), sems=0, space=VM):
+
+    def out_copy(i):
+        part = (slice(None), pl.ds(4 * i, 4))
+        return pltpu.make_async_copy(out.at[part], out_hbm.at[part], sems.at[i])
+
+    batches(0, NL, 4, final, lambda i: out_copy(i).start())
+    for i in range(4):
+        out_copy(i).wait()
+    h_copy.wait()
+
+
+def call(body, ins, outs, scratch=(), sems=0, space=VM, out_space=VM):
     shapes = tuple(jax.ShapeDtypeStruct(s, F32) for s in outs)
     return pl.pallas_call(
         body,
         out_shape=shapes,
         in_specs=[space] * len(ins),
-        out_specs=tuple([VM] * len(shapes)),
+        out_specs=tuple([out_space] * len(shapes)),
         scratch_shapes=[pltpu.VMEM(s, F32) for s in scratch] + [pltpu.SemaphoreType.DMA((sems,))] * (sems > 0),
         compiler_params=pltpu.CompilerParams(vmem_limit_bytes=40 * 1024 * 1024),
     )(*ins)
@@ -584,8 +615,16 @@
     pack_rows(lax.axis_index("az") % 2 == 1, *refs)
 
 
+def stage_own(*refs):
+    own_parts(*refs)
+
+
 def stage_columns(*refs):
     pack_columns(lax.axis_index("sx") % 2 == 0, *refs)
+
+
+def stage_corners(*refs):
+    pack_corners(lax.axis_index("sx") % 2 == 0, *refs)
 
 
 def stage_second(*refs):
@@ -618,28 +657,30 @@
         [pltpu.with_memory_space_constraint(x, pltpu.HBM) for x in (fields, height, behind)],
         [fields.shape, height.shape, behind.shape] + [(HALF, *plane)] * 2,
         sems=3,
-        space=pl.BlockSpec(memory_space=pltpu.HBM),
+        space=HBM,
     )
     a2 = lax.ppermute(two, "az", swaps(around, 1, True))
     a1 = lax.ppermute(one, "az", swaps(around, 0, True))
     right, left, one, two = call(stage_columns, own, [(3, *plane)] * 4)
     s2 = lax.ppermute(two, "sx", swaps(tiles, 1, False))
     s1 = lax.ppermute(one, "sx", swaps(tiles, 0, False))
-    halo, strips, w, near, far, z_right, z_left, one, two = call(
+    parts = call(stage_own, (own[0], right), [(5, NL, *plane)] * 5, [(5, NL, *plane)])
+    halo, strips, w, near, far = call(
         stage_second,
-        (*own, a1, a2, right, left, s1, s2),
-        [(NP, *plane), (UNITS, *plane), (4, *plane), (31, *plane), (27, *plane)] + [(3, *plane)] * 4,
+        (*own, a1, a2, right, left, s1, s2, parts[3]),
+        [(NP, *plane), (UNITS, *plane), (4, *plane), (31, *plane), (27, *plane)],
         [(27, *plane)] * 2,
     )
+    z_right, z_left, one, two = call(stage_corners, (halo,), [(3, *plane)] * 4)
     near = lax.ppermute(near, "wn", [(0, 1), (1, 0), (2, 3), (3, 2)])
     s2 = lax.ppermute(two, "sx", swaps(tiles, 1, False))
     s1 = lax.ppermute(one, "sx", swaps(tiles, 0, False))
-    (far,) = call(stage_far, (far, w, near), [(31, *plane)])
+    (far,) = call(stage_far, (far, w, near, two), [(31, *plane)])
     parts = call(
         stage_prepare,
-        (own[0], own[1], halo, strips, far),
+        (own[0], own[1], halo, strips, *parts, far),
         [(5, NL, *plane)] * 5,
-        [(5, NL, *plane)] * 6 + [(5, NL, 40, 128), (5, 2, *plane)],
+        [(5, NL, *plane)] * 4 + [(5, NL, 40, 128), (5, 2, *plane)],
     )
     far = lax.ppermute(far, "wn", [(1, 2), (2, 1), (3, 0)])
     return call(
@@ -651,7 +692,9 @@
         + [(5, 12, *plane)] * 2
         + [(5, 20, *plane)] * 3
         + [(5, 20, 40, 128)]
-        + [(5, 20, *plane), (5, NL, *plane), (5, 3, *plane), (5, 2, *plane), (UNITS, *plane)],
+        + [(5, 20, *plane), (5, NL, *plane), (5, 3, *plane), (5, 2, *plane), (UNITS, *plane), (5, NL, *plane), plane],
+        sems=5,
+        out_space=HBM,
     )
 
 

time: 47.3 us -> 46.9 us (level)
  waiting for transfers between devices: 2.03 us -> 1.07 us
  Pallas kernels: 7.81 us -> 8.36 us
    ppermute x2, waiting for transfers between devices: 1.06 us -> 0.32 us  [per_device(): s2 = lax.ppermute(two, 'sx', swaps(tiles, 1, False))]
    pallas_call x6 -> x8, Pallas kernels: 7.81 us -> 8.36 us  [call(): pl.pallas_call(body, out_shape=shapes, in_specs=[space] * len(ins), out_s...]
  transfers between devices with their start and end apart: 8 -> 8, of which waited for: 2 -> 2; matrix products, arithmetic and copies ran while one was open for 0% -> 0% of each run, Pallas kernels for 5% -> 6%
where the time goes in v6:
time: 46.9 us; the launch traced here: 46.6 us
  starting transfers between devices  36.4 us (78%)
  Pallas kernels  8.36 us (18%)
  waiting for transfers between devices  1.07 us (2%)
  between operations  0.75 us (2%)
    ppermute x1, starting transfers between devices, per_device(): a2 = lax.ppermute(two, 'az', swaps(around, 1, True))  10.6 us
    ppermute x2, starting transfers between devices, per_device(): s2 = lax.ppermute(two, 'sx', swaps(tiles, 1, False))  9.21 us
    pallas_call x8, Pallas kernels, call(): pl.pallas_call(body, out_shape=shapes, in_specs=[space] * len(ins), out_s...  8.36 us
    ppermute x1, starting transfers between devices, per_device(): far = lax.ppermute(far, 'wn', [(1, 2), (2, 1), (3, 0)])  4.9 us
    ppermute x1, starting transfers between devices, per_device(): near = lax.ppermute(near, 'wn', [(0, 1), (1, 0), (2, 3), (3, 2)])  4.5 us
    ppermute x2, starting transfers between devices, per_device(): s1 = lax.ppermute(one, 'sx', swaps(tiles, 0, False))  4.06 us
    ppermute x1, starting transfers between devices, per_device(): a1 = lax.ppermute(one, 'az', swaps(around, 0, True))  3.12 us
  transfers between devices with their start and end apart: 8, of which 2 were waited for; matrix products, arithmetic and copies ran while one was open for 0% of the time, Pallas kernels for 6%

profile of v6, /device:TPU:25, one launch (start us, length us, event | category | flops | bytes accessed | tf_op | source)
XLA Modules:
  0.0 46.6 jit_solution(7897418610989209505)
XLA Ops:
  0.6 1.0 %shard_map.50 = (f32[5,16,8,128]{3,2,1,0:T(8,128)S(1)}, f32[8,128]{1,0:T(8,128)S(1)}, f32[5,8,128]{2,1,0:T(8,128)S(1)}, f32[43,8,128]{2,1,0:T(8,128)S(1)}, f32[43,8,128]{2,1,0:T(8,128)S(1)}) custom-call(f32[5,16,8,128]{3,2,1,0:T(8,128)} %refs_0_.1, f32[8,128]{1,0:T(8,128)} %refs_1_.1, f32[5,8,128]{2,1,0:T(8,128)} %refs_2_.1), custom_call_target="tpu_custom_call" | custom-call | tf_op jit(solution)/shard_map/pallas_call | solution.py:600
  1.7 3.1 %collective-permute-start = (f32[43,8,128]{2,1,0:T(8,128)S(1)}, f32[43,8,128]{2,1,0:T(8,128)S(1)}, u32[]{:S(2)}, u32[]{:S(2)}) collective-permute-start(f32[43,8,128]{2,1,0:T(8,128)S(1)} %get-tuple-element.33), channel_id=1, source_target_pairs={{0,1},{2,3},{4,5},{6,7},{8,9},{10,11},{12,13},{14,15},{1,0},{3,2},... | collective-permute-start | bytes 528392 | tf_op jit(solution)/shard_map/ppermute | solution.py:663
  4.8 10.6 %collective-permute-start.1 = (f32[43,8,128]{2,1,0:T(8,128)S(1)}, f32[43,8,128]{2,1,0:T(8,128)S(1)}, u32[]{:S(2)}, u32[]{:S(2)}) collective-permute-start(f32[43,8,128]{2,1,0:T(8,128)S(1)} %get-tuple-element.34), channel_id=1, source_target_pairs={{1,2},{3,4},{5,6},{7,8},{9,10},{11,12},{13,14},{15,0},{2,1},{4,3},... | collective-permute-start | bytes 528392 | tf_op jit(solution)/shard_map/ppermute | solution.py:662
  15.4 0.2 shard_map.51
  15.7 2.1 %collective-permute-start.2 = (f32[3,8,128]{2,1,0:T(8,128)S(1)}, f32[3,8,128]{2,1,0:T(8,128)S(1)}, u32[]{:S(2)}, u32[]{:S(2)}) collective-permute-start(f32[3,8,128]{2,1,0:T(8,128)S(1)} %get-tuple-element.37), channel_id=1, source_target_pairs={{0,16},{32,48},{64,80},{96,112},{16,0},{48,32},{80,64},{112,96},{1... | collective-permute-start | bytes 36872 | tf_op jit(solution)/shard_map/ppermute | solution.py:666
  17.7 4.6 %collective-permute-start.3 = (f32[3,8,128]{2,1,0:T(8,128)S(1)}, f32[3,8,128]{2,1,0:T(8,128)S(1)}, u32[]{:S(2)}, u32[]{:S(2)}) collective-permute-start(f32[3,8,128]{2,1,0:T(8,128)S(1)} %get-tuple-element.38), channel_id=1, source_target_pairs={{16,32},{48,64},{80,96},{32,16},{64,48},{96,80},{17,33},{49,65},{8... | collective-permute-start | bytes 36872 | tf_op jit(solution)/shard_map/ppermute | solution.py:665
  22.4 0.7 %shard_map.52 = (f32[5,16,8,128]{3,2,1,0:T(8,128)S(1)}, f32[5,16,8,128]{3,2,1,0:T(8,128)S(1)}, f32[5,16,8,128]{3,2,1,0:T(8,128)S(1)}, f32[5,16,8,128]{3,2,1,0:T(8,128)S(1)}, f32[5,16,8,128]{3,2,1,0:T(8,128)S(1)}) custom-call(f32[5,16,8,128]{3,2,1,0:T(8,128)S(1)} %get-tuple-element.30.refs_0_, f32[3,8,128]{2,1,0:T(8,128)S(1)} %get-tuple-element.35.refs_1_.refs_5_), custom_call_target="tpu_custom_call" | custom-call | tf_op jit(solution)/shard_map/pallas_call | solution.py:600
  23.1 0.0 collective-permute-done.2.refs_7_
  23.1 0.3 collective-permute-done.3.refs_8_
  23.5 0.0 collective-permute-done.refs_3_
  23.5 0.0 collective-permute-done.1.refs_4_
  23.5 0.5 %shard_map.53 = (f32[86,8,128]{2,1,0:T(8,128)S(1)}, f32[11,8,128]{2,1,0:T(8,128)S(1)}, f32[4,8,128]{2,1,0:T(8,128)S(1)}, f32[31,8,128]{2,1,0:T(8,128)S(1)}, f32[27,8,128]{2,1,0:T(8,128)S(1)}) custom-call(f32[5,16,8,128]{3,2,1,0:T(8,128)S(1)} %get-tuple-element.30.refs_0_, f32[8,128]{1,0:T(8,128)S(1)} %get-tuple-element.31.refs_1_, ...), custom_call_target="tpu_custom_call" | custom-call | tf_op jit(solution)/shard_map/pallas_call | solution.py:600
  24.0 4.5 %collective-permute-start.4 = (f32[31,8,128]{2,1,0:T(8,128)S(1)}, f32[31,8,128]{2,1,0:T(8,128)S(1)}, u32[]{:S(2)}, u32[]{:S(2)}) collective-permute-start(f32[31,8,128]{2,1,0:T(8,128)S(1)} %get-tuple-element.43), channel_id=1, source_target_pairs={{0,128},{128,0},{256,384},{384,256},{1,129},{129,1},{257,385},{385... | collective-permute-start | bytes 380936 | tf_op jit(solution)/shard_map/ppermute | solution.py:675
  28.5 0.2 shard_map.54
  28.7 0.7 %collective-permute-done.4.refs_2_.refs_6_ = f32[31,8,128]{2,1,0:T(8,128)S(1)} collective-permute-done((f32[31,8,128]{2,1,0:T(8,128)S(1)}, f32[31,8,128]{2,1,0:T(8,128)S(1)}, u32[]{:S(2)}, u32[]{:S(2)}) %collective-permute-start.4) | collective-permute-done | bytes 127008 | tf_op jit(solution)/shard_map/ppermute | solution.py:675
  29.5 4.9 %collective-permute-start.5 = (f32[31,8,128]{2,1,0:T(8,128)S(1)}, f32[31,8,128]{2,1,0:T(8,128)S(1)}, u32[]{:S(2)}, u32[]{:S(2)}) collective-permute-start(f32[31,8,128]{2,1,0:T(8,128)S(1)} %shard_map.55.refs_9_), channel_id=1, source_target_pairs={{128,256},{256,128},{384,0},{129,257},{257,129},{385,1},{130,258},... | collective-permute-start | bytes 380936 | tf_op jit(solution)/shard_map/ppermute | solution.py:685
  34.4 2.0 %collective-permute-start.6 = (f32[3,8,128]{2,1,0:T(8,128)S(1)}, f32[3,8,128]{2,1,0:T(8,128)S(1)}, u32[]{:S(2)}, u32[]{:S(2)}) collective-permute-start(f32[3,8,128]{2,1,0:T(8,128)S(1)} %get-tuple-element.48), channel_id=1, source_target_pairs={{0,16},{32,48},{64,80},{96,112},{16,0},{48,32},{80,64},{112,96},{1... | collective-permute-start | bytes 36872 | tf_op jit(solution)/shard_map/ppermute | solution.py:677
  36.4 4.6 %collective-permute-start.7 = (f32[3,8,128]{2,1,0:T(8,128)S(1)}, f32[3,8,128]{2,1,0:T(8,128)S(1)}, u32[]{:S(2)}, u32[]{:S(2)}) collective-permute-start(f32[3,8,128]{2,1,0:T(8,128)S(1)} %get-tuple-element.45.refs_3_), channel_id=1, source_target_pairs={{16,32},{48,64},{80,96},{32,16},{64,48},{96,80},{17,33},{49,65},{8... | collective-permute-start | bytes 36872 | tf_op jit(solution)/shard_map/ppermute | solution.py:676
  41.0 1.6 %shard_map.56 = (f32[5,16,8,128]{3,2,1,0:T(8,128)S(1)}, f32[5,16,8,128]{3,2,1,0:T(8,128)S(1)}, f32[5,16,8,128]{3,2,1,0:T(8,128)S(1)}, f32[5,16,8,128]{3,2,1,0:T(8,128)S(1)}, f32[5,16,8,128]{3,2,1,0:T(8,128)S(1)}) custom-call(f32[5,16,8,128]{3,2,1,0:T(8,128)S(1)} %get-tuple-element.30.refs_0_, f32[8,128]{1,0:T(8,128)S(1)} %get-tuple-element.31.refs_1_, ...), custom_call_target="tpu_custom_call" | custom-call | tf_op jit(solution)/shard_map/pallas_call | solution.py:600
  42.6 0.0 collective-permute-done.6.refs_10_
  42.6 0.0 collective-permute-done.7.refs_11_
  42.6 0.0 collective-permute-done.5.refs_7_
  42.6 4.0 %shard_map.57 = (f32[5,16,8,128]{3,2,1,0:T(8,128)}, f32[8,128]{1,0:T(8,128)}) custom-call(f32[5,16,8,128]{3,2,1,0:T(8,128)S(1)} %get-tuple-element.30.refs_0_, f32[8,128]{1,0:T(8,128)S(1)} %get-tuple-element.31.refs_1_, f32[5,8,128]{2,1,0:T(8,128)S(1)} %get-tuple-element.32.refs_2_, f32[86,8,128]{2,1,0:T(8,128)S(1)} %get-tuple-element.40.refs_0_.refs_2_.refs_3_, ...), custom_call_target="tpu_custom_call" | custom-call | tf_op jit(solution)/shard_map/pallas_call | solution.py:600
  (1 shorter events, 0.0 us)
Async XLA Ops:
  1.7 21.8 %collective-permute-start = (f32[43,8,128]{2,1,0:T(8,128)S(1)}, f32[43,8,128]{2,1,0:T(8,128)S(1)}, u32[]{:S(2)}, u32[]{:S(2)}) collective-permute-start(f32[43,8,128]{2,1,0:T(8,128)S(1)} %get-tuple-element.33), channel_id=1, source_target_pairs={{0,1},{2,3},{4,5},{6,7},{8,9},{10,11},{12,13},{14,15},{1,0},{3,2},... | collective-permute-start | bytes 528392 | tf_op jit(solution)/shard_map/ppermute | solution.py:663
  4.8 18.7 %collective-permute-start.1 = (f32[43,8,128]{2,1,0:T(8,128)S(1)}, f32[43,8,128]{2,1,0:T(8,128)S(1)}, u32[]{:S(2)}, u32[]{:S(2)}) collective-permute-start(f32[43,8,128]{2,1,0:T(8,128)S(1)} %get-tuple-element.34), channel_id=1, source_target_pairs={{1,2},{3,4},{5,6},{7,8},{9,10},{11,12},{13,14},{15,0},{2,1},{4,3},... | collective-permute-start | bytes 528392 | tf_op jit(solution)/shard_map/ppermute | solution.py:662
  15.7 7.5 %collective-permute-start.2 = (f32[3,8,128]{2,1,0:T(8,128)S(1)}, f32[3,8,128]{2,1,0:T(8,128)S(1)}, u32[]{:S(2)}, u32[]{:S(2)}) collective-permute-start(f32[3,8,128]{2,1,0:T(8,128)S(1)} %get-tuple-element.37), channel_id=1, source_target_pairs={{0,16},{32,48},{64,80},{96,112},{16,0},{48,32},{80,64},{112,96},{1... | collective-permute-start | bytes 36872 | tf_op jit(solution)/shard_map/ppermute | solution.py:666
  17.7 5.7 %collective-permute-start.3 = (f32[3,8,128]{2,1,0:T(8,128)S(1)}, f32[3,8,128]{2,1,0:T(8,128)S(1)}, u32[]{:S(2)}, u32[]{:S(2)}) collective-permute-start(f32[3,8,128]{2,1,0:T(8,128)S(1)} %get-tuple-element.38), channel_id=1, source_target_pairs={{16,32},{48,64},{80,96},{32,16},{64,48},{96,80},{17,33},{49,65},{8... | collective-permute-start | bytes 36872 | tf_op jit(solution)/shard_map/ppermute | solution.py:665
  24.0 5.5 %collective-permute-start.4 = (f32[31,8,128]{2,1,0:T(8,128)S(1)}, f32[31,8,128]{2,1,0:T(8,128)S(1)}, u32[]{:S(2)}, u32[]{:S(2)}) collective-permute-start(f32[31,8,128]{2,1,0:T(8,128)S(1)} %get-tuple-element.43), channel_id=1, source_target_pairs={{0,128},{128,0},{256,384},{384,256},{1,129},{129,1},{257,385},{385... | collective-permute-start | bytes 380936 | tf_op jit(solution)/shard_map/ppermute | solution.py:675
  29.5 13.1 %collective-permute-start.5 = (f32[31,8,128]{2,1,0:T(8,128)S(1)}, f32[31,8,128]{2,1,0:T(8,128)S(1)}, u32[]{:S(2)}, u32[]{:S(2)}) collective-permute-start(f32[31,8,128]{2,1,0:T(8,128)S(1)} %shard_map.55.refs_9_), channel_id=1, source_target_pairs={{128,256},{256,128},{384,0},{129,257},{257,129},{385,1},{130,258},... | collective-permute-start | bytes 380936 | tf_op jit(solution)/shard_map/ppermute | solution.py:685
  34.4 8.2 %collective-permute-start.6 = (f32[3,8,128]{2,1,0:T(8,128)S(1)}, f32[3,8,128]{2,1,0:T(8,128)S(1)}, u32[]{:S(2)}, u32[]{:S(2)}) collective-permute-start(f32[3,8,128]{2,1,0:T(8,128)S(1)} %get-tuple-element.48), channel_id=1, source_target_pairs={{0,16},{32,48},{64,80},{96,112},{16,0},{48,32},{80,64},{112,96},{1... | collective-permute-start | bytes 36872 | tf_op jit(solution)/shard_map/ppermute | solution.py:677
  36.4 6.2 %collective-permute-start.7 = (f32[3,8,128]{2,1,0:T(8,128)S(1)}, f32[3,8,128]{2,1,0:T(8,128)S(1)}, u32[]{:S(2)}, u32[]{:S(2)}) collective-permute-start(f32[3,8,128]{2,1,0:T(8,128)S(1)} %get-tuple-element.45.refs_3_), channel_id=1, source_target_pairs={{16,32},{48,64},{80,96},{32,16},{64,48},{96,80},{17,33},{49,65},{8... | collective-permute-start | bytes 36872 | tf_op jit(solution)/shard_map/ppermute | solution.py:676

commit v7 on v6

--- a/solution.py
+++ b/solution.py
@@ -269,8 +269,12 @@
         out[27 + k] = jnp.where(wn == 2, near[27 + k], w[k])
 
 
+def rows(at):
+    return pl.ds(2 * at, 8, 2)
+
+
 def d_rows(f3, f, l, at):
-    m2, m1, p1, p2 = (f3[f, l, pl.ds(at + k, 8)] for k in (-2, -1, 1, 2))
+    m2, m1, p1, p2 = (f3[f, l, rows(at + k)] for k in (-2, -1, 1, 2))
     return (m2 - p2) + 8.0 * (p1 - m1)
 
 
@@ -283,7 +287,7 @@
 
 
 def put_halo(f3, f, l, x):
-    return [(f3, (f, l, slice(24, 32)), x), (f3, (f, l, slice(8, 16)), x)]
+    return [(f3, (f, l, rows(24)), x), (f3, (f, l, rows(8)), x)]
 
 
 def d_normal(get, l):
@@ -345,7 +349,7 @@
         todo = []
         for f in range(5):
             a = f3x[f, l]
-            todo += [(gx, (f, l), hx * f1x[f, l] + hz * a), (f3, (f, l, slice(16, 24)), a)]
+            todo += [(gx, (f, l), hx * f1x[f, l] + hz * a), (f3, (f, l, rows(16)), a)]
         return todo
 
     def halo_flux(l):
@@ -492,7 +496,7 @@
         todo = []
         for f in range(5):
             todo += [(r, (f, k), x[f]) for r, x in ((f1w, a1), (f2w, a2), (gw, g))]
-            todo += [(f3, (f, k, slice(16, 24)), a3[f])]
+            todo += [(f3, (f, k, rows(16)), a3[f])]
         return todo
 
     def eta_of(l):
@@ -565,7 +569,7 @@
         todo = []
         for f in range(5):
             todo += [(r, (f, l + 2), x[f]) for r, x in ((f1x, a1), (f2x, a2), (gx, g))]
-            todo += [(f3, (f, l + 2, slice(16, 24)), a3[f])]
+            todo += [(f3, (f, l + 2, rows(16)), a3[f])]
         return todo
 
     def halo_flux_two(l):
@@ -680,7 +684,7 @@
         stage_prepare,
         (own[0], own[1], halo, strips, *parts, far),
         [(5, NL, *plane)] * 5,
-        [(5, NL, *plane)] * 4 + [(5, NL, 40, 128), (5, 2, *plane)],
+        [(5, NL, *plane)] * 4 + [(5, NL, 80, 128), (5, 2, *plane)],
     )
     far = lax.ppermute(far, "wn", [(1, 2), (2, 1), (3, 0)])
     return call(
@@ -691,7 +695,7 @@
         + [(5, 16, *plane)] * 3
         + [(5, 12, *plane)] * 2
         + [(5, 20, *plane)] * 3
-        + [(5, 20, 40, 128)]
+        + [(5, 20, 80, 128)]
         + [(5, 20, *plane), (5, NL, *plane), (5, 3, *plane), (5, 2, *plane), (UNITS, *plane), (5, NL, *plane), plane],
         sems=5,
         out_space=HBM,

time: 46.9 us -> 47 us (level)
  no operation moved by 1% of the time
where the time goes in v7:
time: 47 us; the launch traced here: 46.7 us
  starting transfers between devices  36.4 us (77%)
  Pallas kernels  8.46 us (18%)
  waiting for transfers between devices  1.07 us (2%)
  between operations  0.76 us (2%)
    ppermute x1, starting transfers between devices, per_device(): a2 = lax.ppermute(two, 'az', swaps(around, 1, True))  10.6 us
    ppermute x2, starting transfers between devices, per_device(): s2 = lax.ppermute(two, 'sx', swaps(tiles, 1, False))  9.21 us
    pallas_call x8, Pallas kernels, call(): pl.pallas_call(body, out_shape=shapes, in_specs=[space] * len(ins), out_s...  8.46 us
    ppermute x1, starting transfers between devices, per_device(): far = lax.ppermute(far, 'wn', [(1, 2), (2, 1), (3, 0)])  4.9 us
    ppermute x1, starting transfers between devices, per_device(): near = lax.ppermute(near, 'wn', [(0, 1), (1, 0), (2, 3), (3, 2)])  4.5 us
    ppermute x2, starting transfers between devices, per_device(): s1 = lax.ppermute(one, 'sx', swaps(tiles, 0, False))  4.06 us
    ppermute x1, starting transfers between devices, per_device(): a1 = lax.ppermute(one, 'az', swaps(around, 0, True))  3.12 us
  transfers between devices with their start and end apart: 8, of which 2 were waited for; matrix products, arithmetic and copies ran while one was open for 0% of the time, Pallas kernels for 6%

profile of v7, /device:TPU:25, one launch (start us, length us, event | category | flops | bytes accessed | tf_op | source)
XLA Modules:
  0.0 46.7 jit_solution(2657684510452886661)
XLA Ops:
  0.6 1.0 %shard_map.50 = (f32[5,16,8,128]{3,2,1,0:T(8,128)S(1)}, f32[8,128]{1,0:T(8,128)S(1)}, f32[5,8,128]{2,1,0:T(8,128)S(1)}, f32[43,8,128]{2,1,0:T(8,128)S(1)}, f32[43,8,128]{2,1,0:T(8,128)S(1)}) custom-call(f32[5,16,8,128]{3,2,1,0:T(8,128)} %refs_0_.1, f32[8,128]{1,0:T(8,128)} %refs_1_.1, f32[5,8,128]{2,1,0:T(8,128)} %refs_2_.1), custom_call_target="tpu_custom_call" | custom-call | tf_op jit(solution)/shard_map/pallas_call | solution.py:604
  1.7 3.1 %collective-permute-start = (f32[43,8,128]{2,1,0:T(8,128)S(1)}, f32[43,8,128]{2,1,0:T(8,128)S(1)}, u32[]{:S(2)}, u32[]{:S(2)}) collective-permute-start(f32[43,8,128]{2,1,0:T(8,128)S(1)} %get-tuple-element.33), channel_id=1, source_target_pairs={{0,1},{2,3},{4,5},{6,7},{8,9},{10,11},{12,13},{14,15},{1,0},{3,2},... | collective-permute-start | bytes 528392 | tf_op jit(solution)/shard_map/ppermute | solution.py:667
  4.8 10.6 %collective-permute-start.1 = (f32[43,8,128]{2,1,0:T(8,128)S(1)}, f32[43,8,128]{2,1,0:T(8,128)S(1)}, u32[]{:S(2)}, u32[]{:S(2)}) collective-permute-start(f32[43,8,128]{2,1,0:T(8,128)S(1)} %get-tuple-element.34), channel_id=1, source_target_pairs={{1,2},{3,4},{5,6},{7,8},{9,10},{11,12},{13,14},{15,0},{2,1},{4,3},... | collective-permute-start | bytes 528392 | tf_op jit(solution)/shard_map/ppermute | solution.py:666
  15.4 0.2 shard_map.51
  15.7 2.1 %collective-permute-start.2 = (f32[3,8,128]{2,1,0:T(8,128)S(1)}, f32[3,8,128]{2,1,0:T(8,128)S(1)}, u32[]{:S(2)}, u32[]{:S(2)}) collective-permute-start(f32[3,8,128]{2,1,0:T(8,128)S(1)} %get-tuple-element.37), channel_id=1, source_target_pairs={{0,16},{32,48},{64,80},{96,112},{16,0},{48,32},{80,64},{112,96},{1... | collective-permute-start | bytes 36872 | tf_op jit(solution)/shard_map/ppermute | solution.py:670
  17.7 4.6 %collective-permute-start.3 = (f32[3,8,128]{2,1,0:T(8,128)S(1)}, f32[3,8,128]{2,1,0:T(8,128)S(1)}, u32[]{:S(2)}, u32[]{:S(2)}) collective-permute-start(f32[3,8,128]{2,1,0:T(8,128)S(1)} %get-tuple-element.38), channel_id=1, source_target_pairs={{16,32},{48,64},{80,96},{32,16},{64,48},{96,80},{17,33},{49,65},{8... | collective-permute-start | bytes 36872 | tf_op jit(solution)/shard_map/ppermute | solution.py:669
  22.4 0.7 %shard_map.52 = (f32[5,16,8,128]{3,2,1,0:T(8,128)S(1)}, f32[5,16,8,128]{3,2,1,0:T(8,128)S(1)}, f32[5,16,8,128]{3,2,1,0:T(8,128)S(1)}, f32[5,16,8,128]{3,2,1,0:T(8,128)S(1)}, f32[5,16,8,128]{3,2,1,0:T(8,128)S(1)}) custom-call(f32[5,16,8,128]{3,2,1,0:T(8,128)S(1)} %get-tuple-element.30.refs_0_, f32[3,8,128]{2,1,0:T(8,128)S(1)} %get-tuple-element.35.refs_1_.refs_5_), custom_call_target="tpu_custom_call" | custom-call | tf_op jit(solution)/shard_map/pallas_call | solution.py:604
  23.1 0.0 collective-permute-done.2.refs_7_
  23.1 0.3 collective-permute-done.3.refs_8_
  23.5 0.0 collective-permute-done.refs_3_
  23.5 0.0 collective-permute-done.1.refs_4_
  23.5 0.5 %shard_map.53 = (f32[86,8,128]{2,1,0:T(8,128)S(1)}, f32[11,8,128]{2,1,0:T(8,128)S(1)}, f32[4,8,128]{2,1,0:T(8,128)S(1)}, f32[31,8,128]{2,1,0:T(8,128)S(1)}, f32[27,8,128]{2,1,0:T(8,128)S(1)}) custom-call(f32[5,16,8,128]{3,2,1,0:T(8,128)S(1)} %get-tuple-element.30.refs_0_, f32[8,128]{1,0:T(8,128)S(1)} %get-tuple-element.31.refs_1_, ...), custom_call_target="tpu_custom_call" | custom-call | tf_op jit(solution)/shard_map/pallas_call | solution.py:604
  24.0 4.5 %collective-permute-start.4 = (f32[31,8,128]{2,1,0:T(8,128)S(1)}, f32[31,8,128]{2,1,0:T(8,128)S(1)}, u32[]{:S(2)}, u32[]{:S(2)}) collective-permute-start(f32[31,8,128]{2,1,0:T(8,128)S(1)} %get-tuple-element.43), channel_id=1, source_target_pairs={{0,128},{128,0},{256,384},{384,256},{1,129},{129,1},{257,385},{385... | collective-permute-start | bytes 380936 | tf_op jit(solution)/shard_map/ppermute | solution.py:679
  28.5 0.2 shard_map.54
  28.7 0.7 %collective-permute-done.4.refs_2_.refs_6_ = f32[31,8,128]{2,1,0:T(8,128)S(1)} collective-permute-done((f32[31,8,128]{2,1,0:T(8,128)S(1)}, f32[31,8,128]{2,1,0:T(8,128)S(1)}, u32[]{:S(2)}, u32[]{:S(2)}) %collective-permute-start.4) | collective-permute-done | bytes 127008 | tf_op jit(solution)/shard_map/ppermute | solution.py:679
  29.5 4.9 %collective-permute-start.5 = (f32[31,8,128]{2,1,0:T(8,128)S(1)}, f32[31,8,128]{2,1,0:T(8,128)S(1)}, u32[]{:S(2)}, u32[]{:S(2)}) collective-permute-start(f32[31,8,128]{2,1,0:T(8,128)S(1)} %shard_map.55.refs_9_), channel_id=1, source_target_pairs={{128,256},{256,128},{384,0},{129,257},{257,129},{385,1},{130,258},... | collective-permute-start | bytes 380936 | tf_op jit(solution)/shard_map/ppermute | solution.py:689
  34.4 2.0 %collective-permute-start.6 = (f32[3,8,128]{2,1,0:T(8,128)S(1)}, f32[3,8,128]{2,1,0:T(8,128)S(1)}, u32[]{:S(2)}, u32[]{:S(2)}) collective-permute-start(f32[3,8,128]{2,1,0:T(8,128)S(1)} %get-tuple-element.48), channel_id=1, source_target_pairs={{0,16},{32,48},{64,80},{96,112},{16,0},{48,32},{80,64},{112,96},{1... | collective-permute-start | bytes 36872 | tf_op jit(solution)/shard_map/ppermute | solution.py:681
  36.4 4.6 %collective-permute-start.7 = (f32[3,8,128]{2,1,0:T(8,128)S(1)}, f32[3,8,128]{2,1,0:T(8,128)S(1)}, u32[]{:S(2)}, u32[]{:S(2)}) collective-permute-start(f32[3,8,128]{2,1,0:T(8,128)S(1)} %get-tuple-element.45.refs_3_), channel_id=1, source_target_pairs={{16,32},{48,64},{80,96},{32,16},{64,48},{96,80},{17,33},{49,65},{8... | collective-permute-start | bytes 36872 | tf_op jit(solution)/shard_map/ppermute | solution.py:680
  41.0 1.7 %shard_map.56 = (f32[5,16,8,128]{3,2,1,0:T(8,128)S(1)}, f32[5,16,8,128]{3,2,1,0:T(8,128)S(1)}, f32[5,16,8,128]{3,2,1,0:T(8,128)S(1)}, f32[5,16,8,128]{3,2,1,0:T(8,128)S(1)}, f32[5,16,8,128]{3,2,1,0:T(8,128)S(1)}) custom-call(f32[5,16,8,128]{3,2,1,0:T(8,128)S(1)} %get-tuple-element.30.refs_0_, f32[8,128]{1,0:T(8,128)S(1)} %get-tuple-element.31.refs_1_, ...), custom_call_target="tpu_custom_call" | custom-call | tf_op jit(solution)/shard_map/pallas_call | solution.py:604
  42.6 0.0 collective-permute-done.6.refs_10_
  42.6 0.0 collective-permute-done.7.refs_11_
  42.6 0.0 collective-permute-done.5.refs_7_
  42.7 4.1 %shard_map.57 = (f32[5,16,8,128]{3,2,1,0:T(8,128)}, f32[8,128]{1,0:T(8,128)}) custom-call(f32[5,16,8,128]{3,2,1,0:T(8,128)S(1)} %get-tuple-element.30.refs_0_, f32[8,128]{1,0:T(8,128)S(1)} %get-tuple-element.31.refs_1_, f32[5,8,128]{2,1,0:T(8,128)S(1)} %get-tuple-element.32.refs_2_, f32[86,8,128]{2,1,0:T(8,128)S(1)} %get-tuple-element.40.refs_0_.refs_2_.refs_3_, ...), custom_call_target="tpu_custom_call" | custom-call | tf_op jit(solution)/shard_map/pallas_call | solution.py:604
  (1 shorter events, 0.0 us)
Async XLA Ops:
  1.7 21.8 %collective-permute-start = (f32[43,8,128]{2,1,0:T(8,128)S(1)}, f32[43,8,128]{2,1,0:T(8,128)S(1)}, u32[]{:S(2)}, u32[]{:S(2)}) collective-permute-start(f32[43,8,128]{2,1,0:T(8,128)S(1)} %get-tuple-element.33), channel_id=1, source_target_pairs={{0,1},{2,3},{4,5},{6,7},{8,9},{10,11},{12,13},{14,15},{1,0},{3,2},... | collective-permute-start | bytes 528392 | tf_op jit(solution)/shard_map/ppermute | solution.py:667
  4.8 18.7 %collective-permute-start.1 = (f32[43,8,128]{2,1,0:T(8,128)S(1)}, f32[43,8,128]{2,1,0:T(8,128)S(1)}, u32[]{:S(2)}, u32[]{:S(2)}) collective-permute-start(f32[43,8,128]{2,1,0:T(8,128)S(1)} %get-tuple-element.34), channel_id=1, source_target_pairs={{1,2},{3,4},{5,6},{7,8},{9,10},{11,12},{13,14},{15,0},{2,1},{4,3},... | collective-permute-start | bytes 528392 | tf_op jit(solution)/shard_map/ppermute | solution.py:666
  15.7 7.5 %collective-permute-start.2 = (f32[3,8,128]{2,1,0:T(8,128)S(1)}, f32[3,8,128]{2,1,0:T(8,128)S(1)}, u32[]{:S(2)}, u32[]{:S(2)}) collective-permute-start(f32[3,8,128]{2,1,0:T(8,128)S(1)} %get-tuple-element.37), channel_id=1, source_target_pairs={{0,16},{32,48},{64,80},{96,112},{16,0},{48,32},{80,64},{112,96},{1... | collective-permute-start | bytes 36872 | tf_op jit(solution)/shard_map/ppermute | solution.py:670
  17.7 5.7 %collective-permute-start.3 = (f32[3,8,128]{2,1,0:T(8,128)S(1)}, f32[3,8,128]{2,1,0:T(8,128)S(1)}, u32[]{:S(2)}, u32[]{:S(2)}) collective-permute-start(f32[3,8,128]{2,1,0:T(8,128)S(1)} %get-tuple-element.38), channel_id=1, source_target_pairs={{16,32},{48,64},{80,96},{32,16},{64,48},{96,80},{17,33},{49,65},{8... | collective-permute-start | bytes 36872 | tf_op jit(solution)/shard_map/ppermute | solution.py:669
  24.0 5.5 %collective-permute-start.4 = (f32[31,8,128]{2,1,0:T(8,128)S(1)}, f32[31,8,128]{2,1,0:T(8,128)S(1)}, u32[]{:S(2)}, u32[]{:S(2)}) collective-permute-start(f32[31,8,128]{2,1,0:T(8,128)S(1)} %get-tuple-element.43), channel_id=1, source_target_pairs={{0,128},{128,0},{256,384},{384,256},{1,129},{129,1},{257,385},{385... | collective-permute-start | bytes 380936 | tf_op jit(solution)/shard_map/ppermute | solution.py:679
  29.5 13.2 %collective-permute-start.5 = (f32[31,8,128]{2,1,0:T(8,128)S(1)}, f32[31,8,128]{2,1,0:T(8,128)S(1)}, u32[]{:S(2)}, u32[]{:S(2)}) collective-permute-start(f32[31,8,128]{2,1,0:T(8,128)S(1)} %shard_map.55.refs_9_), channel_id=1, source_target_pairs={{128,256},{256,128},{384,0},{129,257},{257,129},{385,1},{130,258},... | collective-permute-start | bytes 380936 | tf_op jit(solution)/shard_map/ppermute | solution.py:689
  34.4 8.3 %collective-permute-start.6 = (f32[3,8,128]{2,1,0:T(8,128)S(1)}, f32[3,8,128]{2,1,0:T(8,128)S(1)}, u32[]{:S(2)}, u32[]{:S(2)}) collective-permute-start(f32[3,8,128]{2,1,0:T(8,128)S(1)} %get-tuple-element.48), channel_id=1, source_target_pairs={{0,16},{32,48},{64,80},{96,112},{16,0},{48,32},{80,64},{112,96},{1... | collective-permute-start | bytes 36872 | tf_op jit(solution)/shard_map/ppermute | solution.py:681
  36.4 6.3 %collective-permute-start.7 = (f32[3,8,128]{2,1,0:T(8,128)S(1)}, f32[3,8,128]{2,1,0:T(8,128)S(1)}, u32[]{:S(2)}, u32[]{:S(2)}) collective-permute-start(f32[3,8,128]{2,1,0:T(8,128)S(1)} %get-tuple-element.45.refs_3_), channel_id=1, source_target_pairs={{16,32},{48,64},{80,96},{32,16},{64,48},{96,80},{17,33},{49,65},{8... | collective-permute-start | bytes 36872 | tf_op jit(solution)/shard_map/ppermute | solution.py:680

commit v8 on v6

--- a/solution.py
+++ b/solution.py
@@ -13,7 +13,7 @@
 NL = 16
 NP = 86
 HALF = 43
-UNITS = 11
+UNITS = 12
 SCALE = LAYERS / 12.0
 STEP = CFL_STEP / LAYERS
 C = CFL_STEP / 12.0
@@ -118,15 +118,6 @@
     return out
 
 
-def slopes(h, hz, hs, hsz):
-    ds, dsz = d_lane(hs), d_lane(hsz)
-    x = SCALE * patched(d_lane(h), rl(strip_patch(ds), -12))
-    xz = SCALE * patched(d_lane(hz), rl(strip_patch(dsz), -12))
-    a, az = d_ring(h, hz)
-    s, _ = d_ring(hs, hsz)
-    return (x, SCALE * a), (xz, SCALE * az), (SCALE * ds, SCALE * s)
-
-
 def plane_of(q, h, b):
     def get(i):
         if i < 80:
@@ -137,7 +128,7 @@
 
 
 def unit_planes(u):
-    return [8 * u + j for j in range(8)] if u < 10 else [80 + j for j in range(6)]
+    return [8 * u + j for j in range(8)] if u < 10 else [80] * 8 if u == 11 else [80 + j for j in range(6)]
 
 
 def columns(get, right, left):
@@ -204,7 +195,7 @@
 
 
 def pack_second(odd, wn, tile, tiles, q, h, b, a1, a2, right, left, s1, s2, _parts, *outs):
-    z, strips, w, near, far, hi, lo = outs
+    z, strips, w, near, far, slope, hi, lo = outs
     ln, rw = lane(), row()
     mask = (rw >= 4) ^ odd
     for i in range(HALF):
@@ -223,8 +214,9 @@
     w0 = speed(own, bq)
     w0z = speed(zq, bz)
     w0s = spread(speed(sq, [rl(surf, 16 * (6 - f)) for f in range(5)]), 7)
-    hx = SCALE * patched(d_lane(h[...]), rl(strip_patch(d_lane(surf)), -12))
-    hz = SCALE * d_ring(h[...], z[80])[0]
+    hx = slope[0] = SCALE * patched(d_lane(h[...]), rl(strip_patch(d_lane(strips[11])), -12))
+    hz, hzz = (SCALE * x for x in d_ring(h[...], z[80]))
+    slope[1], slope[2] = hz, hzz
     (f1s,) = fluxes(sq, (1,))
     (f3z,) = fluxes(zq, (3,))
     levels = []
@@ -302,18 +294,19 @@
     return patched(jnp.zeros_like(patch), patch)
 
 
-def batches(first_l, count, size, body, after=None):
+def together(count, *parts, after=None):
     def step(i, _):
         todo = []
-        for k in range(size):
-            todo += body(first_l + i * size + k)
+        for first, size, body in parts:
+            for k in range(size):
+                todo += body(first + i * size + k)
         for ref, at, x in todo:
             ref[at] = x
         if after is not None:
             after(i)
         return 0
 
-    lax.fori_loop(0, count // size, step, 0)
+    lax.fori_loop(0, count, step, 0)
 
 
 def own_parts(q, _right, f1, f3, d1, dn, dq, f2):
@@ -326,16 +319,20 @@
             (r, (f, l), d_normal(plane_at(x, f), l)) for f in range(5) for r, x in ((dn, f2), (dq, q))
         ]
 
-    batches(0, NL, 4, flux)
-    batches(2, 12, 4, inner)
-
-
-def prepare(wn, q, h, z, strips, f1x, f3x, d1x, dnx, dqx, _far, tx, bx, tz, bz, ez, gx, f1z, f2z, gz, f3, pt):
+    together(4, (0, 4, flux))
+    together(3, (2, 4, inner))
+
+
+def prepare(wn, q, h, z, strips, slope, f1x, f3x, d1x, dnx, dqx, _far, tx, bx, tz, bz, ez, ghost, gx, f1z, f2z, gz, f3, pt):
     h0, h0z = h[...], z[80]
-    hx = SCALE * patched(d_lane(h0), rl(strip_patch(d_lane(spread(strips[10], 0))), -12))
-    hz, hzz = (SCALE * x for x in d_ring(h0, h0z))
+    hx, hz, hzz = (slope[k] for k in range(3))
     ih, ihz = C / h0, C / h0z
     base = wn * NL
+    ln = lane()
+    for f in range(5):
+        s_lo = strips[2 * f]
+        mirrored = MIRROR[f] * jnp.where(ln >= 112, rl(s_lo, -16), rl(s_lo, 80))
+        ghost[f] = jnp.where(ln < 64, spread(strips[10], 1 + f), mirrored)
     for v in range(2):
         (a1,) = fluxes([strips[2 * f + v] for f in range(5)], (1,))
         for f in range(5):
@@ -356,15 +353,13 @@
             todo += put_halo(f3, f, l, a3[f])
         return todo
 
-    batches(0, NL, 4, own_moving)
-    batches(0, NL, 4, halo_flux)
+    together(4, (0, 4, own_moving), (0, 4, halo_flux))
 
     def own_surface(f, l):
         dx = patched(d1x[f, l], pltpu.roll(pt[f, l >> 3], patch_shift(l), 1))
         return q[f, l] - C * (dx + d_around(f3, f, l))
 
     def halo_surface(f, l):
-        ln = lane()
         dx = jnp.where((ln < 2) | (ln >= 126), 0.0, d_lane(f1z[f, l]))
         return z[f * NL + l] - C * (dx + d_around_halo(f3, f, l))
 
@@ -383,18 +378,16 @@
             todo += [(ez, (f, l), k * d_normal(plane_at(f1z, f), l))]
         return todo
 
-    def outer(l):
+    def outer(m):
+        l = m + 12 * (m >= 2).astype(jnp.int32)
         return [(tx, (f, l), own_surface(f, l)) for f in range(5)] + [
             (tz, (f, l), halo_surface(f, l)) for f in range(5)
         ]
 
-    batches(2, 12, 4, own_inner)
-    batches(2, 12, 4, halo_inner)
-    for l in (0, 14):
-        batches(l, 2, 2, outer)
-
-
-def advance(wn, tile, tiles, q, h, b, z, strips, w, near, far, z_right, z_left, z_one, z_two, tx, bx, tz, bz, ez, *rest):
+    together(4, (2, 3, own_inner), (2, 3, halo_inner), (0, 1, outer))
+
+
+def advance(wn, tile, tiles, q, h, b, z, strips, w, near, far, z_right, z_left, z_one, z_two, slope, tx, bx, tz, bz, ez, ghost, *rest):
     out_hbm, h_hbm, qw, zw, f1w, f2w, gw, f2zw, gzw, f1x, f2x, gx, f3, sx, sz, pt, ptz, zst, out, h_out, sems = rest
     first, last = tile == 0, tile == tiles - 1
 
@@ -418,7 +411,6 @@
     speeds = [jnp.where(top, w[k], jnp.where(wn == 2, near[27 + k], far[27 + k])) for k in range(4)]
     w0, w0z, w0s, w1 = speeds
 
-    surf, surf_z = strips[10], zst[10]
     strip_q = []
     for f in range(5):
         sign = MIRROR[f]
@@ -440,13 +432,15 @@
             sb, sa = rl(below(25), 96 - 32 * f), rl(above(25), -32 * f)
         else:
             sb, sa = below(26), above(26)
-        sb = jnp.where(bottom, sign * jnp.where(group == 7, rl(s_lo, -16), rl(s_lo, 80)), sb)
-        sa = jnp.where(top, spread(surf, 1 + f), sa)
+        sb = jnp.where(bottom, ghost[f], sb)
+        sa = jnp.where(top, ghost[f], sa)
         strip_q.append((s_lo, s_hi, jnp.where(ln < 64, sa, sb)))
 
     h0, h0z = h[...], z[80]
-    h0s, h0sz = spread(surf, 0), spread(surf_z, 0)
-    (hx, hz), (hxz, hzz), (hxs, hzs) = slopes(h0, h0z, h0s, h0sz)
+    h0s, h0sz = strips[11], zst[11]
+    hx, hz, hzz = (slope[k] for k in range(3))
+    hxz = SCALE * patched(d_lane(h0z), rl(strip_patch(d_lane(h0sz)), -12))
+    hxs, hzs = SCALE * d_lane(h0s), SCALE * d_ring(h0s, h0sz)[0]
     ih, ihz, ihs = 1.0 / h0, 1.0 / h0z, 1.0 / h0s
     base = wn * NL
 
@@ -498,7 +492,6 @@
     def eta_of(l):
         return ((base + l).astype(F32) + 0.5) / LAYERS
 
-    batches(0, 16, 4, own_flux)
 
     def halo_flux(k):
         a2, a3, g = fluxes([zw[f, k] for f in range(5)], (2, 3), move=(hxz, hzz, w0z))
@@ -507,7 +500,7 @@
             todo += [(r, (f, k), x[f]) for r, x in ((f2zw, a2), (gzw, g))] + put_halo(f3, f, k + 2, a3[f])
         return todo
 
-    batches(0, 12, 4, halo_flux)
+    together(4, (0, 4, own_flux), (0, 3, halo_flux))
 
     def normal_own(f, k, eta):
         return ih * (eta * d_normal(plane_at(gw, f), k) - d_normal(plane_at(f2w, f), k))
@@ -540,9 +533,7 @@
             todo.append((sz, (f, l), (tz[f, l] + w0z * bz[f, l]) + (hxz * ez[f, l] - C * edge)))
         return todo
 
-    batches(0, 4, 2, ghost_layer)
-    batches(0, 4, 2, outer)
-    batches(2, 12, 4, inner)
+    together(2, (0, 2, ghost_layer), (0, 2, outer), (2, 6, inner))
     for f in range(5):
         for k in range(2):
             sx[f, k] = jnp.where(bottom, MIRROR[f] * sx[f, 3 - k], sx[f, k])
@@ -582,14 +573,13 @@
             todo.append((out, (f, l), 0.5 * (q[f, l] + sx[f, l + 2] + C * rate)))
         return todo
 
-    batches(-2, 20, 4, own_flux_two)
-    batches(0, NL, 4, halo_flux_two)
+    together(4, (-2, 5, own_flux_two), (0, 4, halo_flux_two))
 
     def out_copy(i):
         part = (slice(None), pl.ds(4 * i, 4))
         return pltpu.make_async_copy(out.at[part], out_hbm.at[part], sems.at[i])
 
-    batches(0, NL, 4, final, lambda i: out_copy(i).start())
+    together(4, (0, 4, final), after=lambda i: out_copy(i).start())
     for i in range(4):
         out_copy(i).wait()
     h_copy.wait()
@@ -665,10 +655,10 @@
     s2 = lax.ppermute(two, "sx", swaps(tiles, 1, False))
     s1 = lax.ppermute(one, "sx", swaps(tiles, 0, False))
     parts = call(stage_own, (own[0], right), [(5, NL, *plane)] * 5, [(5, NL, *plane)])
-    halo, strips, w, near, far = call(
+    halo, strips, w, near, far, slope = call(
         stage_second,
         (*own, a1, a2, right, left, s1, s2, parts[3]),
-        [(NP, *plane), (UNITS, *plane), (4, *plane), (31, *plane), (27, *plane)],
+        [(NP, *plane), (UNITS, *plane), (4, *plane), (31, *plane), (27, *plane), (3, *plane)],
         [(27, *plane)] * 2,
     )
     z_right, z_left, one, two = call(stage_corners, (halo,), [(3, *plane)] * 4)
@@ -678,14 +668,14 @@
     (far,) = call(stage_far, (far, w, near, two), [(31, *plane)])
     parts = call(
         stage_prepare,
-        (own[0], own[1], halo, strips, *parts, far),
-        [(5, NL, *plane)] * 5,
+        (own[0], own[1], halo, strips, slope, *parts, far),
+        [(5, NL, *plane)] * 5 + [(5, *plane)],
         [(5, NL, *plane)] * 4 + [(5, NL, 40, 128), (5, 2, *plane)],
     )
     far = lax.ppermute(far, "wn", [(1, 2), (2, 1), (3, 0)])
     return call(
         stage_advance,
-        (*own, halo, strips, w, near, far, z_right, z_left, s1, s2, *parts),
+        (*own, halo, strips, w, near, far, z_right, z_left, s1, s2, slope, *parts),
         [(5, NL, *plane), plane],
         [(5, 16, *plane), (5, 12, *plane)]
         + [(5, 16, *plane)] * 3

time: 46.9 us -> 46.2 us (0.985)
  Pallas kernels: 8.36 us -> 7.65 us
    pallas_call x8, Pallas kernels: 8.36 us -> 7.65 us  [call(): pl.pallas_call(body, out_shape=shapes, in_specs=[space] * len(ins), out_s...]
  transfers between devices with their start and end apart: 8 -> 8, of which waited for: 2 -> 2; matrix products, arithmetic and copies ran while one was open for 0% -> 0% of each run, Pallas kernels for 6% -> 5%
where the time goes in v8:
time: 46.2 us; the launch traced here: 45.9 us
  starting transfers between devices  36.4 us (79%)
  Pallas kernels  7.65 us (17%)
  waiting for transfers between devices  1.08 us (2%)
  between operations  0.76 us (2%)
    ppermute x1, starting transfers between devices, per_device(): a2 = lax.ppermute(two, 'az', swaps(around, 1, True))  10.6 us
    ppermute x2, starting transfers between devices, per_device(): s2 = lax.ppermute(two, 'sx', swaps(tiles, 1, False))  9.21 us
    pallas_call x8, Pallas kernels, call(): pl.pallas_call(body, out_shape=shapes, in_specs=[space] * len(ins), out_s...  7.65 us
    ppermute x1, starting transfers between devices, per_device(): far = lax.ppermute(far, 'wn', [(1, 2), (2, 1), (3, 0)])  4.9 us
    ppermute x1, starting transfers between devices, per_device(): near = lax.ppermute(near, 'wn', [(0, 1), (1, 0), (2, 3), (3, 2)])  4.5 us
    ppermute x2, starting transfers between devices, per_device(): s1 = lax.ppermute(one, 'sx', swaps(tiles, 0, False))  4.06 us
    ppermute x1, starting transfers between devices, per_device(): a1 = lax.ppermute(one, 'az', swaps(around, 0, True))  3.12 us
  transfers between devices with their start and end apart: 8, of which 2 were waited for; matrix products, arithmetic and copies ran while one was open for 0% of the time, Pallas kernels for 5%

profile of v8, /device:TPU:25, one launch (start us, length us, event | category | flops | bytes accessed | tf_op | source)
XLA Modules:
  0.0 45.9 jit_solution(4562565173151028018)
XLA Ops:
  0.6 1.0 %shard_map.50 = (f32[5,16,8,128]{3,2,1,0:T(8,128)S(1)}, f32[8,128]{1,0:T(8,128)S(1)}, f32[5,8,128]{2,1,0:T(8,128)S(1)}, f32[43,8,128]{2,1,0:T(8,128)S(1)}, f32[43,8,128]{2,1,0:T(8,128)S(1)}) custom-call(f32[5,16,8,128]{3,2,1,0:T(8,128)} %refs_0_.1, f32[8,128]{1,0:T(8,128)} %refs_1_.1, f32[5,8,128]{2,1,0:T(8,128)} %refs_2_.1), custom_call_target="tpu_custom_call" | custom-call | tf_op jit(solution)/shard_map/pallas_call | solution.py:590
  1.7 3.1 %collective-permute-start = (f32[43,8,128]{2,1,0:T(8,128)S(1)}, f32[43,8,128]{2,1,0:T(8,128)S(1)}, u32[]{:S(2)}, u32[]{:S(2)}) collective-permute-start(f32[43,8,128]{2,1,0:T(8,128)S(1)} %get-tuple-element.35), channel_id=1, source_target_pairs={{0,1},{2,3},{4,5},{6,7},{8,9},{10,11},{12,13},{14,15},{1,0},{3,2},... | collective-permute-start | bytes 528392 | tf_op jit(solution)/shard_map/ppermute | solution.py:653
  4.8 10.6 %collective-permute-start.1 = (f32[43,8,128]{2,1,0:T(8,128)S(1)}, f32[43,8,128]{2,1,0:T(8,128)S(1)}, u32[]{:S(2)}, u32[]{:S(2)}) collective-permute-start(f32[43,8,128]{2,1,0:T(8,128)S(1)} %get-tuple-element.36), channel_id=1, source_target_pairs={{1,2},{3,4},{5,6},{7,8},{9,10},{11,12},{13,14},{15,0},{2,1},{4,3},... | collective-permute-start | bytes 528392 | tf_op jit(solution)/shard_map/ppermute | solution.py:652
  15.4 0.2 shard_map.51
  15.7 2.1 %collective-permute-start.2 = (f32[3,8,128]{2,1,0:T(8,128)S(1)}, f32[3,8,128]{2,1,0:T(8,128)S(1)}, u32[]{:S(2)}, u32[]{:S(2)}) collective-permute-start(f32[3,8,128]{2,1,0:T(8,128)S(1)} %get-tuple-element.39), channel_id=1, source_target_pairs={{0,16},{32,48},{64,80},{96,112},{16,0},{48,32},{80,64},{112,96},{1... | collective-permute-start | bytes 36872 | tf_op jit(solution)/shard_map/ppermute | solution.py:656
  17.8 4.6 %collective-permute-start.3 = (f32[3,8,128]{2,1,0:T(8,128)S(1)}, f32[3,8,128]{2,1,0:T(8,128)S(1)}, u32[]{:S(2)}, u32[]{:S(2)}) collective-permute-start(f32[3,8,128]{2,1,0:T(8,128)S(1)} %get-tuple-element.40), channel_id=1, source_target_pairs={{16,32},{48,64},{80,96},{32,16},{64,48},{96,80},{17,33},{49,65},{8... | collective-permute-start | bytes 36872 | tf_op jit(solution)/shard_map/ppermute | solution.py:655
  22.4 0.7 %shard_map.52 = (f32[5,16,8,128]{3,2,1,0:T(8,128)S(1)}, f32[5,16,8,128]{3,2,1,0:T(8,128)S(1)}, f32[5,16,8,128]{3,2,1,0:T(8,128)S(1)}, f32[5,16,8,128]{3,2,1,0:T(8,128)S(1)}, f32[5,16,8,128]{3,2,1,0:T(8,128)S(1)}) custom-call(f32[5,16,8,128]{3,2,1,0:T(8,128)S(1)} %get-tuple-element.32.refs_0_, f32[3,8,128]{2,1,0:T(8,128)S(1)} %get-tuple-element.37.refs_1_.refs_5_), custom_call_target="tpu_custom_call" | custom-call | tf_op jit(solution)/shard_map/pallas_call | solution.py:590
  23.1 0.0 collective-permute-done.2.refs_7_
  23.1 0.3 collective-permute-done.3.refs_8_
  23.5 0.0 collective-permute-done.refs_3_
  23.5 0.0 collective-permute-done.1.refs_4_
  23.5 0.5 %shard_map.53 = (f32[86,8,128]{2,1,0:T(8,128)S(1)}, f32[12,8,128]{2,1,0:T(8,128)S(1)}, f32[4,8,128]{2,1,0:T(8,128)S(1)}, f32[31,8,128]{2,1,0:T(8,128)S(1)}, f32[...) custom-call(f32[5,16,8,128]{3,2,1,0:T(8,128)S(1)} %get-tuple-element.32.refs_0_, f32[8,128]{1,0:T(8,128)S(1)} %get-tuple-element.33.refs_1_, ...), custom_call_target="tpu_custom_call" | custom-call | tf_op jit(solution)/shard_map/pallas_call | solution.py:590
  24.0 4.5 %collective-permute-start.4 = (f32[31,8,128]{2,1,0:T(8,128)S(1)}, f32[31,8,128]{2,1,0:T(8,128)S(1)}, u32[]{:S(2)}, u32[]{:S(2)}) collective-permute-start(f32[31,8,128]{2,1,0:T(8,128)S(1)} %get-tuple-element.45), channel_id=1, source_target_pairs={{0,128},{128,0},{256,384},{384,256},{1,129},{129,1},{257,385},{385... | collective-permute-start | bytes 380936 | tf_op jit(solution)/shard_map/ppermute | solution.py:665
  28.5 0.2 shard_map.54
  28.7 0.7 %collective-permute-done.4.refs_2_.refs_6_ = f32[31,8,128]{2,1,0:T(8,128)S(1)} collective-permute-done((f32[31,8,128]{2,1,0:T(8,128)S(1)}, f32[31,8,128]{2,1,0:T(8,128)S(1)}, u32[]{:S(2)}, u32[]{:S(2)}) %collective-permute-start.4) | collective-permute-done | bytes 127008 | tf_op jit(solution)/shard_map/ppermute | solution.py:665
  29.5 4.9 %collective-permute-start.5 = (f32[31,8,128]{2,1,0:T(8,128)S(1)}, f32[31,8,128]{2,1,0:T(8,128)S(1)}, u32[]{:S(2)}, u32[]{:S(2)}) collective-permute-start(f32[31,8,128]{2,1,0:T(8,128)S(1)} %shard_map.55.refs_10_), channel_id=1, source_target_pairs={{128,256},{256,128},{384,0},{129,257},{257,129},{385,1},{130,258},... | collective-permute-start | bytes 380936 | tf_op jit(solution)/shard_map/ppermute | solution.py:675
  34.4 2.0 %collective-permute-start.6 = (f32[3,8,128]{2,1,0:T(8,128)S(1)}, f32[3,8,128]{2,1,0:T(8,128)S(1)}, u32[]{:S(2)}, u32[]{:S(2)}) collective-permute-start(f32[3,8,128]{2,1,0:T(8,128)S(1)} %get-tuple-element.50), channel_id=1, source_target_pairs={{0,16},{32,48},{64,80},{96,112},{16,0},{48,32},{80,64},{112,96},{1... | collective-permute-start | bytes 36872 | tf_op jit(solution)/shard_map/ppermute | solution.py:667
  36.4 4.6 %collective-permute-start.7 = (f32[3,8,128]{2,1,0:T(8,128)S(1)}, f32[3,8,128]{2,1,0:T(8,128)S(1)}, u32[]{:S(2)}, u32[]{:S(2)}) collective-permute-start(f32[3,8,128]{2,1,0:T(8,128)S(1)} %get-tuple-element.47.refs_3_), channel_id=1, source_target_pairs={{16,32},{48,64},{80,96},{32,16},{64,48},{96,80},{17,33},{49,65},{8... | collective-permute-start | bytes 36872 | tf_op jit(solution)/shard_map/ppermute | solution.py:666
  41.0 1.2 %shard_map.56 = (f32[5,16,8,128]{3,2,1,0:T(8,128)S(1)}, f32[5,16,8,128]{3,2,1,0:T(8,128)S(1)}, f32[5,16,8,128]{3,2,1,0:T(8,128)S(1)}, f32[5,16,8,128]{3,2,1,0:T(...) custom-call(f32[5,16,8,128]{3,2,1,0:T(8,128)S(1)} %get-tuple-element.32.refs_0_, ...), custom_call_target="tpu_custom_call" | custom-call | tf_op jit(solution)/shard_map/pallas_call | solution.py:590
  42.2 0.0 collective-permute-done.6.refs_10_
  42.2 0.0 collective-permute-done.7.refs_11_
  42.2 0.0 collective-permute-done.5.refs_7_
  42.2 3.7 %shard_map.57 = (f32[5,16,8,128]{3,2,1,0:T(8,128)}, f32[8,128]{1,0:T(8,128)}) custom-call(f32[5,16,8,128]{3,2,1,0:T(8,128)S(1)} %get-tuple-element.32.refs_0_, f32[8,128]{1,0:T(8,128)S(1)} %get-tuple-element.33.refs_1_, f32[5,8,128]{2,1,0:T(8,128)S(1)} %get-tuple-element.34.refs_2_, f32[86,8,128]{2,1,0:T(8,128)S(1)} %get-tuple-element.42.refs_0_.refs_2_.refs_3_, ...), custom_call_target="tpu_custom_call" | custom-call | tf_op jit(solution)/shard_map/pallas_call | solution.py:590
  (1 shorter events, 0.0 us)
Async XLA Ops:
  1.7 21.8 %collective-permute-start = (f32[43,8,128]{2,1,0:T(8,128)S(1)}, f32[43,8,128]{2,1,0:T(8,128)S(1)}, u32[]{:S(2)}, u32[]{:S(2)}) collective-permute-start(f32[43,8,128]{2,1,0:T(8,128)S(1)} %get-tuple-element.35), channel_id=1, source_target_pairs={{0,1},{2,3},{4,5},{6,7},{8,9},{10,11},{12,13},{14,15},{1,0},{3,2},... | collective-permute-start | bytes 528392 | tf_op jit(solution)/shard_map/ppermute | solution.py:653
  4.8 18.7 %collective-permute-start.1 = (f32[43,8,128]{2,1,0:T(8,128)S(1)}, f32[43,8,128]{2,1,0:T(8,128)S(1)}, u32[]{:S(2)}, u32[]{:S(2)}) collective-permute-start(f32[43,8,128]{2,1,0:T(8,128)S(1)} %get-tuple-element.36), channel_id=1, source_target_pairs={{1,2},{3,4},{5,6},{7,8},{9,10},{11,12},{13,14},{15,0},{2,1},{4,3},... | collective-permute-start | bytes 528392 | tf_op jit(solution)/shard_map/ppermute | solution.py:652
  15.7 7.5 %collective-permute-start.2 = (f32[3,8,128]{2,1,0:T(8,128)S(1)}, f32[3,8,128]{2,1,0:T(8,128)S(1)}, u32[]{:S(2)}, u32[]{:S(2)}) collective-permute-start(f32[3,8,128]{2,1,0:T(8,128)S(1)} %get-tuple-element.39), channel_id=1, source_target_pairs={{0,16},{32,48},{64,80},{96,112},{16,0},{48,32},{80,64},{112,96},{1... | collective-permute-start | bytes 36872 | tf_op jit(solution)/shard_map/ppermute | solution.py:656
  17.8 5.7 %collective-permute-start.3 = (f32[3,8,128]{2,1,0:T(8,128)S(1)}, f32[3,8,128]{2,1,0:T(8,128)S(1)}, u32[]{:S(2)}, u32[]{:S(2)}) collective-permute-start(f32[3,8,128]{2,1,0:T(8,128)S(1)} %get-tuple-element.40), channel_id=1, source_target_pairs={{16,32},{48,64},{80,96},{32,16},{64,48},{96,80},{17,33},{49,65},{8... | collective-permute-start | bytes 36872 | tf_op jit(solution)/shard_map/ppermute | solution.py:655
  24.0 5.5 %collective-permute-start.4 = (f32[31,8,128]{2,1,0:T(8,128)S(1)}, f32[31,8,128]{2,1,0:T(8,128)S(1)}, u32[]{:S(2)}, u32[]{:S(2)}) collective-permute-start(f32[31,8,128]{2,1,0:T(8,128)S(1)} %get-tuple-element.45), channel_id=1, source_target_pairs={{0,128},{128,0},{256,384},{384,256},{1,129},{129,1},{257,385},{385... | collective-permute-start | bytes 380936 | tf_op jit(solution)/shard_map/ppermute | solution.py:665
  29.5 12.8 %collective-permute-start.5 = (f32[31,8,128]{2,1,0:T(8,128)S(1)}, f32[31,8,128]{2,1,0:T(8,128)S(1)}, u32[]{:S(2)}, u32[]{:S(2)}) collective-permute-start(f32[31,8,128]{2,1,0:T(8,128)S(1)} %shard_map.55.refs_10_), channel_id=1, source_target_pairs={{128,256},{256,128},{384,0},{129,257},{257,129},{385,1},{130,258},... | collective-permute-start | bytes 380936 | tf_op jit(solution)/shard_map/ppermute | solution.py:675
  34.4 7.8 %collective-permute-start.6 = (f32[3,8,128]{2,1,0:T(8,128)S(1)}, f32[3,8,128]{2,1,0:T(8,128)S(1)}, u32[]{:S(2)}, u32[]{:S(2)}) collective-permute-start(f32[3,8,128]{2,1,0:T(8,128)S(1)} %get-tuple-element.50), channel_id=1, source_target_pairs={{0,16},{32,48},{64,80},{96,112},{16,0},{48,32},{80,64},{112,96},{1... | collective-permute-start | bytes 36872 | tf_op jit(solution)/shard_map/ppermute | solution.py:667
  36.4 5.8 %collective-permute-start.7 = (f32[3,8,128]{2,1,0:T(8,128)S(1)}, f32[3,8,128]{2,1,0:T(8,128)S(1)}, u32[]{:S(2)}, u32[]{:S(2)}) collective-permute-start(f32[3,8,128]{2,1,0:T(8,128)S(1)} %get-tuple-element.47.refs_3_), channel_id=1, source_target_pairs={{16,32},{48,64},{80,96},{32,16},{64,48},{96,80},{17,33},{49,65},{8... | collective-permute-start | bytes 36872 | tf_op jit(solution)/shard_map/ppermute | solution.py:666

commit v9 on v8

--- a/solution.py
+++ b/solution.py
@@ -661,7 +661,7 @@
         [(NP, *plane), (UNITS, *plane), (4, *plane), (31, *plane), (27, *plane), (3, *plane)],
         [(27, *plane)] * 2,
     )
-    z_right, z_left, one, two = call(stage_corners, (halo,), [(3, *plane)] * 4)
+    z_right, z_left, one, two = call(stage_corners, (halo,), [(3, *plane)] * 2 + [(31, *plane)] * 2)
     near = lax.ppermute(near, "wn", [(0, 1), (1, 0), (2, 3), (3, 2)])
     s2 = lax.ppermute(two, "sx", swaps(tiles, 1, False))
     s1 = lax.ppermute(one, "sx", swaps(tiles, 0, False))

time: 46.2 us -> 48.3 us (1.045)
  the two profiles are of different devices: /device:TPU:25 before, /device:TPU:9 now
where the time goes in v9:
time: 48.3 us; the launch traced here: 48 us
  starting transfers between devices  36.5 us (76%)
  Pallas kernels  7.64 us (16%)
  waiting for transfers between devices  3.13 us (6%)
  between operations  0.76 us (2%)
    ppermute x1, starting transfers between devices, per_device(): a2 = lax.ppermute(two, 'az', swaps(around, 1, True))  10.6 us
    ppermute x2, starting transfers between devices, per_device(): s2 = lax.ppermute(two, 'sx', swaps(tiles, 1, False))  9.34 us
    pallas_call x8, Pallas kernels, call(): pl.pallas_call(body, out_shape=shapes, in_specs=[space] * len(ins), out_s...  7.64 us
    ppermute x1, starting transfers between devices, per_device(): far = lax.ppermute(far, 'wn', [(1, 2), (2, 1), (3, 0)])  5.11 us
    ppermute x1, starting transfers between devices, per_device(): near = lax.ppermute(near, 'wn', [(0, 1), (1, 0), (2, 3), (3, 2)])  4.29 us
    ppermute x2, starting transfers between devices, per_device(): s1 = lax.ppermute(one, 'sx', swaps(tiles, 0, False))  3.98 us
    ppermute x1, starting transfers between devices, per_device(): a1 = lax.ppermute(one, 'az', swaps(around, 0, True))  3.12 us
    ppermute x1, waiting for transfers between devices, per_device(): far = lax.ppermute(far, 'wn', [(1, 2), (2, 1), (3, 0)])  2.78 us
  transfers between devices with their start and end apart: 8, of which 2 were waited for; matrix products, arithmetic and copies ran while one was open for 0% of the time, Pallas kernels for 5%

profile of v9, /device:TPU:9, one launch (start us, length us, event | category | flops | bytes accessed | tf_op | source)
XLA Modules:
  0.0 48.0 jit_solution(4938028828700354748)
XLA Ops:
  0.6 1.0 %shard_map.50 = (f32[5,16,8,128]{3,2,1,0:T(8,128)S(1)}, f32[8,128]{1,0:T(8,128)S(1)}, f32[5,8,128]{2,1,0:T(8,128)S(1)}, f32[43,8,128]{2,1,0:T(8,128)S(1)}, f32[43,8,128]{2,1,0:T(8,128)S(1)}) custom-call(f32[5,16,8,128]{3,2,1,0:T(8,128)} %refs_0_.1, f32[8,128]{1,0:T(8,128)} %refs_1_.1, f32[5,8,128]{2,1,0:T(8,128)} %refs_2_.1), custom_call_target="tpu_custom_call" | custom-call | tf_op jit(solution)/shard_map/pallas_call | solution.py:590
  1.7 3.1 %collective-permute-start = (f32[43,8,128]{2,1,0:T(8,128)S(1)}, f32[43,8,128]{2,1,0:T(8,128)S(1)}, u32[]{:S(2)}, u32[]{:S(2)}) collective-permute-start(f32[43,8,128]{2,1,0:T(8,128)S(1)} %get-tuple-element.35), channel_id=1, source_target_pairs={{0,1},{2,3},{4,5},{6,7},{8,9},{10,11},{12,13},{14,15},{1,0},{3,2},... | collective-permute-start | bytes 528392 | tf_op jit(solution)/shard_map/ppermute | solution.py:653
  4.8 10.6 %collective-permute-start.1 = (f32[43,8,128]{2,1,0:T(8,128)S(1)}, f32[43,8,128]{2,1,0:T(8,128)S(1)}, u32[]{:S(2)}, u32[]{:S(2)}) collective-permute-start(f32[43,8,128]{2,1,0:T(8,128)S(1)} %get-tuple-element.36), channel_id=1, source_target_pairs={{1,2},{3,4},{5,6},{7,8},{9,10},{11,12},{13,14},{15,0},{2,1},{4,3},... | collective-permute-start | bytes 528392 | tf_op jit(solution)/shard_map/ppermute | solution.py:652
  15.4 0.2 shard_map.51
  15.7 2.1 %collective-permute-start.2 = (f32[3,8,128]{2,1,0:T(8,128)S(1)}, f32[3,8,128]{2,1,0:T(8,128)S(1)}, u32[]{:S(2)}, u32[]{:S(2)}) collective-permute-start(f32[3,8,128]{2,1,0:T(8,128)S(1)} %get-tuple-element.39), channel_id=1, source_target_pairs={{0,16},{32,48},{64,80},{96,112},{16,0},{48,32},{80,64},{112,96},{1... | collective-permute-start | bytes 36872 | tf_op jit(solution)/shard_map/ppermute | solution.py:656
  17.8 4.3 %collective-permute-start.3 = (f32[3,8,128]{2,1,0:T(8,128)S(1)}, f32[3,8,128]{2,1,0:T(8,128)S(1)}, u32[]{:S(2)}, u32[]{:S(2)}) collective-permute-start(f32[3,8,128]{2,1,0:T(8,128)S(1)} %get-tuple-element.40), channel_id=1, source_target_pairs={{16,32},{48,64},{80,96},{32,16},{64,48},{96,80},{17,33},{49,65},{8... | collective-permute-start | bytes 36872 | tf_op jit(solution)/shard_map/ppermute | solution.py:655
  22.1 0.7 %shard_map.52 = (f32[5,16,8,128]{3,2,1,0:T(8,128)S(1)}, f32[5,16,8,128]{3,2,1,0:T(8,128)S(1)}, f32[5,16,8,128]{3,2,1,0:T(8,128)S(1)}, f32[5,16,8,128]{3,2,1,0:T(8,128)S(1)}, f32[5,16,8,128]{3,2,1,0:T(8,128)S(1)}) custom-call(f32[5,16,8,128]{3,2,1,0:T(8,128)S(1)} %get-tuple-element.32.refs_0_, f32[3,8,128]{2,1,0:T(8,128)S(1)} %get-tuple-element.37.refs_1_.refs_5_), custom_call_target="tpu_custom_call" | custom-call | tf_op jit(solution)/shard_map/pallas_call | solution.py:590
  22.8 0.0 collective-permute-done.2.refs_7_
  22.8 0.3 collective-permute-done.3.refs_8_
  23.2 0.0 collective-permute-done.refs_3_
  23.2 0.0 collective-permute-done.1.refs_4_
  23.2 0.5 %shard_map.53 = (f32[86,8,128]{2,1,0:T(8,128)S(1)}, f32[12,8,128]{2,1,0:T(8,128)S(1)}, f32[4,8,128]{2,1,0:T(8,128)S(1)}, f32[31,8,128]{2,1,0:T(8,128)S(1)}, f32[...) custom-call(f32[5,16,8,128]{3,2,1,0:T(8,128)S(1)} %get-tuple-element.32.refs_0_, f32[8,128]{1,0:T(8,128)S(1)} %get-tuple-element.33.refs_1_, ...), custom_call_target="tpu_custom_call" | custom-call | tf_op jit(solution)/shard_map/pallas_call | solution.py:590
  23.7 4.3 %collective-permute-start.4 = (f32[31,8,128]{2,1,0:T(8,128)S(1)}, f32[31,8,128]{2,1,0:T(8,128)S(1)}, u32[]{:S(2)}, u32[]{:S(2)}) collective-permute-start(f32[31,8,128]{2,1,0:T(8,128)S(1)} %get-tuple-element.45), channel_id=1, source_target_pairs={{0,128},{128,0},{256,384},{384,256},{1,129},{129,1},{257,385},{385... | collective-permute-start | bytes 380936 | tf_op jit(solution)/shard_map/ppermute | solution.py:665
  28.0 0.2 shard_map.54
  28.2 1.9 %collective-permute-start.6 = (f32[31,8,128]{2,1,0:T(8,128)S(1)}, f32[31,8,128]{2,1,0:T(8,128)S(1)}, u32[]{:S(2)}, u32[]{:S(2)}) collective-permute-start(f32[31,8,128]{2,1,0:T(8,128)S(1)} %get-tuple-element.50), channel_id=1, source_target_pairs={{0,16},{32,48},{64,80},{96,112},{16,0},{48,32},{80,64},{112,96},{1... | collective-permute-start | bytes 380936 | tf_op jit(solution)/shard_map/ppermute | solution.py:667
  30.1 5.0 %collective-permute-start.7 = (f32[31,8,128]{2,1,0:T(8,128)S(1)}, f32[31,8,128]{2,1,0:T(8,128)S(1)}, u32[]{:S(2)}, u32[]{:S(2)}) collective-permute-start(f32[31,8,128]{2,1,0:T(8,128)S(1)} %get-tuple-element.47.refs_3_), channel_id=1, source_target_pairs={{16,32},{48,64},{80,96},{32,16},{64,48},{96,80},{17,33},{49,65},{8... | collective-permute-start | bytes 380936 | tf_op jit(solution)/shard_map/ppermute | solution.py:666
  35.1 0.0 collective-permute-done.4.refs_2_.refs_6_
  35.2 5.1 %collective-permute-start.5 = (f32[31,8,128]{2,1,0:T(8,128)S(1)}, f32[31,8,128]{2,1,0:T(8,128)S(1)}, u32[]{:S(2)}, u32[]{:S(2)}) collective-permute-start(f32[31,8,128]{2,1,0:T(8,128)S(1)} %shard_map.55.refs_10_), channel_id=1, source_target_pairs={{128,256},{256,128},{384,0},{129,257},{257,129},{385,1},{130,258},... | collective-permute-start | bytes 380936 | tf_op jit(solution)/shard_map/ppermute | solution.py:675
  40.3 1.2 %shard_map.56 = (f32[5,16,8,128]{3,2,1,0:T(8,128)S(1)}, f32[5,16,8,128]{3,2,1,0:T(8,128)S(1)}, f32[5,16,8,128]{3,2,1,0:T(8,128)S(1)}, f32[5,16,8,128]{3,2,1,0:T(...) custom-call(f32[5,16,8,128]{3,2,1,0:T(8,128)S(1)} %get-tuple-element.32.refs_0_, ...), custom_call_target="tpu_custom_call" | custom-call | tf_op jit(solution)/shard_map/pallas_call | solution.py:590
  41.5 0.0 collective-permute-done.6.refs_10_
  41.6 0.0 collective-permute-done.7.refs_11_
  41.6 2.8 %collective-permute-done.5.refs_7_ = f32[31,8,128]{2,1,0:T(8,128)S(1)} collective-permute-done((f32[31,8,128]{2,1,0:T(8,128)S(1)}, f32[31,8,128]{2,1,0:T(8,128)S(1)}, u32[]{:S(2)}, u32[]{:S(2)}) %collective-permute-start.5) | collective-permute-done | bytes 127008 | tf_op jit(solution)/shard_map/ppermute | solution.py:675
  44.3 3.7 %shard_map.57 = (f32[5,16,8,128]{3,2,1,0:T(8,128)}, f32[8,128]{1,0:T(8,128)}) custom-call(f32[5,16,8,128]{3,2,1,0:T(8,128)S(1)} %get-tuple-element.32.refs_0_, f32[8,128]{1,0:T(8,128)S(1)} %get-tuple-element.33.refs_1_, f32[5,8,128]{2,1,0:T(8,128)S(1)} %get-tuple-element.34.refs_2_, f32[86,8,128]{2,1,0:T(8,128)S(1)} %get-tuple-element.42.refs_0_.refs_2_.refs_3_, ...), custom_call_target="tpu_custom_call" | custom-call | tf_op jit(solution)/shard_map/pallas_call | solution.py:590
  (1 shorter events, 0.0 us)
Async XLA Ops:
  1.7 21.5 %collective-permute-start = (f32[43,8,128]{2,1,0:T(8,128)S(1)}, f32[43,8,128]{2,1,0:T(8,128)S(1)}, u32[]{:S(2)}, u32[]{:S(2)}) collective-permute-start(f32[43,8,128]{2,1,0:T(8,128)S(1)} %get-tuple-element.35), channel_id=1, source_target_pairs={{0,1},{2,3},{4,5},{6,7},{8,9},{10,11},{12,13},{14,15},{1,0},{3,2},... | collective-permute-start | bytes 528392 | tf_op jit(solution)/shard_map/ppermute | solution.py:653
  4.8 18.4 %collective-permute-start.1 = (f32[43,8,128]{2,1,0:T(8,128)S(1)}, f32[43,8,128]{2,1,0:T(8,128)S(1)}, u32[]{:S(2)}, u32[]{:S(2)}) collective-permute-start(f32[43,8,128]{2,1,0:T(8,128)S(1)} %get-tuple-element.36), channel_id=1, source_target_pairs={{1,2},{3,4},{5,6},{7,8},{9,10},{11,12},{13,14},{15,0},{2,1},{4,3},... | collective-permute-start | bytes 528392 | tf_op jit(solution)/shard_map/ppermute | solution.py:652
  15.7 7.1 %collective-permute-start.2 = (f32[3,8,128]{2,1,0:T(8,128)S(1)}, f32[3,8,128]{2,1,0:T(8,128)S(1)}, u32[]{:S(2)}, u32[]{:S(2)}) collective-permute-start(f32[3,8,128]{2,1,0:T(8,128)S(1)} %get-tuple-element.39), channel_id=1, source_target_pairs={{0,16},{32,48},{64,80},{96,112},{16,0},{48,32},{80,64},{112,96},{1... | collective-permute-start | bytes 36872 | tf_op jit(solution)/shard_map/ppermute | solution.py:656
  17.8 5.4 %collective-permute-start.3 = (f32[3,8,128]{2,1,0:T(8,128)S(1)}, f32[3,8,128]{2,1,0:T(8,128)S(1)}, u32[]{:S(2)}, u32[]{:S(2)}) collective-permute-start(f32[3,8,128]{2,1,0:T(8,128)S(1)} %get-tuple-element.40), channel_id=1, source_target_pairs={{16,32},{48,64},{80,96},{32,16},{64,48},{96,80},{17,33},{49,65},{8... | collective-permute-start | bytes 36872 | tf_op jit(solution)/shard_map/ppermute | solution.py:655
  23.7 11.5 %collective-permute-start.4 = (f32[31,8,128]{2,1,0:T(8,128)S(1)}, f32[31,8,128]{2,1,0:T(8,128)S(1)}, u32[]{:S(2)}, u32[]{:S(2)}) collective-permute-start(f32[31,8,128]{2,1,0:T(8,128)S(1)} %get-tuple-element.45), channel_id=1, source_target_pairs={{0,128},{128,0},{256,384},{384,256},{1,129},{129,1},{257,385},{385... | collective-permute-start | bytes 380936 | tf_op jit(solution)/shard_map/ppermute | solution.py:665
  28.2 13.3 %collective-permute-start.6 = (f32[31,8,128]{2,1,0:T(8,128)S(1)}, f32[31,8,128]{2,1,0:T(8,128)S(1)}, u32[]{:S(2)}, u32[]{:S(2)}) collective-permute-start(f32[31,8,128]{2,1,0:T(8,128)S(1)} %get-tuple-element.50), channel_id=1, source_target_pairs={{0,16},{32,48},{64,80},{96,112},{16,0},{48,32},{80,64},{112,96},{1... | collective-permute-start | bytes 380936 | tf_op jit(solution)/shard_map/ppermute | solution.py:667
  30.1 11.4 %collective-permute-start.7 = (f32[31,8,128]{2,1,0:T(8,128)S(1)}, f32[31,8,128]{2,1,0:T(8,128)S(1)}, u32[]{:S(2)}, u32[]{:S(2)}) collective-permute-start(f32[31,8,128]{2,1,0:T(8,128)S(1)} %get-tuple-element.47.refs_3_), channel_id=1, source_target_pairs={{16,32},{48,64},{80,96},{32,16},{64,48},{96,80},{17,33},{49,65},{8... | collective-permute-start | bytes 380936 | tf_op jit(solution)/shard_map/ppermute | solution.py:666
  35.2 9.2 %collective-permute-start.5 = (f32[31,8,128]{2,1,0:T(8,128)S(1)}, f32[31,8,128]{2,1,0:T(8,128)S(1)}, u32[]{:S(2)}, u32[]{:S(2)}) collective-permute-start(f32[31,8,128]{2,1,0:T(8,128)S(1)} %shard_map.55.refs_10_), channel_id=1, source_target_pairs={{128,256},{256,128},{384,0},{129,257},{257,129},{385,1},{130,258},... | collective-permute-start | bytes 380936 | tf_op jit(solution)/shard_map/ppermute | solution.py:675

commit v10 on v8

--- a/solution.py
+++ b/solution.py
@@ -387,8 +387,115 @@
     together(4, (2, 3, own_inner), (2, 3, halo_inner), (0, 1, outer))
 
 
-def advance(wn, tile, tiles, q, h, b, z, strips, w, near, far, z_right, z_left, z_one, z_two, slope, tx, bx, tz, bz, ez, ghost, *rest):
-    out_hbm, h_hbm, qw, zw, f1w, f2w, gw, f2zw, gzw, f1x, f2x, gx, f3, sx, sz, pt, ptz, zst, out, h_out, sems = rest
+def advance_own(wn, q, h, b, z, strips, w, near, far, slope, tx, bx, ghost, *rest):
+    sx, f1x, f2x, gx, f3x, qw, f1w, f2w, gw, f3, pt = rest
+    ln = lane()
+    bottom, top = wn == 0, wn == 3
+    odd = wn % 2 == 1
+
+    def below(i):
+        return jnp.where(odd, near[i], far[i])
+
+    def above(i):
+        return jnp.where(odd, far[i], near[i])
+
+    speeds = [jnp.where(top, w[k], jnp.where(wn == 2, near[27 + k], far[27 + k])) for k in range(4)]
+    w0, w0z, w0s, w1 = speeds
+
+    h0, h0z, h0s = h[...], z[80], strips[11]
+    hx, hz, _ = (slope[k] for k in range(3))
+    ih = 1.0 / h0
+    base = wn * NL
+    side = []
+    for f in range(5):
+        sign, bq, bz = MIRROR[f], b[f], z[81 + f]
+        for k in range(4):
+            qw[f, k] = jnp.where(bottom, sign * q[f, 3 - k], below(4 * f + k))
+            qw[f, 4 + k] = q[f, k]
+            qw[f, 8 + k] = q[f, 12 + k]
+            qw[f, 12 + k] = jnp.where(top, bq, above(4 * f + k))
+        zb, za = below(20 + f), above(20 + f)
+        side.append(
+            (
+                jnp.where(bottom, sign * z[f * NL + 1], zb),
+                jnp.where(bottom, sign * z[f * NL], rs(zb, 4)),
+                jnp.where(top, bz, za),
+                jnp.where(top, bz, rs(za, 4)),
+            )
+        )
+    for i, k in enumerate((2, 3, 12, 13)):
+        (a3,) = fluxes([side[f][i] for f in range(5)], (3,))
+        for f in range(5):
+            for ref, at, x in put_halo(f3, f, k, a3[f]):
+                ref[at] = x
+    strip_q = []
+    for f in range(5):
+        if f < 4:
+            sb, sa = rl(below(25), 96 - 32 * f), rl(above(25), -32 * f)
+        else:
+            sb, sa = below(26), above(26)
+        sb, sa = jnp.where(bottom, ghost[f], sb), jnp.where(top, ghost[f], sa)
+        strip_q.append(jnp.where(ln < 64, sa, sb))
+    (a1,) = fluxes(strip_q, (1,))
+    for f in range(5):
+        pt[f] = strip_patch(d_lane(a1[f]))
+
+    def own_flux(k):
+        a1, a2, a3, g = fluxes([qw[f, k] for f in range(5)], move=(hx, hz, w0))
+        todo = []
+        for f in range(5):
+            todo += [(r, (f, k), x[f]) for r, x in ((f1w, a1), (f2w, a2), (gw, g))]
+            todo += [(f3, (f, k, slice(16, 24)), a3[f])]
+        return todo
+
+    def eta_of(l):
+        return ((base + l).astype(F32) + 0.5) / LAYERS
+
+
+    def normal_own(f, k, eta):
+        return ih * (eta * d_normal(plane_at(gw, f), k) - d_normal(plane_at(f2w, f), k))
+
+    def ghost_layer(m):
+        upper = (m >= 2).astype(jnp.int32)
+        k, l, todo = 2 + m + 8 * upper, m - 2 + 16 * upper, []
+        for f in range(5):
+            dx = patched(d_lane(f1w[f, k]), pltpu.roll(pt[f], patch_shift(l), 1))
+            s = qw[f, k] + C * (normal_own(f, k, eta_of(l)) - (dx + d_around(f3, f, k)))
+            todo.append((sx, (f, l + 2), s))
+        return todo
+
+    def outer(m):
+        upper = (m >= 2).astype(jnp.int32)
+        k, l = 4 + m + 4 * upper, m + 12 * upper
+        return [(sx, (f, l + 2), tx[f, l] + C * normal_own(f, k, eta_of(l))) for f in range(5)]
+
+    def inner(l):
+        return [(sx, (f, l + 2), tx[f, l] + w0 * bx[f, l]) for f in range(5)]
+
+    together(4, (0, 4, own_flux))
+    together(2, (0, 2, ghost_layer), (0, 2, outer), (2, 6, inner))
+    for f in range(5):
+        for k in range(2):
+            sx[f, k] = jnp.where(bottom, MIRROR[f] * sx[f, 3 - k], sx[f, k])
+            sx[f, 18 + k] = jnp.where(top, b[f], sx[f, 18 + k])
+
+    h1, h1z, h1s = h0 + STEP * w0, h0z + STEP * w0z, h0s + STEP * w0s
+    hx1 = SCALE * d_ends(h1, rl(strip_ends(h1s), -12))
+    hz1 = SCALE * d_ring(h1, h1z)[0]
+
+    def own_flux_two(l):
+        a1, a2, a3, g = fluxes([sx[f, l + 2] for f in range(5)], move=(hx1, hz1, w1))
+        todo = []
+        for f in range(5):
+            todo += [(r, (f, l + 2), x[f]) for r, x in ((f1x, a1), (f2x, a2), (gx, g))]
+            todo += [(f3x, (f, l + 2), a3[f])]
+        return todo
+
+    together(4, (-2, 5, own_flux_two))
+
+
+def advance(wn, tile, tiles, q, h, b, z, strips, w, near, far, z_right, z_left, z_one, z_two, slope, tz, bz, ez, ghost, sx, f1x, f2x, gx, f3x, *rest):
+    out_hbm, h_hbm, zw, f2zw, gzw, f3, sz, pt, ptz, zst, out, h_out, sems = rest
     first, last = tile == 0, tile == tiles - 1
 
     def put_strip(u, x):
@@ -416,10 +523,6 @@
         sign = MIRROR[f]
         bq, bz_ = b[f], z[81 + f]
         for k in range(4):
-            qw[f, k] = jnp.where(bottom, sign * q[f, 3 - k], below(4 * f + k))
-            qw[f, 4 + k] = q[f, k]
-            qw[f, 8 + k] = q[f, 12 + k]
-            qw[f, 12 + k] = jnp.where(top, bq, above(4 * f + k))
             zw[f, 2 + k] = z[f * NL + k]
             zw[f, 6 + k] = z[f * NL + 12 + k]
         zb, za = below(20 + f), above(20 + f)
@@ -481,14 +584,6 @@
             done.append(s)
         strip_s.append(done)
 
-    def own_flux(k):
-        a1, a2, a3, g = fluxes([qw[f, k] for f in range(5)], move=(hx, hz, w0))
-        todo = []
-        for f in range(5):
-            todo += [(r, (f, k), x[f]) for r, x in ((f1w, a1), (f2w, a2), (gw, g))]
-            todo += [(f3, (f, k, slice(16, 24)), a3[f])]
-        return todo
-
     def eta_of(l):
         return ((base + l).astype(F32) + 0.5) / LAYERS
 
@@ -500,26 +595,13 @@
             todo += [(r, (f, k), x[f]) for r, x in ((f2zw, a2), (gzw, g))] + put_halo(f3, f, k + 2, a3[f])
         return todo
 
-    together(4, (0, 4, own_flux), (0, 3, halo_flux))
-
-    def normal_own(f, k, eta):
-        return ih * (eta * d_normal(plane_at(gw, f), k) - d_normal(plane_at(f2w, f), k))
-
-    def ghost_layer(m):
-        upper = (m >= 2).astype(jnp.int32)
-        k, l, todo = 2 + m + 8 * upper, m - 2 + 16 * upper, []
-        for f in range(5):
-            dx = patched(d_lane(f1w[f, k]), pltpu.roll(pt[f, 2], patch_shift(l), 1))
-            s = qw[f, k] + C * (normal_own(f, k, eta_of(l)) - (dx + d_around(f3, f, k)))
-            todo.append((sx, (f, l + 2), s))
-        return todo
+    together(3, (0, 4, halo_flux))
 
     def outer(m):
         upper = (m >= 2).astype(jnp.int32)
-        k, kz, l, todo = 4 + m + 4 * upper, 2 + m + 4 * upper, m + 12 * upper, []
+        kz, l, todo = 2 + m + 4 * upper, m + 12 * upper, []
         eta, half, shift = eta_of(l), l >> 3, patch_shift(l)
         for f in range(5):
-            todo.append((sx, (f, l + 2), tx[f, l] + C * normal_own(f, k, eta)))
             dn, dg = d_normal(plane_at(f2zw, f), kz), d_normal(plane_at(gzw, f), kz)
             edge = edges(pltpu.roll(ptz[f, half], shift, 1))
             todo.append((sz, (f, l), tz[f, l] + C * (ihz * (eta * dg - dn) - edge)))
@@ -528,17 +610,11 @@
     def inner(l):
         half, shift, todo = l >> 3, patch_shift(l), []
         for f in range(5):
-            todo.append((sx, (f, l + 2), tx[f, l] + w0 * bx[f, l]))
             edge = edges(pltpu.roll(ptz[f, half], shift, 1))
             todo.append((sz, (f, l), (tz[f, l] + w0z * bz[f, l]) + (hxz * ez[f, l] - C * edge)))
         return todo
 
-    together(2, (0, 2, ghost_layer), (0, 2, outer), (2, 6, inner))
-    for f in range(5):
-        for k in range(2):
-            sx[f, k] = jnp.where(bottom, MIRROR[f] * sx[f, 3 - k], sx[f, k])
-            sx[f, 18 + k] = jnp.where(top, b[f], sx[f, 18 + k])
-
+    together(2, (0, 2, outer), (2, 6, inner))
     h1, h1z, h1s = h0 + STEP * w0, h0z + STEP * w0z, h0s + STEP * w0s
     hx1 = SCALE * d_ends(h1, rl(strip_ends(h1s), -12))
     hz1 = SCALE * d_ring(h1, h1z)[0]
@@ -551,17 +627,10 @@
         for f in range(5):
             pt[f, v] = strip_ends(a1[f])
 
-    def own_flux_two(l):
-        a1, a2, a3, g = fluxes([sx[f, l + 2] for f in range(5)], move=(hx1, hz1, w1))
-        todo = []
-        for f in range(5):
-            todo += [(r, (f, l + 2), x[f]) for r, x in ((f1x, a1), (f2x, a2), (gx, g))]
-            todo += [(f3, (f, l + 2, slice(16, 24)), a3[f])]
-        return todo
-
     def halo_flux_two(l):
         (a3,) = fluxes([sz[f, l] for f in range(5)], (3,))
-        return [x for f in range(5) for x in put_halo(f3, f, l + 2, a3[f])]
+        todo = [(f3, (f, l + 2, slice(16, 24)), f3x[f, l + 2]) for f in range(5)]
+        return todo + [x for f in range(5) for x in put_halo(f3, f, l + 2, a3[f])]
 
     def final(l):
         eta, shift, todo = eta_of(l), patch_shift(l), []
@@ -573,7 +642,7 @@
             todo.append((out, (f, l), 0.5 * (q[f, l] + sx[f, l + 2] + C * rate)))
         return todo
 
-    together(4, (-2, 5, own_flux_two), (0, 4, halo_flux_two))
+    together(4, (0, 4, halo_flux_two))
 
     def out_copy(i):
         part = (slice(None), pl.ds(4 * i, 4))
@@ -627,6 +696,10 @@
 
 def stage_prepare(*refs):
     prepare(lax.axis_index("wn"), *refs)
+
+
+def stage_own_section(*refs):
+    advance_own(lax.axis_index("wn"), *refs)
 
 
 def stage_advance(*refs):
@@ -673,16 +746,20 @@
         [(5, NL, *plane)] * 4 + [(5, NL, 40, 128), (5, 2, *plane)],
     )
     far = lax.ppermute(far, "wn", [(1, 2), (2, 1), (3, 0)])
+    tx, bx, tz, bz, ez, ghost = parts
+    section = call(
+        stage_own_section,
+        (*own, halo, strips, w, near, far, slope, tx, bx, ghost),
+        [(5, 20, *plane)] * 5,
+        [(5, 16, *plane)] * 4 + [(5, 16, 40, 128), (5, *plane)],
+    )
     return call(
         stage_advance,
-        (*own, halo, strips, w, near, far, z_right, z_left, s1, s2, slope, *parts),
+        (*own, halo, strips, w, near, far, z_right, z_left, s1, s2, slope, tz, bz, ez, ghost, *section),
         [(5, NL, *plane), plane],
-        [(5, 16, *plane), (5, 12, *plane)]
-        + [(5, 16, *plane)] * 3
-        + [(5, 12, *plane)] * 2
-        + [(5, 20, *plane)] * 3
+        [(5, 12, *plane)] * 3
         + [(5, 20, 40, 128)]
-        + [(5, 20, *plane), (5, NL, *plane), (5, 3, *plane), (5, 2, *plane), (UNITS, *plane), (5, NL, *plane), plane],
+        + [(5, NL, *plane), (5, 3, *plane), (5, 2, *plane), (UNITS, *plane), (5, NL, *plane), plane],
         sems=5,
         out_space=HBM,
     )

time: 46.2 us -> 46.8 us (1.013)
  Pallas kernels: 7.65 us -> 8.17 us
    pallas_call x8 -> x9, Pallas kernels: 7.65 us -> 8.17 us  [call(): pl.pallas_call(body, out_shape=shapes, in_specs=[space] * len(ins), out_s...]
  transfers between devices with their start and end apart: 8 -> 8, of which waited for: 2 -> 2; matrix products, arithmetic and copies ran while one was open for 0% -> 0% of each run, Pallas kernels for 5% -> 8%
where the time goes in v10:
time: 46.8 us; the launch traced here: 46.4 us
  starting transfers between devices  36.4 us (78%)
  Pallas kernels  8.17 us (17%)
  waiting for transfers between devices  1.08 us (2%)
  between operations  0.77 us (2%)
    ppermute x1, starting transfers between devices, per_device(): a2 = lax.ppermute(two, 'az', swaps(around, 1, True))  10.6 us
    ppermute x2, starting transfers between devices, per_device(): s2 = lax.ppermute(two, 'sx', swaps(tiles, 1, False))  9.21 us
    pallas_call x9, Pallas kernels, call(): pl.pallas_call(body, out_shape=shapes, in_specs=[space] * len(ins), out_s...  8.17 us
    ppermute x1, starting transfers between devices, per_device(): far = lax.ppermute(far, 'wn', [(1, 2), (2, 1), (3, 0)])  4.9 us
    ppermute x1, starting transfers between devices, per_device(): near = lax.ppermute(near, 'wn', [(0, 1), (1, 0), (2, 3), (3, 2)])  4.5 us
    ppermute x2, starting transfers between devices, per_device(): s1 = lax.ppermute(one, 'sx', swaps(tiles, 0, False))  4.06 us
    ppermute x1, starting transfers between devices, per_device(): a1 = lax.ppermute(one, 'az', swaps(around, 0, True))  3.12 us
  transfers between devices with their start and end apart: 8, of which 2 were waited for; matrix products, arithmetic and copies ran while one was open for 0% of the time, Pallas kernels for 8%

profile of v10, /device:TPU:25, one launch (start us, length us, event | category | flops | bytes accessed | tf_op | source)
XLA Modules:
  0.0 46.4 jit_solution(9214327750961177041)
XLA Ops:
  0.6 1.0 %shard_map.50 = (f32[5,16,8,128]{3,2,1,0:T(8,128)S(1)}, f32[8,128]{1,0:T(8,128)S(1)}, f32[5,8,128]{2,1,0:T(8,128)S(1)}, f32[43,8,128]{2,1,0:T(8,128)S(1)}, f32[43,8,128]{2,1,0:T(8,128)S(1)}) custom-call(f32[5,16,8,128]{3,2,1,0:T(8,128)} %refs_0_.1, f32[8,128]{1,0:T(8,128)} %refs_1_.1, f32[5,8,128]{2,1,0:T(8,128)} %refs_2_.1), custom_call_target="tpu_custom_call" | custom-call | tf_op jit(solution)/shard_map/pallas_call | solution.py:659
  1.7 3.1 %collective-permute-start = (f32[43,8,128]{2,1,0:T(8,128)S(1)}, f32[43,8,128]{2,1,0:T(8,128)S(1)}, u32[]{:S(2)}, u32[]{:S(2)}) collective-permute-start(f32[43,8,128]{2,1,0:T(8,128)S(1)} %get-tuple-element.40), channel_id=1, source_target_pairs={{0,1},{2,3},{4,5},{6,7},{8,9},{10,11},{12,13},{14,15},{1,0},{3,2},... | collective-permute-start | bytes 528392 | tf_op jit(solution)/shard_map/ppermute | solution.py:726
  4.8 10.6 %collective-permute-start.1 = (f32[43,8,128]{2,1,0:T(8,128)S(1)}, f32[43,8,128]{2,1,0:T(8,128)S(1)}, u32[]{:S(2)}, u32[]{:S(2)}) collective-permute-start(f32[43,8,128]{2,1,0:T(8,128)S(1)} %get-tuple-element.41), channel_id=1, source_target_pairs={{1,2},{3,4},{5,6},{7,8},{9,10},{11,12},{13,14},{15,0},{2,1},{4,3},... | collective-permute-start | bytes 528392 | tf_op jit(solution)/shard_map/ppermute | solution.py:725
  15.4 0.2 shard_map.51
  15.7 2.1 %collective-permute-start.2 = (f32[3,8,128]{2,1,0:T(8,128)S(1)}, f32[3,8,128]{2,1,0:T(8,128)S(1)}, u32[]{:S(2)}, u32[]{:S(2)}) collective-permute-start(f32[3,8,128]{2,1,0:T(8,128)S(1)} %get-tuple-element.44), channel_id=1, source_target_pairs={{0,16},{32,48},{64,80},{96,112},{16,0},{48,32},{80,64},{112,96},{1... | collective-permute-start | bytes 36872 | tf_op jit(solution)/shard_map/ppermute | solution.py:729
  17.8 4.6 %collective-permute-start.3 = (f32[3,8,128]{2,1,0:T(8,128)S(1)}, f32[3,8,128]{2,1,0:T(8,128)S(1)}, u32[]{:S(2)}, u32[]{:S(2)}) collective-permute-start(f32[3,8,128]{2,1,0:T(8,128)S(1)} %get-tuple-element.45), channel_id=1, source_target_pairs={{16,32},{48,64},{80,96},{32,16},{64,48},{96,80},{17,33},{49,65},{8... | collective-permute-start | bytes 36872 | tf_op jit(solution)/shard_map/ppermute | solution.py:728
  22.4 0.7 %shard_map.52 = (f32[5,16,8,128]{3,2,1,0:T(8,128)S(1)}, f32[5,16,8,128]{3,2,1,0:T(8,128)S(1)}, f32[5,16,8,128]{3,2,1,0:T(8,128)S(1)}, f32[5,16,8,128]{3,2,1,0:T(8,128)S(1)}, f32[5,16,8,128]{3,2,1,0:T(8,128)S(1)}) custom-call(f32[5,16,8,128]{3,2,1,0:T(8,128)S(1)} %get-tuple-element.37.refs_0_, f32[3,8,128]{2,1,0:T(8,128)S(1)} %get-tuple-element.42.refs_1_.refs_5_), custom_call_target="tpu_custom_call" | custom-call | tf_op jit(solution)/shard_map/pallas_call | solution.py:659
  23.1 0.0 collective-permute-done.2.refs_7_
  23.1 0.3 collective-permute-done.3.refs_8_
  23.5 0.0 collective-permute-done.refs_3_
  23.5 0.0 collective-permute-done.1.refs_4_
  23.5 0.5 %shard_map.53 = (f32[86,8,128]{2,1,0:T(8,128)S(1)}, f32[12,8,128]{2,1,0:T(8,128)S(1)}, f32[4,8,128]{2,1,0:T(8,128)S(1)}, f32[31,8,128]{2,1,0:T(8,128)S(1)}, f32[...) custom-call(f32[5,16,8,128]{3,2,1,0:T(8,128)S(1)} %get-tuple-element.37.refs_0_, f32[8,128]{1,0:T(8,128)S(1)} %get-tuple-element.38.refs_1_, ...), custom_call_target="tpu_custom_call" | custom-call | tf_op jit(solution)/shard_map/pallas_call | solution.py:659
  24.0 4.5 %collective-permute-start.4 = (f32[31,8,128]{2,1,0:T(8,128)S(1)}, f32[31,8,128]{2,1,0:T(8,128)S(1)}, u32[]{:S(2)}, u32[]{:S(2)}) collective-permute-start(f32[31,8,128]{2,1,0:T(8,128)S(1)} %get-tuple-element.50), channel_id=1, source_target_pairs={{0,128},{128,0},{256,384},{384,256},{1,129},{129,1},{257,385},{385... | collective-permute-start | bytes 380936 | tf_op jit(solution)/shard_map/ppermute | solution.py:738
  28.5 0.2 shard_map.54
  28.7 0.7 %collective-permute-done.4.refs_2_.refs_6_ = f32[31,8,128]{2,1,0:T(8,128)S(1)} collective-permute-done((f32[31,8,128]{2,1,0:T(8,128)S(1)}, f32[31,8,128]{2,1,0:T(8,128)S(1)}, u32[]{:S(2)}, u32[]{:S(2)}) %collective-permute-start.4) | collective-permute-done | bytes 127008 | tf_op jit(solution)/shard_map/ppermute | solution.py:738
  29.5 4.9 %collective-permute-start.5 = (f32[31,8,128]{2,1,0:T(8,128)S(1)}, f32[31,8,128]{2,1,0:T(8,128)S(1)}, u32[]{:S(2)}, u32[]{:S(2)}) collective-permute-start(f32[31,8,128]{2,1,0:T(8,128)S(1)} %shard_map.55.refs_10_), channel_id=1, source_target_pairs={{128,256},{256,128},{384,0},{129,257},{257,129},{385,1},{130,258},... | collective-permute-start | bytes 380936 | tf_op jit(solution)/shard_map/ppermute | solution.py:748
  34.4 2.0 %collective-permute-start.6 = (f32[3,8,128]{2,1,0:T(8,128)S(1)}, f32[3,8,128]{2,1,0:T(8,128)S(1)}, u32[]{:S(2)}, u32[]{:S(2)}) collective-permute-start(f32[3,8,128]{2,1,0:T(8,128)S(1)} %get-tuple-element.55), channel_id=1, source_target_pairs={{0,16},{32,48},{64,80},{96,112},{16,0},{48,32},{80,64},{112,96},{1... | collective-permute-start | bytes 36872 | tf_op jit(solution)/shard_map/ppermute | solution.py:740
  36.4 4.6 %collective-permute-start.7 = (f32[3,8,128]{2,1,0:T(8,128)S(1)}, f32[3,8,128]{2,1,0:T(8,128)S(1)}, u32[]{:S(2)}, u32[]{:S(2)}) collective-permute-start(f32[3,8,128]{2,1,0:T(8,128)S(1)} %get-tuple-element.52.refs_3_), channel_id=1, source_target_pairs={{16,32},{48,64},{80,96},{32,16},{64,48},{96,80},{17,33},{49,65},{8... | collective-permute-start | bytes 36872 | tf_op jit(solution)/shard_map/ppermute | solution.py:739
  41.0 1.2 %shard_map.56 = (f32[5,16,8,128]{3,2,1,0:T(8,128)S(1)}, f32[5,16,8,128]{3,2,1,0:T(8,128)S(1)}, f32[5,16,8,128]{3,2,1,0:T(8,128)S(1)}, f32[5,16,8,128]{3,2,1,0:T(...) custom-call(f32[5,16,8,128]{3,2,1,0:T(8,128)S(1)} %get-tuple-element.37.refs_0_, ...), custom_call_target="tpu_custom_call" | custom-call | tf_op jit(solution)/shard_map/pallas_call | solution.py:659
  42.2 0.0 collective-permute-done.5.refs_7_
  42.2 1.1 %shard_map.57 = (f32[5,20,8,128]{3,2,1,0:T(8,128)S(1)}, f32[5,20,8,128]{3,2,1,0:T(8,128)S(1)}, f32[5,20,8,128]{3,2,1,0:T(8,128)S(1)}, f32[5,20,8,128]{3,2,1,0:T(8,128)S(1)}, f32[5,20,8,128]{3,2,1,0:T(8,128)S(1)}) custom-call(f32[5,16,8,128]{3,2,1,0:T(8,128)S(1)} %get-tuple-element.37.refs_0_, f32[8,128]{1,0:T(8,128)S(1)} %get-tuple-element.38.refs_1_, ...), custom_call_target="tpu_custom_call" | custom-call | tf_op jit(solution)/shard_map/pallas_call | solution.py:659
  43.3 0.0 collective-permute-done.6.refs_10_
  43.3 0.0 collective-permute-done.7.refs_11_
  43.3 3.1 %shard_map.58 = (f32[5,16,8,128]{3,2,1,0:T(8,128)}, f32[8,128]{1,0:T(8,128)}) custom-call(f32[5,16,8,128]{3,2,1,0:T(8,128)S(1)} %get-tuple-element.37.refs_0_, f32[8,128]{1,0:T(8,128)S(1)} %get-tuple-element.38.refs_1_, f32[5,8,128]{2,1,0:T(8,128)S(1)} %get-tuple-element.39.refs_2_, f32[86,8,128]{2,1,0:T(8,128)S(1)} %get-tuple-element.47.refs_0_.refs_2_.refs_3_, ...), custom_call_target="tpu_custom_call" | custom-call | tf_op jit(solution)/shard_map/pallas_call | solution.py:659
  (1 shorter events, 0.0 us)
Async XLA Ops:
  1.7 21.8 %collective-permute-start = (f32[43,8,128]{2,1,0:T(8,128)S(1)}, f32[43,8,128]{2,1,0:T(8,128)S(1)}, u32[]{:S(2)}, u32[]{:S(2)}) collective-permute-start(f32[43,8,128]{2,1,0:T(8,128)S(1)} %get-tuple-element.40), channel_id=1, source_target_pairs={{0,1},{2,3},{4,5},{6,7},{8,9},{10,11},{12,13},{14,15},{1,0},{3,2},... | collective-permute-start | bytes 528392 | tf_op jit(solution)/shard_map/ppermute | solution.py:726
  4.8 18.7 %collective-permute-start.1 = (f32[43,8,128]{2,1,0:T(8,128)S(1)}, f32[43,8,128]{2,1,0:T(8,128)S(1)}, u32[]{:S(2)}, u32[]{:S(2)}) collective-permute-start(f32[43,8,128]{2,1,0:T(8,128)S(1)} %get-tuple-element.41), channel_id=1, source_target_pairs={{1,2},{3,4},{5,6},{7,8},{9,10},{11,12},{13,14},{15,0},{2,1},{4,3},... | collective-permute-start | bytes 528392 | tf_op jit(solution)/shard_map/ppermute | solution.py:725
  15.7 7.5 %collective-permute-start.2 = (f32[3,8,128]{2,1,0:T(8,128)S(1)}, f32[3,8,128]{2,1,0:T(8,128)S(1)}, u32[]{:S(2)}, u32[]{:S(2)}) collective-permute-start(f32[3,8,128]{2,1,0:T(8,128)S(1)} %get-tuple-element.44), channel_id=1, source_target_pairs={{0,16},{32,48},{64,80},{96,112},{16,0},{48,32},{80,64},{112,96},{1... | collective-permute-start | bytes 36872 | tf_op jit(solution)/shard_map/ppermute | solution.py:729
  17.8 5.7 %collective-permute-start.3 = (f32[3,8,128]{2,1,0:T(8,128)S(1)}, f32[3,8,128]{2,1,0:T(8,128)S(1)}, u32[]{:S(2)}, u32[]{:S(2)}) collective-permute-start(f32[3,8,128]{2,1,0:T(8,128)S(1)} %get-tuple-element.45), channel_id=1, source_target_pairs={{16,32},{48,64},{80,96},{32,16},{64,48},{96,80},{17,33},{49,65},{8... | collective-permute-start | bytes 36872 | tf_op jit(solution)/shard_map/ppermute | solution.py:728
  24.0 5.5 %collective-permute-start.4 = (f32[31,8,128]{2,1,0:T(8,128)S(1)}, f32[31,8,128]{2,1,0:T(8,128)S(1)}, u32[]{:S(2)}, u32[]{:S(2)}) collective-permute-start(f32[31,8,128]{2,1,0:T(8,128)S(1)} %get-tuple-element.50), channel_id=1, source_target_pairs={{0,128},{128,0},{256,384},{384,256},{1,129},{129,1},{257,385},{385... | collective-permute-start | bytes 380936 | tf_op jit(solution)/shard_map/ppermute | solution.py:738
  29.5 12.7 %collective-permute-start.5 = (f32[31,8,128]{2,1,0:T(8,128)S(1)}, f32[31,8,128]{2,1,0:T(8,128)S(1)}, u32[]{:S(2)}, u32[]{:S(2)}) collective-permute-start(f32[31,8,128]{2,1,0:T(8,128)S(1)} %shard_map.55.refs_10_), channel_id=1, source_target_pairs={{128,256},{256,128},{384,0},{129,257},{257,129},{385,1},{130,258},... | collective-permute-start | bytes 380936 | tf_op jit(solution)/shard_map/ppermute | solution.py:748
  34.4 8.9 %collective-permute-start.6 = (f32[3,8,128]{2,1,0:T(8,128)S(1)}, f32[3,8,128]{2,1,0:T(8,128)S(1)}, u32[]{:S(2)}, u32[]{:S(2)}) collective-permute-start(f32[3,8,128]{2,1,0:T(8,128)S(1)} %get-tuple-element.55), channel_id=1, source_target_pairs={{0,16},{32,48},{64,80},{96,112},{16,0},{48,32},{80,64},{112,96},{1... | collective-permute-start | bytes 36872 | tf_op jit(solution)/shard_map/ppermute | solution.py:740
  36.4 6.9 %collective-permute-start.7 = (f32[3,8,128]{2,1,0:T(8,128)S(1)}, f32[3,8,128]{2,1,0:T(8,128)S(1)}, u32[]{:S(2)}, u32[]{:S(2)}) collective-permute-start(f32[3,8,128]{2,1,0:T(8,128)S(1)} %get-tuple-element.52.refs_3_), channel_id=1, source_target_pairs={{16,32},{48,64},{80,96},{32,16},{64,48},{96,80},{17,33},{49,65},{8... | collective-permute-start | bytes 36872 | tf_op jit(solution)/shard_map/ppermute | solution.py:739
